TPU v7x, 256 devices: a whole 4x4x8 slice. The times are simulated.
256 devices in a mesh: train: 16 (over x, z_lo), query: 8 (over y, z_hi), layer: 2 (over core).
Axes of the slice: x: 4, y: 4, z: 8 (z_hi: 2, z_lo: 4; z = z_hi * 4 + z_lo), core: 2. Of those that a mesh axis runs over, the one named last changes fastest.
Arguments:
- train_acts: bfloat16 [16384, 4, 32, 256], P(('train', 'query'), 'layer'), may hold values from -6 to 6
- train_backs: bfloat16 [16384, 4, 32, 256], P(('train', 'query'), 'layer'), may hold values from -6 to 6
- query_acts: bfloat16 [8, 512, 4, 32, 256], P('query', 'train', 'layer'), may hold values from -6 to 6
- query_backs: bfloat16 [8, 512, 4, 32, 256], P('query', 'train', 'layer'), may hold values from -6 to 6
- precond: bfloat16 [4, 1024, 1024], P('layer', 'train'), may hold values from -0.1875 to 0.1875
Outputs:
- scores: float32 [16384, 4096], P('train', 'query')
All inputs are finite; a program needn't handle non-finite values.
Results may differ from a plain program's by a relative error of at most 0.005.
Values may be sent and summed in bfloat16 or wider, within the bound.
No kernel may reach another device: no remote copies, remote signals or barrier semaphores. Data moves between devices by JAX's collectives and lax.ppermute only.
A program may use at most 64 MiB of HBM per device.

v0:
```python
import jax
import jax.numpy as jnp
from jax import lax
from jax.sharding import PartitionSpec as P


def form_grads(acts, backs):
    prod = jnp.einsum("nlbt,nlat->nlba", backs, acts, preferred_element_type=jnp.float32)
    prod = prod * acts.shape[-1] ** (-0.5)
    return prod.reshape(acts.shape[0], acts.shape[1], backs.shape[2] * acts.shape[2]).astype(
        jnp.bfloat16
    )


def apply_rows(grads_q, piece):
    return jnp.einsum("qlc,lrc->qlr", grads_q, piece, preferred_element_type=jnp.float32)


def per_device(train_acts, train_backs, query_acts, query_backs, precond):
    train_grad = form_grads(train_acts, train_backs)
    query_grad = form_grads(query_acts[0], query_backs[0])
    group_grads = lax.all_gather(query_grad, "train", axis=0, tiled=True)
    query_pre = apply_rows(
        group_grads, lax.all_gather(precond, "train", axis=1, tiled=True)
    ).astype(jnp.bfloat16)
    width = query_pre.shape[1] * query_pre.shape[2]
    right_side = query_pre.reshape(query_pre.shape[0], width)
    scale = (width * lax.axis_size("layer")) ** (-0.5)
    piece = lax.all_gather(train_grad, "query", axis=0, tiled=True)
    left_side = piece.reshape(piece.shape[0], width)
    partial_value = lax.dot_general(
        left_side, right_side, (((1,), (1,)), ((), ())), preferred_element_type=jnp.float32
    )
    partial_scores = partial_value * scale
    return lax.psum(partial_scores, "layer")


def solution(mesh):
    in_specs = (
        P(("train", "query"), "layer", None, None),
        P(("train", "query"), "layer", None, None),
        P("query", "train", "layer", None, None),
        P("query", "train", "layer", None, None),
        P("layer", "train", None),
    )
    out_specs = P("train", "query")
    return jax.shard_map(
        per_device, mesh=mesh, in_specs=in_specs, out_specs=out_specs, check_vma=False
    )
```

profile of v0, /device:TPU:1, one launch (start us, length us, event | category | flops | bytes accessed | tf_op | source)
XLA Modules:
  0.0 358.5 jit_solution(8254505558494453229)
XLA Ops:
  6.5 0.0 copy-start
  6.5 0.0 all-gather.6.cloned.1.call-start
  6.5 1.2 copy-done
  7.8 1.6 fusion.7
  9.4 1.2 convert_element_type.21
  10.6 0.0 all-gather.6.cloned.1.call-update
  10.6 0.0 all-gather.4.cloned.1.call-start
  10.7 6.6 %fusion.14 = f32[128,2,32,32]{3,2,1,0:T(8,128)} fusion(bf16[128,2,32,256]{3,2,1,0:T(8,128)(2,1)} %param.6, bf16[128,2,32,256]{3,2,1,0:T(8,128)(2,1)} %param.5), kind=kOutput, calls=%fused_computation.11 | convolution fusion | flops 134217728 | bytes 9437184 | tf_op jit(solution)/shard_map/nlbt,nlat->nlba/dot_general | solution.py:8
  17.3 3.7 %copy.12 = f32[128,2,32,32]{0,3,2,1:T(8,128)S(1)} copy(f32[128,2,32,32]{3,2,1,0:T(8,128)} %fusion.14) | data formatting | bytes 2097152 | tf_op jit(solution)/shard_map/nlbt,nlat->nlba/dot_general | solution.py:8
  21.1 0.1 multiply_convert_fusion
  21.2 1.0 copy.13
  22.2 0.0 all-gather.4.cloned.1.call-update
  22.2 0.0 all-gather.8.cloned.1.call-start
  22.3 0.7 all-gather.8.cloned.1.call-update
  22.9 0.0 all-reduce.2.cloned.1.call-start
  23.0 69.6 %all-gather.6.cloned.1.call-done = bf16[512,2,1024]{2,1,0:T(2,128)(2,1)} async-done(((bf16[32,2,1024]{2,1,0:T(2,128)(2,1)}), bf16[512,2,1024]{2,1,0:T(2,128)(2,1)}) %all-gather.6.cloned.1.call-update) | async-done | bytes 2097168 | tf_op jit(solution)/shard_map/all_gather | solution.py:22
  92.6 117.4 %all-gather.4.cloned.1.call-done = bf16[1024,2,1024]{2,0,1:T(8,128)(2,1)} async-done(((bf16[128,2,1024]{2,0,1:T(8,128)(2,1)}), bf16[1024,2,1024]{2,0,1:T(8,128)(2,1)}) %all-gather.4.cloned.1.call-update) | async-done | bytes 4194320 | tf_op jit(solution)/shard_map/all_gather | solution.py:29
  210.0 98.6 %all-gather.8.cloned.1.call-done = bf16[2,1024,1024]{2,1,0:T(8,128)(2,1)} async-done(((bf16[2,64,1024]{2,1,0:T(8,128)(2,1)}), bf16[2,1024,1024]{2,1,0:T(8,128)(2,1)}) %all-gather.8.cloned.1.call-update) | async-done | bytes 4194320 | tf_op jit(solution)/shard_map/all_gather | solution.py:24
  308.6 9.9 %bitcast_multiply_fusion = f32[1024,512]{1,0:T(8,128)} fusion(bf16[1024,2,1024]{2,0,1:T(8,128)(2,1)} %all-gather.4.cloned.1.call-done, bf16[2,1024,1024]{2,1,0:T(8,128)(2,1)} %all-gather.8.cloned.1.call-done, bf16[512,2,1024]{2,1,0:T(2,128)(2,1)} %all-gather.6.cloned.1.call-done), kind=kOutput, calls=%fused_computation | convolution fusion | flops 4296540160 | bytes 12582912 | tf_op jit(solution)/shard_map/dot_general | solution.py:31
  318.5 0.0 all-reduce.2.cloned.1.call-update
  318.5 30.3 %all-reduce.2.cloned.1.call-done = f32[1024,512]{1,0:T(8,128)} async-done(((f32[1024,512]{1,0:T(8,128)}), f32[1024,512]{1,0:T(8,128)}) %all-reduce.2.cloned.1.call-update) | async-done | bytes 2097168 | tf_op jit(solution)/shard_map/psum | solution.py:35
  348.9 3.1 copy.22
Async XLA Ops:
  6.5 1.2 copy-start
  6.5 86.1 %all-gather.6.cloned.1.call-start = ((), (), s32[]{:S(2)}) async-start(), calls=%async_computation.1 | async-start | bytes 2228224 | tf_op jit(solution)/shard_map/all_gather | solution.py:22
  10.6 199.4 %all-gather.4.cloned.1.call-start = ((), (), s32[]{:S(2)}) async-start(), calls=%async_computation | async-start | bytes 4718592 | tf_op jit(solution)/shard_map/all_gather | solution.py:29
  22.2 286.4 %all-gather.8.cloned.1.call-start = ((), (), s32[]{:S(2)}) async-start(), calls=%async_computation.2 | async-start | bytes 4456448 | tf_op jit(solution)/shard_map/all_gather | solution.py:24
  22.9 325.9 %all-reduce.2.cloned.1.call-start = ((), (), s32[]{:S(2)}) async-start(), calls=%async_computation.3 | async-start | bytes 4194304 | tf_op jit(solution)/shard_map/psum | solution.py:35
Sparse Core Ops, SparseCore 0:
  10.7 81.8 all-gather.5
  95.2 114.6 all-gather.3
  211.8 96.7 all-gather.7
  318.6 30.1 all-reduce.1
where the time goes:
time: 359 us; the launch traced here: 358 us
  waiting for transfers between devices  317 us (88%)
  matrix products  18.2 us (5%)
  between operations  13.1 us (4%)
  local copies, waits for them, and re-layouts  10.2 us (3%)
    all_gather x1, waiting for transfers between devices, per_device(): piece = lax.all_gather(train_grad, 'query', axis=0, tiled=True)  117 us
    all_gather x1, waiting for transfers between devices, per_device(): lax.all_gather(precond, 'train', axis=1, tiled=True)  98.6 us
    all_gather x1, waiting for transfers between devices, per_device(): group_grads = lax.all_gather(query_grad, 'train', axis=0, tiled=True)  69.6 us
    psum x1, waiting for transfers between devices, per_device(): return lax.psum(partial_scores, 'layer')  30.3 us
    dot_general x1, matrix products, per_device(): lax.dot_general(left_side, right_side, (((1,), (1,)), ((), ())), preferre...  9.9 us
    dot_general x2, matrix products, form_grads(): jnp.einsum('nlbt,nlat->nlba', backs, acts, preferred_element_type=jnp.flo...  8.28 us
  transfers between devices with their start and end apart: 4, of which 4 were waited for; matrix products, arithmetic and copies ran while one was open for 3% of the time, Pallas kernels for 0%

commit v1 on v0

v1 whole, which is shorter than its diff:
```python
import functools

import jax
import jax.numpy as jnp
from jax import lax
from jax.experimental import pallas as pl
from jax.experimental.pallas import tpu as pltpu
from jax.sharding import PartitionSpec as P

AXES = ("train", "query", "layer")
NX, NY, NZL, NZH = 4, 4, 4, 2
NT = (((1,), (1,)), ((), ()))
MIB = 1 << 20


def device(x, y, z, core):
    return (((x % NX) * NZL + z % NZL) * (NY * NZH) + (y % NY) * NZH + (z // NZL) % NZH) * 2 + core


def pairs(move):
    out = []
    for x in range(NX):
        for y in range(NY):
            for z in range(NZL * NZH):
                for core in range(2):
                    out.append((device(x, y, z, core), device(*move(x, y, z, core))))
    return out


def send(value, dx=0, dy=0, dz=0, dzl=0, dcore=0):
    def move(x, y, z, core):
        low = z // NZL * NZL + (z % NZL + dzl) % NZL
        return x + dx, y + dy, (low + dz) % (NZL * NZH), core ^ dcore

    return lax.ppermute(value, AXES, pairs(move))


def form_kernel(acts_ref, backs_ref, out_ref, prod_ref):
    count, layers, width, toks = acts_ref.shape
    scale = toks ** (-0.5)
    row = lax.broadcasted_iota(jnp.int32, (count, 128), 0) % 4
    lane = lax.broadcasted_iota(jnp.int32, (count, 128), 1) // width
    turn = (lane - row + 4) % 4
    for layer in range(layers):
        for part in range(count // 8):
            rows = pl.ds(part * 8, 8)
            left = backs_ref[rows, layer].reshape(8 * width, toks)
            right = acts_ref[rows, layer].reshape(8 * width, toks)
            prod = lax.dot_general(left, right, NT, preferred_element_type=jnp.float32)
            for half in range(2):
                here = pl.ds((part * 2 + half) * 128, 128)
                prod_ref[layer, here, :] = prod[half * 128 : half * 128 + 128, half * 128 : half * 128 + 128]
        for group in range(width // 4):
            held = [prod_ref[layer, pl.ds(group * 4 + s, count, stride=width), :] for s in range(4)]
            tile = None
            for r in range(4):
                value = held[r]
                for n in range(1, 4):
                    value = jnp.where(row == n, held[(n + r) % 4], value)
                if r > 0:
                    value = pltpu.roll(value, r * width, 1)
                tile = value if tile is None else jnp.where(turn == r, value, tile)
            at = layer * width * width + group * 128
            out_ref[:, pl.ds(at, 128)] = (tile * scale).astype(out_ref.dtype)


def form_grads(acts, backs, block=16):
    count, layers, width, toks = acts.shape
    entries = layers * width * width
    spec = pl.BlockSpec((block, layers, width, toks), lambda i: (i, 0, 0, 0))
    return pl.pallas_call(
        form_kernel,
        grid=(count // block,),
        in_specs=[spec, spec],
        out_specs=pl.BlockSpec((block, entries), lambda i: (i, 0)),
        out_shape=jax.ShapeDtypeStruct((count, entries), jnp.bfloat16),
        scratch_shapes=[pltpu.VMEM((layers, block * width, 128), jnp.float32)],
        compiler_params=pltpu.CompilerParams(vmem_limit_bytes=32 * MIB),
        cost_estimate=pl.CostEstimate(
            flops=2 * 8 * count * layers * width * width * toks,
            bytes_accessed=count * layers * width * toks * 4 + count * entries * 2,
            transcendentals=0,
        ),
        name="form",
    )(acts, backs)


def whole():
    return pl.BlockSpec(memory_space=pltpu.VMEM)


def apply_kernel(pos_ref, *refs):
    grads, precs = refs[:NX], refs[NX : NX + NZL]
    out_ref, query_ref, rows_ref = refs[NX + NZL :]
    x, zl = pos_ref[0], pos_ref[1]
    for s in range(NX):
        count = grads[s].shape[0]
        at = pl.multiple_of(lax.rem(x + s, NX) * count, count)
        query_ref[pl.ds(at, count), :] = grads[s][...]
    for s in range(NZL):
        count = precs[s].shape[1]
        at = pl.multiple_of(lax.rem(zl + s, NZL) * count, count)
        rows_ref[:, pl.ds(at, count), :] = precs[s][...]
    layers, rows, grad = rows_ref.shape
    for layer in range(layers):
        prod = lax.dot_general(
            query_ref[:, layer * grad : (layer + 1) * grad],
            rows_ref[layer],
            NT,
            preferred_element_type=jnp.float32,
        )
        out_ref[:, layer * rows : (layer + 1) * rows] = prod.astype(out_ref.dtype)


def apply_rows(pos, grads, precs):
    count, entries = grads[0].shape
    layers, rows, grad = precs[0].shape
    return pl.pallas_call(
        apply_kernel,
        in_specs=[pl.BlockSpec(memory_space=pltpu.SMEM)] + [whole()] * (NX + NZL),
        out_specs=whole(),
        out_shape=jax.ShapeDtypeStruct((NX * count, layers * NZL * rows), jnp.bfloat16),
        scratch_shapes=[
            pltpu.VMEM((NX * count, entries), jnp.bfloat16),
            pltpu.VMEM((layers, NZL * rows, grad), jnp.bfloat16),
        ],
        compiler_params=pltpu.CompilerParams(vmem_limit_bytes=32 * MIB),
        cost_estimate=pl.CostEstimate(
            flops=2 * NX * count * entries * NZL * rows, bytes_accessed=3 * MIB, transcendentals=0
        ),
        name="apply",
    )(pos, *grads, *precs)


def join_kernel(pos_ref, *refs):
    parts, out_ref = refs[:NZL], refs[NZL]
    zl = pos_ref[1]
    count = parts[0].shape[0] // NX
    for s in range(NZL):
        at = pl.multiple_of(lax.rem(zl + s, NZL) * count, count)
        for x in range(NX):
            out_ref[x, pl.ds(at, count), :] = parts[s][pl.ds(x * count, count), :]


def join_queries(pos, parts):
    count, width = parts[0].shape
    out = pl.pallas_call(
        join_kernel,
        in_specs=[pl.BlockSpec(memory_space=pltpu.SMEM)] + [whole()] * NZL,
        out_specs=whole(),
        out_shape=jax.ShapeDtypeStruct((NX, NZL * count // NX, width), jnp.bfloat16),
        compiler_params=pltpu.CompilerParams(vmem_limit_bytes=32 * MIB),
        cost_estimate=pl.CostEstimate(flops=0, bytes_accessed=MIB, transcendentals=0),
        name="join",
    )(pos, *parts)
    return out.reshape(NZL * count, width)


def score_kernel(scale, pos_ref, *refs):
    trains, queries = refs[:NY], refs[NY : NY + NX]
    out_ref, right_ref = refs[NY + NX :]
    x = pos_ref[0]
    layers = 2
    rows = queries[0].shape[1] // layers
    for s in range(NX):
        for layer in range(layers):
            at = layer * NX * rows + lax.rem(x + s, NX) * rows
            right_ref[:, pl.ds(pl.multiple_of(at, rows), rows)] = queries[s][:, layer * rows : (layer + 1) * rows]
    count = trains[0].shape[0]
    for s in range(NY):
        prod = lax.dot_general(trains[s][...], right_ref[...], NT, preferred_element_type=jnp.float32)
        out_ref[s * count : (s + 1) * count, :] = (prod * scale).astype(out_ref.dtype)


def score_terms(pos, trains, queries, scale):
    count, entries = trains[0].shape
    columns = queries[0].shape[0]
    return pl.pallas_call(
        functools.partial(score_kernel, scale),
        in_specs=[pl.BlockSpec(memory_space=pltpu.SMEM)] + [whole()] * (NY + NX),
        out_specs=whole(),
        out_shape=jax.ShapeDtypeStruct((NY * count, columns), jnp.bfloat16),
        scratch_shapes=[pltpu.VMEM((columns, entries), jnp.bfloat16)],
        compiler_params=pltpu.CompilerParams(vmem_limit_bytes=40 * MIB),
        cost_estimate=pl.CostEstimate(
            flops=2 * NY * count * entries * columns, bytes_accessed=5 * MIB, transcendentals=0
        ),
        name="score",
    )(pos, *trains, *queries)


def add_kernel(pos_ref, own_ref, other_ref, *refs):
    out_ref = refs[-1]
    out_ref[...] = own_ref[...].astype(jnp.float32) + other_ref[...].astype(jnp.float32)


def add_terms(places, own, other, total, held=None):
    count = own.shape[0] // NY
    columns = own.shape[1]
    spec = pl.BlockSpec((count, columns), lambda i, places: (i, 0))
    extra = [] if held is None else [held]
    return pl.pallas_call(
        add_kernel,
        grid_spec=pltpu.PrefetchScalarGridSpec(
            num_scalar_prefetch=1,
            grid=(NY,),
            in_specs=[spec, spec] + [pl.BlockSpec(memory_space=pl.ANY)] * len(extra),
            out_specs=pl.BlockSpec((count, columns), lambda i, places: (places[i], 0)),
        ),
        out_shape=jax.ShapeDtypeStruct((total, columns), jnp.float32),
        input_output_aliases={} if held is None else {3: 0},
        compiler_params=pltpu.CompilerParams(vmem_limit_bytes=32 * MIB),
        cost_estimate=pl.CostEstimate(flops=own.size, bytes_accessed=own.size * 8, transcendentals=0),
        name="add",
    )(places, own, other, *extra)


def per_device(train_acts, train_backs, query_acts, query_backs, precond):
    t, k = lax.axis_index("train"), lax.axis_index("query")
    x, zl, y, zh = t // NZL, t % NZL, k // NZH, k % NZH
    pos = jnp.stack([x, zl, y, zh]).astype(jnp.int32)
    precs = [precond, send(precond, dz=-1), send(precond, dz=2), send(precond, dz=1)]
    query_grad = form_grads(query_acts[0], query_backs[0])
    grads = [query_grad, send(query_grad, dx=-1), send(query_grad, dx=2), send(query_grad, dx=1)]
    train_grad = form_grads(train_acts, train_backs)
    far_grad = send(train_grad, dz=NZL)
    near = [train_grad, send(train_grad, dy=-1), send(train_grad, dy=2), send(train_grad, dy=1)]
    part = apply_rows(pos, grads, precs)
    parts = [part] + [send(part, dzl=-s) for s in (1, 2, 3)]
    mine = join_queries(pos, parts)
    queries = [mine, send(mine, dx=-1), send(mine, dx=2), send(mine, dx=1)]
    far = [far_grad, send(far_grad, dy=-1), send(far_grad, dy=2), send(far_grad, dy=1)]
    layers = train_acts.shape[1] * lax.axis_size("layer")
    scale = (layers * train_acts.shape[2] * train_backs.shape[2]) ** (-0.5)
    total = train_acts.shape[0] * lax.axis_size("query")
    steps = jnp.arange(NY, dtype=jnp.int32)
    near_terms = score_terms(pos, near, queries, scale)
    near_other = send(near_terms, dcore=1)
    far_terms = score_terms(pos, far, queries, scale)
    far_other = send(far_terms, dcore=1)
    ys = (y + steps) % NY * NZH
    out = add_terms((ys + zh).astype(jnp.int32), near_terms, near_other, total)
    return add_terms((ys + 1 - zh).astype(jnp.int32), far_terms, far_other, total, out)


def solution(mesh):
    in_specs = (
        P(("train", "query"), "layer", None, None),
        P(("train", "query"), "layer", None, None),
        P("query", "train", "layer", None, None),
        P("query", "train", "layer", None, None),
        P("layer", "train", None),
    )
    out_specs = P("train", "query")
    return jax.shard_map(
        per_device, mesh=mesh, in_specs=in_specs, out_specs=out_specs, check_vma=False
    )
```

time: 359 us -> 113 us (0.31)
  waiting for transfers between devices: 317 us -> 50.1 us
  starting transfers between devices: 0.12 us -> 35.6 us
  Pallas kernels: 0 us -> 19.5 us
  matrix products: 18.2 us -> 0 us
  between operations: 13.1 us -> 0.08 us
    all_gather x3 -> x0, waiting for transfers between devices: 286 us -> none  [the longest x1 117 us: per_device(): piece = lax.all_gather(train_grad, 'query', axis=0, tiled=True)]
    ppermute x0 -> x21, waiting for transfers between devices: none -> 50.1 us  [send(): return lax.ppermute(value, AXES, pairs(move))]
    ppermute x0 -> x21, starting transfers between devices: none -> 35.6 us  [send(): return lax.ppermute(value, AXES, pairs(move))]
    psum x1 -> x0, waiting for transfers between devices: 30.3 us -> none  [per_device(): return lax.psum(partial_scores, 'layer')]
    pallas_call x0 -> x8, Pallas kernels: none -> 19.5 us  [the longest x2 7.15 us: score_terms(): pl.pallas_call(functools.partial(score_kernel, scale), in_specs=[pl.Block...]
    dot_general x3 -> x0, matrix products: 18.2 us -> none  [the longest x1 9.9 us: per_device(): lax.dot_general(left_side, right_side, (((1,), (1,)), ((), ())), preferre...]
    dot_general x1 -> x0, local copies, waits for them, and re-layouts: 3.74 us -> none  [form_grads(): jnp.einsum('nlbt,nlat->nlba', backs, acts, preferred_element_type=jnp.flo...]
    unnamed x3 -> x10, local copies, waits for them, and re-layouts: 4.3 us -> 7.77 us
  transfers between devices with their start and end apart: 4 -> 21, of which waited for: 4 -> 8; matrix products, arithmetic and copies ran while one was open for 3% -> 0% of each run, Pallas kernels for 0% -> 13%
where the time goes in v1:
time: 113 us
  waiting for transfers between devices  50.1 us (44%)
  starting transfers between devices  35.6 us (32%)
  Pallas kernels  19.5 us (17%)
  local copies, waits for them, and re-layouts  7.77 us (7%)
    ppermute x21, waiting for transfers between devices, send(): return lax.ppermute(value, AXES, pairs(move))  50.1 us
    ppermute x21, starting transfers between devices, send(): return lax.ppermute(value, AXES, pairs(move))  35.6 us
    unnamed x10, local copies, waits for them, and re-layouts  7.77 us
    pallas_call x2, Pallas kernels, score_terms(): pl.pallas_call(functools.partial(score_kernel, scale), in_specs=[pl.Block...  7.15 us
    pallas_call x2, Pallas kernels, form_grads(): pl.pallas_call(form_kernel, grid=(count // block,), in_specs=[spec, spec]...  6.37 us
    pallas_call x2, Pallas kernels, add_terms(): pl.pallas_call(add_kernel, grid_spec=pltpu.PrefetchScalarGridSpec(num_sca...  4.22 us
  transfers between devices with their start and end apart: 21, of which 8 were waited for; matrix products, arithmetic and copies ran while one was open for 0% of the time, Pallas kernels for 13%

profile of v1, /device:TPU:1, one launch (start us, length us, event | category | flops | bytes accessed | tf_op | source)
XLA Modules:
  0.0 113.1 jit_solution(10218789657464727818)
XLA Ops:
  0.0 0.0 copy-start.2
  0.0 1.2 %copy-done.2 = bf16[1,32,2,32,256]{4,3,2,1,0:T(8,128)(2,1)S(1)} copy-done((bf16[1,32,2,32,256]{4,3,2,1,0:T(8,128)(2,1)S(1)}, bf16[1,32,2,32,256]{4,3,2,1,0:T(8,128)(2,1)}, u32[]{:S(2)}) %copy-start.2) | copy-done | bytes 1048600
  1.2 0.0 copy-start.3
  1.2 1.2 %copy-done.3 = bf16[1,32,2,32,256]{4,3,2,1,0:T(8,128)(2,1)S(1)} copy-done((bf16[1,32,2,32,256]{4,3,2,1,0:T(8,128)(2,1)S(1)}, bf16[1,32,2,32,256]{4,3,2,1,0:T(8,128)(2,1)}, u32[]{:S(2)}) %copy-start.3) | copy-done | bytes 1048600
  2.5 1.3 %form.3.refs_0_ = bf16[32,2048]{1,0:T(8,128)(2,1)S(1)} custom-call(bf16[32,2,32,256]{3,2,1,0:T(8,128)(2,1)S(1)} %bitcast.12, bf16[32,2,32,256]{3,2,1,0:T(8,128)(2,1)S(1)} %bitcast.13), custom_call_target="tpu_custom_call" | custom-call | flops 268435456 | bytes 2228224 | tf_op jit(solution)/shard_map/form/pallas_call | solution.py:71
  3.7 3.4 %collective-permute-start.4 = (bf16[32,2048]{1,0:T(8,128)(2,1)S(1)}, bf16[32,2048]{1,0:T(8,128)(2,1)S(1)}, u32[]{:S(2)}, u32[]{:S(2)}) collective-permute-start(bf16[32,2048]{1,0:T(8,128)(2,1)S(1)} %form.3.refs_0_), channel_id=1, source_target_pairs={{0,192},{1,193},{16,208},{17,209},{32,224},{33,225},{48,240},{49,2... | collective-permute-start | bytes 393224 | tf_op jit(solution)/shard_map/ppermute | solution.py:35
  7.1 5.6 %collective-permute-start.7 = (bf16[2,64,1024]{2,1,0:T(8,128)(2,1)}, bf16[2,64,1024]{2,1,0:T(8,128)(2,1)S(1)}, u32[]{:S(2)}, u32[]{:S(2)}) collective-permute-start(bf16[2,64,1024]{2,1,0:T(8,128)(2,1)} %refs_4_.1), channel_id=1, source_target_pairs={{0,50},{1,51},{16,0},{17,1},{32,16},{33,17},{48,32},{49,33},{2,48}... | collective-permute-start | bytes 786440 | tf_op jit(solution)/shard_map/ppermute | solution.py:35
  12.7 0.0 collective-permute-start.8
  12.7 0.0 collective-permute-start.9
  12.7 0.5 collective-permute-start.5
  13.2 0.0 collective-permute-done.4.refs_1_
  13.2 0.6 collective-permute-start.6
  13.8 0.1 pad_add_fusion.pos_ref
  13.9 4.2 %collective-permute-done.5.refs_2_ = bf16[32,2048]{1,0:T(8,128)(2,1)S(1)} collective-permute-done((bf16[32,2048]{1,0:T(8,128)(2,1)S(1)}, bf16[32,2048]{1,0:T(8,128)(2,1)S(1)}, u32[]{:S(2)}, u32[]{:S(2)}) %collective-permute-start.5) | collective-permute-done | bytes 131104 | tf_op jit(solution)/shard_map/ppermute | solution.py:35
  18.1 3.8 %collective-permute-done.6.refs_3_ = bf16[32,2048]{1,0:T(8,128)(2,1)S(1)} collective-permute-done((bf16[32,2048]{1,0:T(8,128)(2,1)S(1)}, bf16[32,2048]{1,0:T(8,128)(2,1)S(1)}, u32[]{:S(2)}, u32[]{:S(2)}) %collective-permute-start.6) | collective-permute-done | bytes 131104 | tf_op jit(solution)/shard_map/ppermute | solution.py:35
  21.9 0.0 collective-permute-done.7.refs_5_
  21.9 3.0 %collective-permute-done.8.refs_6_ = bf16[2,64,1024]{2,1,0:T(8,128)(2,1)S(1)} collective-permute-done((bf16[2,64,1024]{2,1,0:T(8,128)(2,1)}, bf16[2,64,1024]{2,1,0:T(8,128)(2,1)S(1)}, u32[]{:S(2)}, u32[]{:S(2)}) %collective-permute-start.8) | collective-permute-done | bytes 262176 | tf_op jit(solution)/shard_map/ppermute | solution.py:35
  24.8 5.5 %collective-permute-done.9.refs_7_ = bf16[2,64,1024]{2,1,0:T(8,128)(2,1)S(1)} collective-permute-done((bf16[2,64,1024]{2,1,0:T(8,128)(2,1)}, bf16[2,64,1024]{2,1,0:T(8,128)(2,1)S(1)}, u32[]{:S(2)}, u32[]{:S(2)}) %collective-permute-start.9) | collective-permute-done | bytes 262176 | tf_op jit(solution)/shard_map/ppermute | solution.py:35
  30.3 0.0 copy-start.4
  30.3 0.9 copy-done.4
  31.3 1.1 %apply.1.refs_0_ = bf16[128,512]{1,0:T(8,128)(2,1)S(1)} custom-call(s32[4]{0:T(128)S(1)} %pad_add_fusion.pos_ref, bf16[32,2048]{1,0:T(8,128)(2,1)S(1)} %form.3.refs_0_, bf16[32,2048]{1,0:T(8,128)(2,1)S(1)} %collective-permute-done.4.refs_1_, bf16[32,2048]{1,0:T(8,128)(2,1)S(1)} %collective-permute-done.5.refs_2_, ...), custom_call_target="tpu_custom_call" | custom-call | flops 134217728 | bytes 3145728 | tf_op jit(solution)/shard_map/apply/pallas_call | solution.py:118
  32.4 1.8 %collective-permute-start.10 = (bf16[128,512]{1,0:T(8,128)(2,1)S(1)}, bf16[128,512]{1,0:T(8,128)(2,1)S(1)}, u32[]{:S(2)}, u32[]{:S(2)}) collective-permute-start(bf16[128,512]{1,0:T(8,128)(2,1)S(1)} %apply.1.refs_0_), channel_id=1, source_target_pairs={{0,48},{1,49},{16,0},{17,1},{32,16},{33,17},{48,32},{49,33},{2,50}... | collective-permute-start | bytes 393224 | tf_op jit(solution)/shard_map/ppermute | solution.py:35
  34.2 1.1 %collective-permute-start.11 = (bf16[128,512]{1,0:T(8,128)(2,1)S(1)}, bf16[128,512]{1,0:T(8,128)(2,1)S(1)}, u32[]{:S(2)}, u32[]{:S(2)}) collective-permute-start(bf16[128,512]{1,0:T(8,128)(2,1)S(1)} %apply.1.refs_0_), channel_id=1, source_target_pairs={{0,32},{1,33},{16,48},{17,49},{32,0},{33,1},{48,16},{49,17},{2,34}... | collective-permute-start | bytes 393224 | tf_op jit(solution)/shard_map/ppermute | solution.py:35
  35.3 0.0 collective-permute-start.12
  35.3 0.0 copy-start
  35.3 2.2 %copy-done = bf16[128,2,32,256]{3,2,1,0:T(8,128)(2,1)S(1)} copy-done((bf16[128,2,32,256]{3,2,1,0:T(8,128)(2,1)S(1)}, bf16[128,2,32,256]{3,2,1,0:T(8,128)(2,1)}, u32[]{:S(2)}) %copy-start) | copy-done | bytes 4194328
  37.5 0.0 copy-start.1
  37.5 2.2 %copy-done.1 = bf16[128,2,32,256]{3,2,1,0:T(8,128)(2,1)S(1)} copy-done((bf16[128,2,32,256]{3,2,1,0:T(8,128)(2,1)S(1)}, bf16[128,2,32,256]{3,2,1,0:T(8,128)(2,1)}, u32[]{:S(2)}) %copy-start.1) | copy-done | bytes 4194328
  39.7 5.1 %form.2.refs_0_ = bf16[128,2048]{1,0:T(8,128)(2,1)S(1)} custom-call(bf16[128,2,32,256]{3,2,1,0:T(8,128)(2,1)S(1)} %copy-done, bf16[128,2,32,256]{3,2,1,0:T(8,128)(2,1)S(1)} %copy-done.1), custom_call_target="tpu_custom_call" | custom-call | flops 1073741824 | bytes 8912896 | tf_op jit(solution)/shard_map/form/pallas_call | solution.py:71
  44.8 4.0 %collective-permute-start = (bf16[128,2048]{1,0:T(8,128)(2,1)S(1)}, bf16[128,2048]{1,0:T(8,128)(2,1)S(1)}, u32[]{:S(2)}, u32[]{:S(2)}) collective-permute-start(bf16[128,2048]{1,0:T(8,128)(2,1)S(1)} %form.2.refs_0_), channel_id=1, source_target_pairs={{0,2},{1,3},{16,18},{17,19},{32,34},{33,35},{48,50},{49,51},{2,0},... | collective-permute-start | bytes 1572872 | tf_op jit(solution)/shard_map/ppermute | solution.py:35
  48.8 2.7 %collective-permute-start.17 = (bf16[128,2048]{1,0:T(8,128)(2,1)S(1)}, bf16[128,2048]{1,0:T(8,128)(2,1)S(1)}, u32[]{:S(2)}, u32[]{:S(2)}) collective-permute-start(bf16[128,2048]{1,0:T(8,128)(2,1)S(1)} %form.2.refs_0_), channel_id=1, source_target_pairs={{0,12},{1,13},{16,28},{17,29},{32,44},{33,45},{48,60},{49,61},{2,1... | collective-permute-start | bytes 1572872 | tf_op jit(solution)/shard_map/ppermute | solution.py:35
  51.5 0.0 collective-permute-done.10.refs_1_
  51.5 0.3 collective-permute-start.18
  51.9 0.0 collective-permute-done.11.refs_2_
  51.9 0.7 collective-permute-start.19
  52.6 0.0 collective-permute-done.12.refs_3_
  52.6 0.6 join.1
  53.2 0.6 collective-permute-start.13
  53.8 9.3 %collective-permute-done.refs_0_ = bf16[128,2048]{1,0:T(8,128)(2,1)S(1)} collective-permute-done((bf16[128,2048]{1,0:T(8,128)(2,1)S(1)}, bf16[128,2048]{1,0:T(8,128)(2,1)S(1)}, u32[]{:S(2)}, u32[]{:S(2)}) %collective-permute-start) | collective-permute-done | bytes 524320 | tf_op jit(solution)/shard_map/ppermute | solution.py:35
  63.1 0.5 collective-permute-start.14
  63.6 0.0 collective-permute-done.17.refs_1_
  63.6 0.6 collective-permute-start.15
  64.2 0.0 collective-permute-done.18.refs_2_
  64.2 9.5 %collective-permute-start.1 = (bf16[128,2048]{1,0:T(8,128)(2,1)S(1)}, bf16[128,2048]{1,0:T(8,128)(2,1)S(1)}, u32[]{:S(2)}, u32[]{:S(2)}) collective-permute-start(bf16[128,2048]{1,0:T(8,128)(2,1)S(1)} %collective-permute-done.refs_0_), channel_id=1, source_target_pairs={{0,12},{1,13},{16,28},{17,29},{32,44},{33,45},{48,60},{49,61},{2,1... | collective-permute-start | bytes 1572872 | tf_op jit(solution)/shard_map/ppermute | solution.py:35
  73.7 4.4 %collective-permute-done.19.refs_3_ = bf16[128,2048]{1,0:T(8,128)(2,1)S(1)} collective-permute-done((bf16[128,2048]{1,0:T(8,128)(2,1)S(1)}, bf16[128,2048]{1,0:T(8,128)(2,1)S(1)}, u32[]{:S(2)}, u32[]{:S(2)}) %collective-permute-start.19) | collective-permute-done | bytes 524320 | tf_op jit(solution)/shard_map/ppermute | solution.py:35
  78.1 0.3 collective-permute-start.2
  78.5 0.0 collective-permute-done.13.refs_5_
  78.5 0.0 collective-permute-start.3
  78.5 0.0 collective-permute-done.14.refs_6_
  78.5 9.1 %collective-permute-done.15.refs_7_ = bf16[512,512]{1,0:T(8,128)(2,1)S(1)} collective-permute-done((bf16[512,512]{1,0:T(8,128)(2,1)S(1)}, bf16[512,512]{1,0:T(8,128)(2,1)S(1)}, u32[]{:S(2)}, u32[]{:S(2)}) %collective-permute-start.15) | collective-permute-done | bytes 524320 | tf_op jit(solution)/shard_map/ppermute | solution.py:35
  87.6 3.6 %score.3.own_ref = bf16[512,512]{1,0:T(8,128)(2,1)S(1)} custom-call(s32[4]{0:T(128)S(1)} %pad_add_fusion.pos_ref, bf16[128,2048]{1,0:T(8,128)(2,1)S(1)} %form.2.refs_0_, bf16[128,2048]{1,0:T(8,128)(2,1)S(1)} %collective-permute-done.17.refs_1_, bf16[128,2048]{1,0:T(8,128)(2,1)S(1)} %collective-permute-done.18.refs_2_, ...), custom_call_target="tpu_custom_call" | custom-call | flops 1073741824 | bytes 5242880 | tf_op jit(solution)/shard_map/score/pallas_call | solution.py:178
  91.1 2.7 %collective-permute-start.20 = (bf16[512,512]{1,0:T(8,128)(2,1)S(1)}, bf16[512,512]{1,0:T(8,128)(2,1)S(1)}, u32[]{:S(2)}, u32[]{:S(2)}) collective-permute-start(bf16[512,512]{1,0:T(8,128)(2,1)S(1)} %score.3.own_ref), channel_id=1, source_target_pairs={{0,1},{1,0},{16,17},{17,16},{32,33},{33,32},{48,49},{49,48},{2,3},... | collective-permute-start | bytes 1572872 | tf_op jit(solution)/shard_map/ppermute | solution.py:35
  93.8 0.0 collective-permute-done.1.refs_1_
  93.8 0.0 collective-permute-done.2.refs_2_
  93.8 10.9 %collective-permute-done.3.refs_3_ = bf16[128,2048]{1,0:T(8,128)(2,1)S(1)} collective-permute-done((bf16[128,2048]{1,0:T(8,128)(2,1)S(1)}, bf16[128,2048]{1,0:T(8,128)(2,1)S(1)}, u32[]{:S(2)}, u32[]{:S(2)}) %collective-permute-start.3) | collective-permute-done | bytes 524320 | tf_op jit(solution)/shard_map/ppermute | solution.py:35
  104.7 3.6 %score.2.own_ref = bf16[512,512]{1,0:T(8,128)(2,1)S(1)} custom-call(s32[4]{0:T(128)S(1)} %pad_add_fusion.pos_ref, bf16[128,2048]{1,0:T(8,128)(2,1)S(1)} %collective-permute-done.refs_0_, bf16[128,2048]{1,0:T(8,128)(2,1)S(1)} %collective-permute-done.1.refs_1_, bf16[128,2048]{1,0:T(8,128)(2,1)S(1)} %collective-permute-done.2.refs_2_, ...), custom_call_target="tpu_custom_call" | custom-call | flops 1073741824 | bytes 5242880 | tf_op jit(solution)/shard_map/score/pallas_call | solution.py:178
  108.3 0.6 collective-permute-start.16
  108.9 0.0 collective-permute-done.20.other_ref
  108.9 2.1 %add.62.refs_0_ = f32[1024,512]{1,0:T(8,128)} custom-call(s32[4]{0:T(128)S(1)} %get-tuple-element.6.pos_ref, bf16[512,512]{1,0:T(8,128)(2,1)S(1)} %score.3.own_ref, bf16[512,512]{1,0:T(8,128)(2,1)S(1)} %collective-permute-done.20.other_ref), custom_call_target="tpu_custom_call" | custom-call | flops 262144 | bytes 2097152 | tf_op jit(solution)/shard_map/add/pallas_call | solution.py:202
  111.0 0.0 collective-permute-done.16.other_ref
  111.0 2.1 %add.63 = f32[1024,512]{1,0:T(8,128)} custom-call(s32[4]{0:T(128)S(1)} %get-tuple-element.5.pos_ref, bf16[512,512]{1,0:T(8,128)(2,1)S(1)} %score.2.own_ref, bf16[512,512]{1,0:T(8,128)(2,1)S(1)} %collective-permute-done.16.other_ref, f32[1024,512]{1,0:T(8,128)} %add.62.refs_0_), custom_call_target="tpu_custom_call", output_to_operand_aliasing={{}: (3, {})} | custom-call | flops 262144 | bytes 2097152 | tf_op jit(solution)/shard_map/add/pallas_call | solution.py:202
  (1 shorter events, 0.0 us)
Async XLA Ops:
  0.0 1.2 %copy-start.2 = (bf16[1,32,2,32,256]{4,3,2,1,0:T(8,128)(2,1)S(1)}, bf16[1,32,2,32,256]{4,3,2,1,0:T(8,128)(2,1)}, u32[]{:S(2)}) copy-start(bf16[1,32,2,32,256]{4,3,2,1,0:T(8,128)(2,1)} %param.7) | copy-start | bytes 3145732
  1.2 1.2 %copy-start.3 = (bf16[1,32,2,32,256]{4,3,2,1,0:T(8,128)(2,1)S(1)}, bf16[1,32,2,32,256]{4,3,2,1,0:T(8,128)(2,1)}, u32[]{:S(2)}) copy-start(bf16[1,32,2,32,256]{4,3,2,1,0:T(8,128)(2,1)} %param.8) | copy-start | bytes 3145732
  3.7 9.5 %collective-permute-start.4 = (bf16[32,2048]{1,0:T(8,128)(2,1)S(1)}, bf16[32,2048]{1,0:T(8,128)(2,1)S(1)}, u32[]{:S(2)}, u32[]{:S(2)}) collective-permute-start(bf16[32,2048]{1,0:T(8,128)(2,1)S(1)} %form.3.refs_0_), channel_id=1, source_target_pairs={{0,192},{1,193},{16,208},{17,209},{32,224},{33,225},{48,240},{49,2... | collective-permute-start | bytes 393224 | tf_op jit(solution)/shard_map/ppermute | solution.py:35
  7.1 14.8 %collective-permute-start.7 = (bf16[2,64,1024]{2,1,0:T(8,128)(2,1)}, bf16[2,64,1024]{2,1,0:T(8,128)(2,1)S(1)}, u32[]{:S(2)}, u32[]{:S(2)}) collective-permute-start(bf16[2,64,1024]{2,1,0:T(8,128)(2,1)} %refs_4_.1), channel_id=1, source_target_pairs={{0,50},{1,51},{16,0},{17,1},{32,16},{33,17},{48,32},{49,33},{2,48}... | collective-permute-start | bytes 786440 | tf_op jit(solution)/shard_map/ppermute | solution.py:35
  12.7 12.2 %collective-permute-start.8 = (bf16[2,64,1024]{2,1,0:T(8,128)(2,1)}, bf16[2,64,1024]{2,1,0:T(8,128)(2,1)S(1)}, u32[]{:S(2)}, u32[]{:S(2)}) collective-permute-start(bf16[2,64,1024]{2,1,0:T(8,128)(2,1)} %refs_4_.1), channel_id=1, source_target_pairs={{0,32},{1,33},{16,48},{17,49},{32,2},{33,3},{48,18},{49,19},{2,34}... | collective-permute-start | bytes 786440 | tf_op jit(solution)/shard_map/ppermute | solution.py:35
  12.7 17.6 %collective-permute-start.9 = (bf16[2,64,1024]{2,1,0:T(8,128)(2,1)}, bf16[2,64,1024]{2,1,0:T(8,128)(2,1)S(1)}, u32[]{:S(2)}, u32[]{:S(2)}) collective-permute-start(bf16[2,64,1024]{2,1,0:T(8,128)(2,1)} %refs_4_.1), channel_id=1, source_target_pairs={{0,16},{1,17},{16,32},{17,33},{32,48},{33,49},{48,2},{49,3},{2,18}... | collective-permute-start | bytes 786440 | tf_op jit(solution)/shard_map/ppermute | solution.py:35
  12.7 5.4 %collective-permute-start.5 = (bf16[32,2048]{1,0:T(8,128)(2,1)S(1)}, bf16[32,2048]{1,0:T(8,128)(2,1)S(1)}, u32[]{:S(2)}, u32[]{:S(2)}) collective-permute-start(bf16[32,2048]{1,0:T(8,128)(2,1)S(1)} %form.3.refs_0_), channel_id=1, source_target_pairs={{0,128},{1,129},{16,144},{17,145},{32,160},{33,161},{48,176},{49,1... | collective-permute-start | bytes 393224 | tf_op jit(solution)/shard_map/ppermute | solution.py:35
  13.2 8.7 %collective-permute-start.6 = (bf16[32,2048]{1,0:T(8,128)(2,1)S(1)}, bf16[32,2048]{1,0:T(8,128)(2,1)S(1)}, u32[]{:S(2)}, u32[]{:S(2)}) collective-permute-start(bf16[32,2048]{1,0:T(8,128)(2,1)S(1)} %form.3.refs_0_), channel_id=1, source_target_pairs={{0,64},{1,65},{16,80},{17,81},{32,96},{33,97},{48,112},{49,113},{2... | collective-permute-start | bytes 393224 | tf_op jit(solution)/shard_map/ppermute | solution.py:35
  30.3 1.0 copy-start.4
  32.4 19.1 %collective-permute-start.10 = (bf16[128,512]{1,0:T(8,128)(2,1)S(1)}, bf16[128,512]{1,0:T(8,128)(2,1)S(1)}, u32[]{:S(2)}, u32[]{:S(2)}) collective-permute-start(bf16[128,512]{1,0:T(8,128)(2,1)S(1)} %apply.1.refs_0_), channel_id=1, source_target_pairs={{0,48},{1,49},{16,0},{17,1},{32,16},{33,17},{48,32},{49,33},{2,50}... | collective-permute-start | bytes 393224 | tf_op jit(solution)/shard_map/ppermute | solution.py:35
  34.2 17.7 %collective-permute-start.11 = (bf16[128,512]{1,0:T(8,128)(2,1)S(1)}, bf16[128,512]{1,0:T(8,128)(2,1)S(1)}, u32[]{:S(2)}, u32[]{:S(2)}) collective-permute-start(bf16[128,512]{1,0:T(8,128)(2,1)S(1)} %apply.1.refs_0_), channel_id=1, source_target_pairs={{0,32},{1,33},{16,48},{17,49},{32,0},{33,1},{48,16},{49,17},{2,34}... | collective-permute-start | bytes 393224 | tf_op jit(solution)/shard_map/ppermute | solution.py:35
  35.3 17.3 %collective-permute-start.12 = (bf16[128,512]{1,0:T(8,128)(2,1)S(1)}, bf16[128,512]{1,0:T(8,128)(2,1)S(1)}, u32[]{:S(2)}, u32[]{:S(2)}) collective-permute-start(bf16[128,512]{1,0:T(8,128)(2,1)S(1)} %apply.1.refs_0_), channel_id=1, source_target_pairs={{0,16},{1,17},{16,32},{17,33},{32,48},{33,49},{48,0},{49,1},{2,18}... | collective-permute-start | bytes 393224 | tf_op jit(solution)/shard_map/ppermute | solution.py:35
  35.3 2.2 %copy-start = (bf16[128,2,32,256]{3,2,1,0:T(8,128)(2,1)S(1)}, bf16[128,2,32,256]{3,2,1,0:T(8,128)(2,1)}, u32[]{:S(2)}) copy-start(bf16[128,2,32,256]{3,2,1,0:T(8,128)(2,1)} %acts_ref.1) | copy-start | bytes 12582916
  37.5 2.2 %copy-start.1 = (bf16[128,2,32,256]{3,2,1,0:T(8,128)(2,1)S(1)}, bf16[128,2,32,256]{3,2,1,0:T(8,128)(2,1)}, u32[]{:S(2)}) copy-start(bf16[128,2,32,256]{3,2,1,0:T(8,128)(2,1)} %backs_ref.1) | copy-start | bytes 12582916
  44.8 18.3 %collective-permute-start = (bf16[128,2048]{1,0:T(8,128)(2,1)S(1)}, bf16[128,2048]{1,0:T(8,128)(2,1)S(1)}, u32[]{:S(2)}, u32[]{:S(2)}) collective-permute-start(bf16[128,2048]{1,0:T(8,128)(2,1)S(1)} %form.2.refs_0_), channel_id=1, source_target_pairs={{0,2},{1,3},{16,18},{17,19},{32,34},{33,35},{48,50},{49,51},{2,0},... | collective-permute-start | bytes 1572872 | tf_op jit(solution)/shard_map/ppermute | solution.py:35
  48.8 14.8 %collective-permute-start.17 = (bf16[128,2048]{1,0:T(8,128)(2,1)S(1)}, bf16[128,2048]{1,0:T(8,128)(2,1)S(1)}, u32[]{:S(2)}, u32[]{:S(2)}) collective-permute-start(bf16[128,2048]{1,0:T(8,128)(2,1)S(1)} %form.2.refs_0_), channel_id=1, source_target_pairs={{0,12},{1,13},{16,28},{17,29},{32,44},{33,45},{48,60},{49,61},{2,1... | collective-permute-start | bytes 1572872 | tf_op jit(solution)/shard_map/ppermute | solution.py:35
  51.5 12.7 %collective-permute-start.18 = (bf16[128,2048]{1,0:T(8,128)(2,1)S(1)}, bf16[128,2048]{1,0:T(8,128)(2,1)S(1)}, u32[]{:S(2)}, u32[]{:S(2)}) collective-permute-start(bf16[128,2048]{1,0:T(8,128)(2,1)S(1)} %form.2.refs_0_), channel_id=1, source_target_pairs={{0,8},{1,9},{16,24},{17,25},{32,40},{33,41},{48,56},{49,57},{2,10}... | collective-permute-start | bytes 1572872 | tf_op jit(solution)/shard_map/ppermute | solution.py:35
  51.9 26.2 %collective-permute-start.19 = (bf16[128,2048]{1,0:T(8,128)(2,1)S(1)}, bf16[128,2048]{1,0:T(8,128)(2,1)S(1)}, u32[]{:S(2)}, u32[]{:S(2)}) collective-permute-start(bf16[128,2048]{1,0:T(8,128)(2,1)S(1)} %form.2.refs_0_), channel_id=1, source_target_pairs={{0,4},{1,5},{16,20},{17,21},{32,36},{33,37},{48,52},{49,53},{2,6},... | collective-permute-start | bytes 1572872 | tf_op jit(solution)/shard_map/ppermute | solution.py:35
  53.2 25.3 %collective-permute-start.13 = (bf16[512,512]{1,0:T(8,128)(2,1)S(1)}, bf16[512,512]{1,0:T(8,128)(2,1)S(1)}, u32[]{:S(2)}, u32[]{:S(2)}) collective-permute-start(bf16[512,512]{1,0:T(8,128)(2,1)S(1)} %bitcast.7), channel_id=1, source_target_pairs={{0,192},{1,193},{16,208},{17,209},{32,224},{33,225},{48,240},{49,2... | collective-permute-start | bytes 1572872 | tf_op jit(solution)/shard_map/ppermute | solution.py:35
  63.1 15.4 %collective-permute-start.14 = (bf16[512,512]{1,0:T(8,128)(2,1)S(1)}, bf16[512,512]{1,0:T(8,128)(2,1)S(1)}, u32[]{:S(2)}, u32[]{:S(2)}) collective-permute-start(bf16[512,512]{1,0:T(8,128)(2,1)S(1)} %bitcast.8), channel_id=1, source_target_pairs={{0,128},{1,129},{16,144},{17,145},{32,160},{33,161},{48,176},{49,1... | collective-permute-start | bytes 1572872 | tf_op jit(solution)/shard_map/ppermute | solution.py:35
  63.6 24.0 %collective-permute-start.15 = (bf16[512,512]{1,0:T(8,128)(2,1)S(1)}, bf16[512,512]{1,0:T(8,128)(2,1)S(1)}, u32[]{:S(2)}, u32[]{:S(2)}) collective-permute-start(bf16[512,512]{1,0:T(8,128)(2,1)S(1)} %bitcast.9), channel_id=1, source_target_pairs={{0,64},{1,65},{16,80},{17,81},{32,96},{33,97},{48,112},{49,113},{2... | collective-permute-start | bytes 1572872 | tf_op jit(solution)/shard_map/ppermute | solution.py:35
  64.2 29.6 %collective-permute-start.1 = (bf16[128,2048]{1,0:T(8,128)(2,1)S(1)}, bf16[128,2048]{1,0:T(8,128)(2,1)S(1)}, u32[]{:S(2)}, u32[]{:S(2)}) collective-permute-start(bf16[128,2048]{1,0:T(8,128)(2,1)S(1)} %collective-permute-done.refs_0_), channel_id=1, source_target_pairs={{0,12},{1,13},{16,28},{17,29},{32,44},{33,45},{48,60},{49,61},{2,1... | collective-permute-start | bytes 1572872 | tf_op jit(solution)/shard_map/ppermute | solution.py:35
  78.1 15.7 %collective-permute-start.2 = (bf16[128,2048]{1,0:T(8,128)(2,1)S(1)}, bf16[128,2048]{1,0:T(8,128)(2,1)S(1)}, u32[]{:S(2)}, u32[]{:S(2)}) collective-permute-start(bf16[128,2048]{1,0:T(8,128)(2,1)S(1)} %collective-permute-done.refs_0_), channel_id=1, source_target_pairs={{0,8},{1,9},{16,24},{17,25},{32,40},{33,41},{48,56},{49,57},{2,10}... | collective-permute-start | bytes 1572872 | tf_op jit(solution)/shard_map/ppermute | solution.py:35
  78.5 26.2 %collective-permute-start.3 = (bf16[128,2048]{1,0:T(8,128)(2,1)S(1)}, bf16[128,2048]{1,0:T(8,128)(2,1)S(1)}, u32[]{:S(2)}, u32[]{:S(2)}) collective-permute-start(bf16[128,2048]{1,0:T(8,128)(2,1)S(1)} %collective-permute-done.refs_0_), channel_id=1, source_target_pairs={{0,4},{1,5},{16,20},{17,21},{32,36},{33,37},{48,52},{49,53},{2,6},... | collective-permute-start | bytes 1572872 | tf_op jit(solution)/shard_map/ppermute | solution.py:35
  91.1 17.7 %collective-permute-start.20 = (bf16[512,512]{1,0:T(8,128)(2,1)S(1)}, bf16[512,512]{1,0:T(8,128)(2,1)S(1)}, u32[]{:S(2)}, u32[]{:S(2)}) collective-permute-start(bf16[512,512]{1,0:T(8,128)(2,1)S(1)} %score.3.own_ref), channel_id=1, source_target_pairs={{0,1},{1,0},{16,17},{17,16},{32,33},{33,32},{48,49},{49,48},{2,3},... | collective-permute-start | bytes 1572872 | tf_op jit(solution)/shard_map/ppermute | solution.py:35
  108.3 2.7 %collective-permute-start.16 = (bf16[512,512]{1,0:T(8,128)(2,1)S(1)}, bf16[512,512]{1,0:T(8,128)(2,1)S(1)}, u32[]{:S(2)}, u32[]{:S(2)}) collective-permute-start(bf16[512,512]{1,0:T(8,128)(2,1)S(1)} %score.2.own_ref), channel_id=1, source_target_pairs={{0,1},{1,0},{16,17},{17,16},{32,33},{33,32},{48,49},{49,48},{2,3},... | collective-permute-start | bytes 1572872 | tf_op jit(solution)/shard_map/ppermute | solution.py:35

commit v2 on v1

v2 whole, which is shorter than its diff:
```python
import functools

import jax
import jax.numpy as jnp
from jax import lax
from jax.experimental import pallas as pl
from jax.experimental.pallas import tpu as pltpu
from jax.sharding import PartitionSpec as P

AXES = ("train", "query", "layer")
NX, NY, NZL, NZH = 4, 4, 4, 2
NT = (((1,), (1,)), ((), ()))
MIB = 1 << 20
FREE = pl.CostEstimate(flops=0, bytes_accessed=0, transcendentals=0)


def device(x, y, z, core):
    return (((x % NX) * NZL + z % NZL) * (NY * NZH) + (y % NY) * NZH + (z // NZL) % NZH) * 2 + core


def pairs(move):
    out = []
    for x in range(NX):
        for y in range(NY):
            for z in range(NZL * NZH):
                for core in range(2):
                    out.append((device(x, y, z, core), device(*move(x, y, z, core))))
    return out


def send(value, name, dx=0, dy=0, dz=0, dzl=0, dcore=0, split=0):
    def move(x, y, z, core):
        low = z // NZL * NZL + (z % NZL + dzl) % NZL + (2 * core - 1) * split
        return x + dx, y + dy, (low + dz) % (NZL * NZH), core ^ dcore

    with jax.named_scope(name):
        return lax.ppermute(value, AXES, pairs(move))


LONG = pl.CostEstimate(flops=4000000000, bytes_accessed=0, transcendentals=0)


def pass_kernel(pos_ref, _, out_ref):
    for i in range(out_ref.shape[0]):
        out_ref[i] = pos_ref[i]


def pass_on(pos, held):
    return pl.pallas_call(
        pass_kernel,
        in_specs=[scalars(), anywhere()],
        out_specs=scalars(),
        out_shape=jax.ShapeDtypeStruct(pos.shape, pos.dtype),
        compiler_params=pltpu.CompilerParams(vmem_limit_bytes=MIB),
        cost_estimate=LONG,
        name="pass",
    )(pos, held)


def after(value, *others):
    return lax.optimization_barrier((value, *others))


def whole():
    return pl.BlockSpec(memory_space=pltpu.VMEM)


def anywhere():
    return pl.BlockSpec(memory_space=pl.ANY)


def scalars():
    return pl.BlockSpec(memory_space=pltpu.SMEM)


def move_all(moves, sems):
    copies = [pltpu.make_async_copy(source, target, sems.at[i]) for i, (source, target) in enumerate(moves)]
    for copy in copies:
        copy.start()
    for copy in copies:
        copy.wait()


def form_block(acts_ref, backs_ref, outs, prod_ref):
    count, layers, width, toks = acts_ref.shape
    scale = toks ** (-0.5)
    row = lax.broadcasted_iota(jnp.int32, (count, 128), 0) % 4
    lane = lax.broadcasted_iota(jnp.int32, (count, 128), 1) // width
    turn = (lane - row + 4) % 4
    for layer in range(layers):
        for part in range(count // 4):
            rows = pl.ds(part * 4, 4)
            left = backs_ref[rows, layer].reshape(4 * width, toks)
            right = acts_ref[rows, layer].reshape(4 * width, toks)
            prod_ref[layer, pl.ds(part * 128, 128), :] = lax.dot_general(
                left, right, NT, preferred_element_type=jnp.float32
            )
        for group in range(width // 4):
            held = [prod_ref[layer, pl.ds(group * 4 + s, count, stride=width), :] for s in range(4)]
            tile = None
            for r in range(4):
                value = held[r]
                for n in range(1, 4):
                    value = jnp.where(row == n, held[(n + r) % 4], value)
                if r > 0:
                    value = pltpu.roll(value, r * width, 1)
                tile = value if tile is None else jnp.where(turn == r, value, tile)
            at = layer * width * width + group * 128
            value = (tile * scale).astype(outs[0].dtype)
            for out_ref in outs:
                out_ref[:, pl.ds(at, 128)] = value


def form_kernel(block, acts_hbm, backs_hbm, *refs):
    outs, (acts_ref, backs_ref, prod_ref, sems) = refs[:-4], refs[-4:]
    steps = acts_hbm.shape[0] // block

    def fetch(i):
        rows = pl.ds(pl.multiple_of(i * block, block), block)
        return (
            pltpu.make_async_copy(acts_hbm.at[rows], acts_ref.at[rows], sems.at[0, i]),
            pltpu.make_async_copy(backs_hbm.at[rows], backs_ref.at[rows], sems.at[1, i]),
        )

    for i in range(steps):
        for copy in fetch(i):
            copy.start()

    for cut, half_ref in enumerate(outs[1:] or (None,)):
        first = cut * steps // max(len(outs) - 1, 1)

        def step(i, carry):
            rows = pl.ds(pl.multiple_of(i * block, block), block)
            here = pl.ds(pl.multiple_of((i - first) * block, block), block)
            for copy in fetch(i):
                copy.wait()
            targets = [outs[0].at[rows]] + ([] if half_ref is None else [half_ref.at[here]])
            form_block(acts_ref.at[rows], backs_ref.at[rows], targets, prod_ref)
            return carry

        lax.fori_loop(first, first + steps // max(len(outs) - 1, 1), step, 0)


def form_grads(acts, backs, cuts=0, block=16):
    count, layers, width, toks = acts.shape
    entries = layers * width * width
    shapes = [jax.ShapeDtypeStruct((rows, entries), jnp.bfloat16) for rows in [count] + [count // max(cuts, 1)] * cuts]
    return pl.pallas_call(
        functools.partial(form_kernel, block),
        in_specs=[anywhere()] * 2,
        out_specs=[whole() for _ in shapes],
        out_shape=shapes,
        scratch_shapes=[
            pltpu.VMEM(acts.shape, acts.dtype),
            pltpu.VMEM(backs.shape, backs.dtype),
            pltpu.VMEM((layers, block * width, 128), jnp.float32),
            pltpu.SemaphoreType.DMA((2, count // block)),
        ],
        compiler_params=pltpu.CompilerParams(vmem_limit_bytes=57 * MIB),
        cost_estimate=FREE,
        name="form",
    )(acts, backs)


def apply_kernel(pos_ref, *refs):
    grads, precs = refs[:NX], refs[NX : NX + NZL]
    out_ref, query_ref, rows_ref, sems = refs[NX + NZL :]
    x, zl = pos_ref[0], pos_ref[1]
    moves = []
    for s in range(NX):
        count = grads[s].shape[0]
        at = pl.multiple_of(lax.rem(x + s, NX) * count, count)
        moves.append((grads[s], query_ref.at[pl.ds(at, count)]))
    for s in range(NZL):
        count = precs[s].shape[1]
        at = pl.multiple_of(lax.rem(zl + s, NZL) * count, count)
        moves.append((precs[s], rows_ref.at[:, pl.ds(at, count)]))
    move_all(moves, sems)
    layers, rows, grad = rows_ref.shape
    for layer in range(layers):
        prod = lax.dot_general(
            query_ref[:, layer * grad : (layer + 1) * grad],
            rows_ref[layer],
            NT,
            preferred_element_type=jnp.float32,
        )
        out_ref[:, layer * rows : (layer + 1) * rows] = prod.astype(out_ref.dtype)


def apply_rows(pos, grads, precs):
    count, entries = grads[0].shape
    layers, rows, grad = precs[0].shape
    return pl.pallas_call(
        apply_kernel,
        in_specs=[scalars()] + [whole()] * (NX + NZL),
        out_specs=whole(),
        out_shape=jax.ShapeDtypeStruct((NX * count, layers * NZL * rows), jnp.bfloat16),
        scratch_shapes=[
            pltpu.VMEM((NX * count, entries), jnp.bfloat16),
            pltpu.VMEM((layers, NZL * rows, grad), jnp.bfloat16),
            pltpu.SemaphoreType.DMA((NX + NZL,)),
        ],
        compiler_params=pltpu.CompilerParams(vmem_limit_bytes=16 * MIB),
        cost_estimate=FREE,
        name="apply",
    )(pos, *grads, *precs)


def join_kernel(pos_ref, *refs):
    parts, (out_ref, sems) = refs[:NZL], refs[NZL:]
    zl = pos_ref[1]
    count = parts[0].shape[0] // NX
    moves = []
    for s in range(NZL):
        at = pl.multiple_of(lax.rem(zl + s, NZL) * count, count)
        for x in range(NX):
            moves.append((parts[s].at[pl.ds(x * count, count)], out_ref.at[x, pl.ds(at, count)]))
    move_all(moves, sems)


def join_queries(pos, parts):
    count, width = parts[0].shape
    out = pl.pallas_call(
        join_kernel,
        in_specs=[scalars()] + [whole()] * NZL,
        out_specs=whole(),
        out_shape=jax.ShapeDtypeStruct((NX, NZL * count // NX, width), jnp.bfloat16),
        scratch_shapes=[pltpu.SemaphoreType.DMA((NZL * NX,))],
        compiler_params=pltpu.CompilerParams(vmem_limit_bytes=16 * MIB),
        cost_estimate=FREE,
        name="join",
    )(pos, *parts)
    return out.reshape(NZL * count, width)


def dot_terms(scale, left_ref, right_ref, out_ref):
    prod = lax.dot_general(left_ref[...], right_ref[...], NT, preferred_element_type=jnp.float32)
    out_ref[...] = (prod * scale).astype(out_ref.dtype)


def place_trains(y, trains, left_ref):
    count = trains[0].shape[0]
    moves = []
    for s in range(NY):
        at = pl.multiple_of(lax.rem(y + s, NY) * count, count)
        moves.append((trains[s], left_ref.at[pl.ds(at, count)]))
    return moves


def near_kernel(scale, pos_ref, *refs):
    queries, trains = refs[:NX], refs[NX : NX + NY]
    out_ref, right_ref, left_ref, sems = refs[NX + NY :]
    x = pos_ref[0]
    layers = 2
    rows = queries[0].shape[1] // layers
    moves = place_trains(pos_ref[2], trains, left_ref)
    for s in range(NX):
        for layer in range(layers):
            at = pl.multiple_of(layer * NX * rows + lax.rem(x + s, NX) * rows, rows)
            moves.append((queries[s].at[:, pl.ds(layer * rows, rows)], right_ref.at[:, pl.ds(at, rows)]))
    move_all(moves, sems)
    dot_terms(scale, left_ref, right_ref, out_ref)


def score_near(pos, queries, trains, scale):
    count, entries = trains[0].shape
    total = NY * count
    columns = queries[0].shape[0]
    return pl.pallas_call(
        functools.partial(near_kernel, scale),
        in_specs=[scalars()] + [whole()] * (NX + NY),
        out_specs=[whole(), whole()],
        out_shape=[
            jax.ShapeDtypeStruct((total, columns), jnp.bfloat16),
            jax.ShapeDtypeStruct((columns, entries), jnp.bfloat16),
        ],
        scratch_shapes=[pltpu.VMEM((total, entries), jnp.bfloat16), pltpu.SemaphoreType.DMA((2 * NX + NY,))],
        compiler_params=pltpu.CompilerParams(vmem_limit_bytes=16 * MIB),
        cost_estimate=FREE,
        name="near",
    )(pos, *queries, *trains)


def far_kernel(scale, pos_ref, right_ref, *refs):
    firsts, seconds, (out_ref, left_ref, sems) = refs[:NY], refs[NY : 2 * NY], refs[2 * NY :]
    y = pos_ref[2]
    count = firsts[0].shape[0]
    moves = []
    for s in range(NY):
        at = lax.rem(y + s, NY) * 2 * count
        moves.append((firsts[s], left_ref.at[pl.ds(pl.multiple_of(at, count), count)]))
        moves.append((seconds[s], left_ref.at[pl.ds(pl.multiple_of(at + count, count), count)]))
    move_all(moves, sems)
    dot_terms(scale, left_ref, right_ref, out_ref)


def score_far(pos, packed, firsts, seconds, scale):
    count, entries = firsts[0].shape
    total = 2 * NY * count
    columns = packed.shape[0]
    return pl.pallas_call(
        functools.partial(far_kernel, scale),
        in_specs=[scalars()] + [whole()] * (1 + 2 * NY),
        out_specs=whole(),
        out_shape=jax.ShapeDtypeStruct((total, columns), jnp.bfloat16),
        scratch_shapes=[pltpu.VMEM((total, entries), jnp.bfloat16), pltpu.SemaphoreType.DMA((2 * NY,))],
        compiler_params=pltpu.CompilerParams(vmem_limit_bytes=16 * MIB),
        cost_estimate=FREE,
        name="far",
    )(pos, packed, *firsts, *seconds)


def add_kernel(places_ref, own_ref, other_ref, *refs):
    out_ref, sum_ref, sems = refs[-3:]
    count = own_ref.shape[0] // NY
    copies = []
    for s in range(NY):
        rows = pl.ds(s * count, count)
        sum_ref[rows, :] = own_ref[rows, :].astype(jnp.float32) + other_ref[rows, :].astype(jnp.float32)
        at = pl.multiple_of(places_ref[s] * count, count)
        copies.append(pltpu.make_async_copy(sum_ref.at[rows], out_ref.at[pl.ds(at, count)], sems.at[s]))
        copies[-1].start()
    for copy in copies:
        copy.wait()


def add_terms(places, own, other, total, held=None):
    columns = own.shape[1]
    extra = [] if held is None else [held]
    return pl.pallas_call(
        add_kernel,
        in_specs=[scalars(), whole(), whole()] + [anywhere()] * len(extra),
        out_specs=anywhere(),
        out_shape=jax.ShapeDtypeStruct((total, columns), jnp.float32),
        scratch_shapes=[pltpu.VMEM(own.shape, jnp.float32), pltpu.SemaphoreType.DMA((NY,))],
        input_output_aliases={} if held is None else {3: 0},
        compiler_params=pltpu.CompilerParams(vmem_limit_bytes=16 * MIB),
        cost_estimate=FREE,
        name="add",
    )(places, own, other, *extra)


def per_device(train_acts, train_backs, query_acts, query_backs, precond):
    t, k = lax.axis_index("train"), lax.axis_index("query")
    x, zl, y, zh = t // NZL, t % NZL, k // NZH, k % NZH
    pos = jnp.stack([x, zl, y, zh]).astype(jnp.int32)
    layers = train_acts.shape[1] * lax.axis_size("layer")
    scale = (layers * train_acts.shape[2] * train_backs.shape[2]) ** (-0.5)
    total = train_acts.shape[0] * lax.axis_size("query")
    precs = [precond, send(precond, "p_up", dz=-1), send(precond, "p_far", split=2), send(precond, "p_down", dz=1)]
    (query_grad,) = form_grads(query_acts[0], query_backs[0])
    grads = [query_grad, send(query_grad, "g_up", dx=-1), send(query_grad, "g_far", dx=2), send(query_grad, "g_down", dx=1)]
    train_acts, query_grad = after(train_acts, query_grad)
    train_grad, first, second = form_grads(train_acts, train_backs, 2)
    train_grad, first, second, *got = after(train_grad, first, second, *grads, *precs)
    near = [train_grad, send(train_grad, "n_up", dy=-1), None, send(train_grad, "n_down", dy=1)]
    part = apply_rows(pos, got[:NX], got[NX:])
    parts = [part] + [send(part, "low%d" % s, dzl=-s) for s in (1, 2, 3)]
    first, second, *parts = after(first, second, *parts)
    first = send(first, "far1", dz=NZL)
    second = send(second, "far2", dz=NZL)
    mine = join_queries(pos, parts)
    mine, again, near[1], near[3] = after(mine, train_grad, near[1], near[3])
    queries = [mine, send(mine, "r_up", dx=-1), None, send(mine, "r_down", dx=1)]
    near[2] = send(again, "n_two", dy=2)
    later = pass_on(pos, first)
    queries[1], queries[3], near[2], first, later = after(queries[1], queries[3], near[2], first, later)
    firsts = [first] + [send(first, "a%d" % s, dy=-s) for s in (1, 2, 3)]
    queries[2] = send(queries[1], "r_next", dx=-1)
    seconds = [second] + [send(second, "b%d" % s, dy=-s) for s in (1, 2, 3)]
    later, *firsts = after(later, *firsts)
    last = pass_on(later, second)
    queries[2], last = after(queries[2], last)
    near_terms, packed = score_near(last, queries, near, scale)
    near_other = send(near_terms, "swap_near", dcore=1)
    far_terms = score_far(pos, packed, firsts, seconds, scale)
    far_other = send(far_terms, "swap_far", dcore=1)
    ys = jnp.arange(NY, dtype=jnp.int32) * NZH
    out = add_terms((ys + zh).astype(jnp.int32), near_terms, near_other, total)
    return add_terms((ys + 1 - zh).astype(jnp.int32), far_terms, far_other, total, out)


def solution(mesh):
    in_specs = (
        P(("train", "query"), "layer", None, None),
        P(("train", "query"), "layer", None, None),
        P("query", "train", "layer", None, None),
        P("query", "train", "layer", None, None),
        P("layer", "train", None),
    )
    out_specs = P("train", "query")
    return jax.shard_map(
        per_device, mesh=mesh, in_specs=in_specs, out_specs=out_specs, check_vma=False
    )
```

time: 113 us -> 98.4 us (0.87)
  waiting for transfers between devices: 50.1 us -> 36.5 us
  local copies, waits for them, and re-layouts: 7.77 us -> 0.02 us
  Pallas kernels: 19.5 us -> 23.2 us
  starting transfers between devices: 35.6 us -> 37.6 us
    ppermute x21 -> x25, waiting for transfers between devices: 50.1 us -> 36.5 us  [send(): return lax.ppermute(value, AXES, pairs(move))]
    unnamed x10 -> x8, local copies, waits for them, and re-layouts: 7.77 us -> 0.02 us
    pallas_call x8 -> x10, Pallas kernels: 19.5 us -> 23.2 us  [the longest x2 10 us: form_grads(): pl.pallas_call(functools.partial(form_kernel, block), in_specs=[anywhere(...]
    ppermute x21 -> x25, starting transfers between devices: 35.6 us -> 37.6 us  [send(): return lax.ppermute(value, AXES, pairs(move))]
  transfers between devices with their start and end apart: 21 -> 25, of which waited for: 8 -> 12; matrix products, arithmetic and copies ran while one was open for 0% -> 0% of each run, Pallas kernels for 13% -> 19%
where the time goes in v2:
time: 98.4 us; the launch traced here: 97.8 us
  starting transfers between devices  37.6 us (38%)
  waiting for transfers between devices  36.5 us (37%)
  Pallas kernels  23.2 us (24%)
    ppermute x25, starting transfers between devices, send(): return lax.ppermute(value, AXES, pairs(move))  37.6 us
    ppermute x25, waiting for transfers between devices, send(): return lax.ppermute(value, AXES, pairs(move))  36.5 us
    pallas_call x2, Pallas kernels, form_grads(): pl.pallas_call(functools.partial(form_kernel, block), in_specs=[anywhere(...  10 us
    pallas_call x2, Pallas kernels, add_terms(): pl.pallas_call(add_kernel, in_specs=[scalars(), whole(), whole()] + [anyw...  3.13 us
    pallas_call x1, Pallas kernels, score_near(): pl.pallas_call(functools.partial(near_kernel, scale), in_specs=[scalars()...  2.43 us
    pallas_call x2, Pallas kernels, pass_on(): pl.pallas_call(pass_kernel, in_specs=[scalars(), anywhere()], out_specs=s...  2.27 us
    pallas_call x1, Pallas kernels, score_far(): pl.pallas_call(functools.partial(far_kernel, scale), in_specs=[scalars()]...  2.08 us
  transfers between devices with their start and end apart: 25, of which 12 were waited for; matrix products, arithmetic and copies ran while one was open for 0% of the time, Pallas kernels for 19%

profile of v2, /device:TPU:1, one launch (start us, length us, event | category | flops | bytes accessed | tf_op | source)
XLA Modules:
  0.0 97.8 jit_solution(2015414564928126649)
XLA Ops:
  0.0 3.1 %form.2.refs_0_ = bf16[32,2048]{1,0:T(8,128)(2,1)} custom-call(bf16[32,2,32,256]{3,2,1,0:T(8,128)(2,1)} %bitcast.10, bf16[32,2,32,256]{3,2,1,0:T(8,128)(2,1)} %bitcast.11), custom_call_target="tpu_custom_call" | custom-call | tf_op jit(solution)/shard_map/form/pallas_call | solution.py:148
  3.1 0.0 copy-start.1
  3.1 3.4 %collective-permute-start = (bf16[32,2048]{1,0:T(8,128)(2,1)}, bf16[32,2048]{1,0:T(8,128)(2,1)S(1)}, u32[]{:S(2)}, u32[]{:S(2)}) collective-permute-start(bf16[32,2048]{1,0:T(8,128)(2,1)} %form.2.refs_0_), channel_id=1, source_target_pairs={{0,192},{1,193},{16,208},{17,209},{32,224},{33,225},{48,240},{49,2... | collective-permute-start | bytes 393224 | tf_op jit(solution)/shard_map/g_up/ppermute | solution.py:37
  6.5 0.0 copy-done.2
  6.5 5.6 %collective-permute-start.3 = (bf16[2,64,1024]{2,1,0:T(8,128)(2,1)S(1)}, bf16[2,64,1024]{2,1,0:T(8,128)(2,1)S(1)}, u32[]{:S(2)}, u32[]{:S(2)}) collective-permute-start(bf16[2,64,1024]{2,1,0:T(8,128)(2,1)S(1)} %copy-done.2), channel_id=1, source_target_pairs={{0,50},{1,51},{16,0},{17,1},{32,16},{33,17},{48,32},{49,33},{2,48}... | collective-permute-start | bytes 786440 | tf_op jit(solution)/shard_map/p_up/ppermute | solution.py:37
  12.1 0.0 collective-permute-start.4
  12.1 0.0 collective-permute-start.5
  12.1 0.5 collective-permute-start.1
  12.6 0.0 collective-permute-done.refs_1_
  12.6 0.6 collective-permute-start.2
  13.2 6.9 %form.3 = (bf16[128,2048]{1,0:T(8,128)(2,1)}, bf16[64,2048]{1,0:T(8,128)(2,1)}, bf16[64,2048]{1,0:T(8,128)(2,1)}) custom-call(bf16[128,2,32,256]{3,2,1,0:T(8,128)(2,1)} %acts_hbm, bf16[128,2,32,256]{3,2,1,0:T(8,128)(2,1)} %backs_hbm.1), custom_call_target="tpu_custom_call" | custom-call | tf_op jit(solution)/shard_map/form/pallas_call | solution.py:148
  20.1 0.0 copy-start
  20.2 0.0 collective-permute-done.1.refs_2_
  20.2 0.0 collective-permute-done.2.refs_3_
  20.2 0.0 collective-permute-done.3.refs_5_
  20.2 2.5 %collective-permute-done.4.refs_6_ = bf16[2,64,1024]{2,1,0:T(8,128)(2,1)S(1)} collective-permute-done((bf16[2,64,1024]{2,1,0:T(8,128)(2,1)S(1)}, bf16[2,64,1024]{2,1,0:T(8,128)(2,1)S(1)}, u32[]{:S(2)}, u32[]{:S(2)}) %collective-permute-start.4) | collective-permute-done | bytes 262176 | tf_op jit(solution)/shard_map/p_far/ppermute | solution.py:37
  22.7 1.9 %collective-permute-done.5.refs_7_ = bf16[2,64,1024]{2,1,0:T(8,128)(2,1)S(1)} collective-permute-done((bf16[2,64,1024]{2,1,0:T(8,128)(2,1)S(1)}, bf16[2,64,1024]{2,1,0:T(8,128)(2,1)S(1)}, u32[]{:S(2)}, u32[]{:S(2)}) %collective-permute-start.5) | collective-permute-done | bytes 262176 | tf_op jit(solution)/shard_map/p_down/ppermute | solution.py:37
  24.6 1.3 %collective-permute-start.10 = (bf16[128,2048]{1,0:T(8,128)(2,1)}, bf16[128,2048]{1,0:T(8,128)(2,1)S(1)}, u32[]{:S(2)}, u32[]{:S(2)}) collective-permute-start(bf16[128,2048]{1,0:T(8,128)(2,1)} %get-tuple-element.64.refs_4_), channel_id=1, source_target_pairs={{0,4},{1,5},{16,20},{17,21},{32,36},{33,37},{48,52},{49,53},{2,6},... | collective-permute-start | bytes 1572872 | tf_op jit(solution)/shard_map/n_down/ppermute | solution.py:37
  25.9 1.4 %collective-permute-start.9 = (bf16[128,2048]{1,0:T(8,128)(2,1)}, bf16[128,2048]{1,0:T(8,128)(2,1)S(1)}, u32[]{:S(2)}, u32[]{:S(2)}) collective-permute-start(bf16[128,2048]{1,0:T(8,128)(2,1)} %get-tuple-element.64.refs_4_), channel_id=1, source_target_pairs={{0,12},{1,13},{16,28},{17,29},{32,44},{33,45},{48,60},{49,61},{2,1... | collective-permute-start | bytes 1572872 | tf_op jit(solution)/shard_map/n_up/ppermute | solution.py:37
  27.3 0.1 pad_add_fusion.pos_ref
  27.4 1.9 %apply.1.refs_0_ = bf16[128,512]{1,0:T(8,128)(2,1)S(1)} custom-call(s32[4]{0:T(128)S(1)} %pad_add_fusion.pos_ref, bf16[32,2048]{1,0:T(8,128)(2,1)S(1)} %copy-done.1, bf16[32,2048]{1,0:T(8,128)(2,1)S(1)} %collective-permute-done.refs_1_, bf16[32,2048]{1,0:T(8,128)(2,1)S(1)} %collective-permute-done.1.refs_2_, ...), custom_call_target="tpu_custom_call" | custom-call | tf_op jit(solution)/shard_map/apply/pallas_call | solution.py:193
  29.3 2.1 %collective-permute-start.6 = (bf16[128,512]{1,0:T(8,128)(2,1)S(1)}, bf16[128,512]{1,0:T(8,128)(2,1)S(1)}, u32[]{:S(2)}, u32[]{:S(2)}) collective-permute-start(bf16[128,512]{1,0:T(8,128)(2,1)S(1)} %apply.1.refs_0_), channel_id=1, source_target_pairs={{0,48},{1,49},{16,0},{17,1},{32,16},{33,17},{48,32},{49,33},{2,50}... | collective-permute-start | bytes 393224 | tf_op jit(solution)/shard_map/low1/ppermute | solution.py:37
  31.4 0.3 collective-permute-start.7
  31.7 0.1 collective-permute-start.8
  31.8 2.7 %collective-permute-done.6.refs_1_ = bf16[128,512]{1,0:T(8,128)(2,1)S(1)} collective-permute-done((bf16[128,512]{1,0:T(8,128)(2,1)S(1)}, bf16[128,512]{1,0:T(8,128)(2,1)S(1)}, u32[]{:S(2)}, u32[]{:S(2)}) %collective-permute-start.6) | collective-permute-done | bytes 131104 | tf_op jit(solution)/shard_map/low1/ppermute | solution.py:37
  34.4 9.3 %collective-permute-done.7.refs_2_ = bf16[128,512]{1,0:T(8,128)(2,1)S(1)} collective-permute-done((bf16[128,512]{1,0:T(8,128)(2,1)S(1)}, bf16[128,512]{1,0:T(8,128)(2,1)S(1)}, u32[]{:S(2)}, u32[]{:S(2)}) %collective-permute-start.7) | collective-permute-done | bytes 131104 | tf_op jit(solution)/shard_map/low2/ppermute | solution.py:37
  43.7 0.0 collective-permute-done.8.refs_3_
  43.7 3.6 %collective-permute-start.14 = (bf16[64,2048]{1,0:T(8,128)(2,1)}, bf16[64,2048]{1,0:T(8,128)(2,1)S(1)}, u32[]{:S(2)}, u32[]{:S(2)}) collective-permute-start(bf16[64,2048]{1,0:T(8,128)(2,1)} %get-tuple-element.65), channel_id=1, source_target_pairs={{0,2},{1,3},{16,18},{17,19},{32,34},{33,35},{48,50},{49,51},{2,0},... | collective-permute-start | bytes 786440 | tf_op jit(solution)/shard_map/far1/ppermute | solution.py:37
  47.3 1.4 %join.1 = bf16[4,128,512]{2,1,0:T(8,128)(2,1)S(1)} custom-call(s32[4]{0:T(128)S(1)} %pad_add_fusion.pos_ref, bf16[128,512]{1,0:T(8,128)(2,1)S(1)} %apply.1.refs_0_, bf16[128,512]{1,0:T(8,128)(2,1)S(1)} %collective-permute-done.6.refs_1_, bf16[128,512]{1,0:T(8,128)(2,1)S(1)} %collective-permute-done.7.refs_2_, bf16[128,512]{1,0:T(8,128)(2,1)S(1)} %collective-permute-done.8.refs_3_), custom_call_target="tpu_custom_call" | custom-call | tf_op jit(solution)/shard_map/join/pallas_call | solution.py:223
  48.7 0.0 collective-permute-done.10.refs_7_
  48.7 0.0 collective-permute-done.9.refs_5_
  48.7 0.1 collective-permute-start.11
  48.8 1.5 %collective-permute-start.12 = (bf16[512,512]{1,0:T(8,128)(2,1)S(1)}, bf16[512,512]{1,0:T(8,128)(2,1)S(1)}, u32[]{:S(2)}, u32[]{:S(2)}) collective-permute-start(bf16[512,512]{1,0:T(8,128)(2,1)S(1)} %bitcast.8), channel_id=1, source_target_pairs={{0,64},{1,65},{16,80},{17,81},{32,96},{33,97},{48,112},{49,113},{2... | collective-permute-start | bytes 1572872 | tf_op jit(solution)/shard_map/r_down/ppermute | solution.py:37
  50.3 1.6 %collective-permute-start.13 = (bf16[128,2048]{1,0:T(8,128)(2,1)S(1)}, bf16[128,2048]{1,0:T(8,128)(2,1)S(1)}, u32[]{:S(2)}, u32[]{:S(2)}) collective-permute-start(bf16[128,2048]{1,0:T(8,128)(2,1)S(1)} %copy-done), channel_id=1, source_target_pairs={{0,8},{1,9},{16,24},{17,25},{32,40},{33,41},{48,56},{49,57},{2,10}... | collective-permute-start | bytes 1572872 | tf_op jit(solution)/shard_map/n_two/ppermute | solution.py:37
  51.9 1.7 %collective-permute-start.19 = (bf16[64,2048]{1,0:T(8,128)(2,1)S(1)}, bf16[64,2048]{1,0:T(8,128)(2,1)S(1)}, u32[]{:S(2)}, u32[]{:S(2)}) collective-permute-start(bf16[64,2048]{1,0:T(8,128)(2,1)S(1)} %copy-done.3), channel_id=1, source_target_pairs={{0,2},{1,3},{16,18},{17,19},{32,34},{33,35},{48,50},{49,51},{2,0},... | collective-permute-start | bytes 786440 | tf_op jit(solution)/shard_map/far2/ppermute | solution.py:37
  53.6 3.2 %collective-permute-done.14._.refs_0_ = bf16[64,2048]{1,0:T(8,128)(2,1)S(1)} collective-permute-done((bf16[64,2048]{1,0:T(8,128)(2,1)}, bf16[64,2048]{1,0:T(8,128)(2,1)S(1)}, u32[]{:S(2)}, u32[]{:S(2)}) %collective-permute-start.14) | collective-permute-done | bytes 262176 | tf_op jit(solution)/shard_map/far1/ppermute | solution.py:37
  56.8 1.1 %pass.2.pos_ref = s32[4]{0:T(128)S(1)} custom-call(s32[4]{0:T(128)S(1)} %pad_add_fusion.pos_ref, bf16[64,2048]{1,0:T(8,128)(2,1)S(1)} %collective-permute-done.14._.refs_0_), custom_call_target="tpu_custom_call" | custom-call | flops 4000000000 | tf_op jit(solution)/shard_map/pass/pallas_call | solution.py:49
  57.9 3.4 %collective-permute-done.11.refs_1_ = bf16[512,512]{1,0:T(8,128)(2,1)S(1)} collective-permute-done((bf16[512,512]{1,0:T(8,128)(2,1)S(1)}, bf16[512,512]{1,0:T(8,128)(2,1)S(1)}, u32[]{:S(2)}, u32[]{:S(2)}) %collective-permute-start.11) | collective-permute-done | bytes 524320 | tf_op jit(solution)/shard_map/r_up/ppermute | solution.py:37
  61.4 0.9 collective-permute-done.12.refs_3_
  62.3 1.5 %collective-permute-done.13.refs_6_ = bf16[128,2048]{1,0:T(8,128)(2,1)S(1)} collective-permute-done((bf16[128,2048]{1,0:T(8,128)(2,1)S(1)}, bf16[128,2048]{1,0:T(8,128)(2,1)S(1)}, u32[]{:S(2)}, u32[]{:S(2)}) %collective-permute-start.13) | collective-permute-done | bytes 524320 | tf_op jit(solution)/shard_map/n_two/ppermute | solution.py:37
  63.8 1.4 %collective-permute-start.16 = (bf16[64,2048]{1,0:T(8,128)(2,1)S(1)}, bf16[64,2048]{1,0:T(8,128)(2,1)S(1)}, u32[]{:S(2)}, u32[]{:S(2)}) collective-permute-start(bf16[64,2048]{1,0:T(8,128)(2,1)S(1)} %collective-permute-done.14._.refs_0_), channel_id=1, source_target_pairs={{0,12},{1,13},{16,28},{17,29},{32,44},{33,45},{48,60},{49,61},{2,1... | collective-permute-start | bytes 786440 | tf_op jit(solution)/shard_map/a1/ppermute | solution.py:37
  65.2 0.4 collective-permute-start.17
  65.5 0.7 collective-permute-start.18
  66.2 1.2 %collective-permute-start.15 = (bf16[512,512]{1,0:T(8,128)(2,1)S(1)}, bf16[512,512]{1,0:T(8,128)(2,1)S(1)}, u32[]{:S(2)}, u32[]{:S(2)}) collective-permute-start(bf16[512,512]{1,0:T(8,128)(2,1)S(1)} %collective-permute-done.11.refs_1_), channel_id=1, source_target_pairs={{0,192},{1,193},{16,208},{17,209},{32,224},{33,225},{48,240},{49,2... | collective-permute-start | bytes 1572872 | tf_op jit(solution)/shard_map/r_next/ppermute | solution.py:37
  67.4 0.3 collective-permute-done.19._.refs_4_
  67.7 1.7 %collective-permute-start.20 = (bf16[64,2048]{1,0:T(8,128)(2,1)S(1)}, bf16[64,2048]{1,0:T(8,128)(2,1)S(1)}, u32[]{:S(2)}, u32[]{:S(2)}) collective-permute-start(bf16[64,2048]{1,0:T(8,128)(2,1)S(1)} %collective-permute-done.19._.refs_4_), channel_id=1, source_target_pairs={{0,12},{1,13},{16,28},{17,29},{32,44},{33,45},{48,60},{49,61},{2,1... | collective-permute-start | bytes 786440 | tf_op jit(solution)/shard_map/b1/ppermute | solution.py:37
  69.4 0.0 collective-permute-done.16.refs_1_
  69.4 1.4 %collective-permute-start.21 = (bf16[64,2048]{1,0:T(8,128)(2,1)S(1)}, bf16[64,2048]{1,0:T(8,128)(2,1)S(1)}, u32[]{:S(2)}, u32[]{:S(2)}) collective-permute-start(bf16[64,2048]{1,0:T(8,128)(2,1)S(1)} %collective-permute-done.19._.refs_4_), channel_id=1, source_target_pairs={{0,8},{1,9},{16,24},{17,25},{32,40},{33,41},{48,56},{49,57},{2,10}... | collective-permute-start | bytes 786440 | tf_op jit(solution)/shard_map/b2/ppermute | solution.py:37
  70.8 1.2 %collective-permute-done.17.refs_2_ = bf16[64,2048]{1,0:T(8,128)(2,1)S(1)} collective-permute-done((bf16[64,2048]{1,0:T(8,128)(2,1)S(1)}, bf16[64,2048]{1,0:T(8,128)(2,1)S(1)}, u32[]{:S(2)}, u32[]{:S(2)}) %collective-permute-start.17) | collective-permute-done | bytes 262176 | tf_op jit(solution)/shard_map/a2/ppermute | solution.py:37
  72.0 3.5 %collective-permute-start.22 = (bf16[64,2048]{1,0:T(8,128)(2,1)S(1)}, bf16[64,2048]{1,0:T(8,128)(2,1)S(1)}, u32[]{:S(2)}, u32[]{:S(2)}) collective-permute-start(bf16[64,2048]{1,0:T(8,128)(2,1)S(1)} %collective-permute-done.19._.refs_4_), channel_id=1, source_target_pairs={{0,4},{1,5},{16,20},{17,21},{32,36},{33,37},{48,52},{49,53},{2,6},... | collective-permute-start | bytes 786440 | tf_op jit(solution)/shard_map/b3/ppermute | solution.py:37
  75.5 7.1 %collective-permute-done.18.refs_3_ = bf16[64,2048]{1,0:T(8,128)(2,1)S(1)} collective-permute-done((bf16[64,2048]{1,0:T(8,128)(2,1)S(1)}, bf16[64,2048]{1,0:T(8,128)(2,1)S(1)}, u32[]{:S(2)}, u32[]{:S(2)}) %collective-permute-start.18) | collective-permute-done | bytes 262176 | tf_op jit(solution)/shard_map/a3/ppermute | solution.py:37
  82.6 1.1 %pass.3.pos_ref = s32[4]{0:T(128)S(1)} custom-call(s32[4]{0:T(128)S(1)} %pass.2.pos_ref, bf16[64,2048]{1,0:T(8,128)(2,1)S(1)} %collective-permute-done.19._.refs_4_), custom_call_target="tpu_custom_call" | custom-call | flops 4000000000 | tf_op jit(solution)/shard_map/pass/pallas_call | solution.py:49
  83.7 0.0 collective-permute-done.15.refs_2_
  83.7 2.4 %near.1 = (bf16[512,512]{1,0:T(8,128)(2,1)S(1)}, bf16[512,2048]{1,0:T(8,128)(2,1)S(1)}) custom-call(s32[4]{0:T(128)S(1)} %pass.3.pos_ref, bf16[512,512]{1,0:T(8,128)(2,1)S(1)} %bitcast.9, bf16[512,512]{1,0:T(8,128)(2,1)S(1)} %collective-permute-done.11.refs_1_, bf16[512,512]{1,0:T(8,128)(2,1)S(1)} %collective-permute-done.15.refs_2_, ...), custom_call_target="tpu_custom_call" | custom-call | tf_op jit(solution)/shard_map/near/pallas_call | solution.py:269
  86.2 2.1 %collective-permute-start.24 = (bf16[512,512]{1,0:T(8,128)(2,1)S(1)}, bf16[512,512]{1,0:T(8,128)(2,1)S(1)}, u32[]{:S(2)}, u32[]{:S(2)}) collective-permute-start(bf16[512,512]{1,0:T(8,128)(2,1)S(1)} %get-tuple-element.82.own_ref), channel_id=1, source_target_pairs={{0,1},{1,0},{16,17},{17,16},{32,33},{33,32},{48,49},{49,48},{2,3},... | collective-permute-start | bytes 1572872 | tf_op jit(solution)/shard_map/swap_near/ppermute | solution.py:37
  88.3 0.0 collective-permute-done.20.refs_5_
  88.3 0.0 collective-permute-done.21.refs_6_
  88.3 2.7 %collective-permute-done.22.refs_7_ = bf16[64,2048]{1,0:T(8,128)(2,1)S(1)} collective-permute-done((bf16[64,2048]{1,0:T(8,128)(2,1)S(1)}, bf16[64,2048]{1,0:T(8,128)(2,1)S(1)}, u32[]{:S(2)}, u32[]{:S(2)}) %collective-permute-start.22) | collective-permute-done | bytes 262176 | tf_op jit(solution)/shard_map/b3/ppermute | solution.py:37
  90.9 2.1 %far.1.own_ref = bf16[512,512]{1,0:T(8,128)(2,1)S(1)} custom-call(s32[4]{0:T(128)S(1)} %pad_add_fusion.pos_ref, bf16[512,2048]{1,0:T(8,128)(2,1)S(1)} %get-tuple-element.77.right_ref, bf16[64,2048]{1,0:T(8,128)(2,1)S(1)} %collective-permute-done.14._.refs_0_, bf16[64,2048]{1,0:T(8,128)(2,1)S(1)} %collective-permute-done.16.refs_1_, ...), custom_call_target="tpu_custom_call" | custom-call | tf_op jit(solution)/shard_map/far/pallas_call | solution.py:301
  93.0 1.4 %collective-permute-start.23 = (bf16[512,512]{1,0:T(8,128)(2,1)S(1)}, bf16[512,512]{1,0:T(8,128)(2,1)S(1)}, u32[]{:S(2)}, u32[]{:S(2)}) collective-permute-start(bf16[512,512]{1,0:T(8,128)(2,1)S(1)} %far.1.own_ref), channel_id=1, source_target_pairs={{0,1},{1,0},{16,17},{17,16},{32,33},{33,32},{48,49},{49,48},{2,3},... | collective-permute-start | bytes 1572872 | tf_op jit(solution)/shard_map/swap_far/ppermute | solution.py:37
  94.4 0.0 collective-permute-done.24.other_ref
  94.4 1.6 %add.30.refs_0_ = f32[1024,512]{1,0:T(8,128)} custom-call(s32[4]{0:T(128)S(1)} %get-tuple-element.84.places_ref, bf16[512,512]{1,0:T(8,128)(2,1)S(1)} %get-tuple-element.82.own_ref, bf16[512,512]{1,0:T(8,128)(2,1)S(1)} %collective-permute-done.24.other_ref), custom_call_target="tpu_custom_call" | custom-call | tf_op jit(solution)/shard_map/add/pallas_call | solution.py:330
  96.0 0.0 collective-permute-done.23.other_ref
  96.0 1.6 %add.31 = f32[1024,512]{1,0:T(8,128)} custom-call(s32[4]{0:T(128)S(1)} %get-tuple-element.83.places_ref, bf16[512,512]{1,0:T(8,128)(2,1)S(1)} %far.1.own_ref, bf16[512,512]{1,0:T(8,128)(2,1)S(1)} %collective-permute-done.23.other_ref, f32[1024,512]{1,0:T(8,128)} %add.30.refs_0_), custom_call_target="tpu_custom_call", output_to_operand_aliasing={{}: (3, {})} | custom-call | tf_op jit(solution)/shard_map/add/pallas_call | solution.py:330
  (6 shorter events, 0.0 us)
Async XLA Ops:
  0.0 6.5 %copy-start.2 = (bf16[2,64,1024]{2,1,0:T(8,128)(2,1)S(1)}, bf16[2,64,1024]{2,1,0:T(8,128)(2,1)}, u32[]{:S(2)}) copy-start(bf16[2,64,1024]{2,1,0:T(8,128)(2,1)} %refs_4_) | copy-start | bytes 786436
  3.1 24.3 %copy-start.1 = (bf16[32,2048]{1,0:T(8,128)(2,1)S(1)}, bf16[32,2048]{1,0:T(8,128)(2,1)}, u32[]{:S(2)}) copy-start(bf16[32,2048]{1,0:T(8,128)(2,1)} %form.2.refs_0_) | copy-start | bytes 393220
  3.1 9.5 %collective-permute-start = (bf16[32,2048]{1,0:T(8,128)(2,1)}, bf16[32,2048]{1,0:T(8,128)(2,1)S(1)}, u32[]{:S(2)}, u32[]{:S(2)}) collective-permute-start(bf16[32,2048]{1,0:T(8,128)(2,1)} %form.2.refs_0_), channel_id=1, source_target_pairs={{0,192},{1,193},{16,208},{17,209},{32,224},{33,225},{48,240},{49,2... | collective-permute-start | bytes 393224 | tf_op jit(solution)/shard_map/g_up/ppermute | solution.py:37
  6.5 13.7 %collective-permute-start.3 = (bf16[2,64,1024]{2,1,0:T(8,128)(2,1)S(1)}, bf16[2,64,1024]{2,1,0:T(8,128)(2,1)S(1)}, u32[]{:S(2)}, u32[]{:S(2)}) collective-permute-start(bf16[2,64,1024]{2,1,0:T(8,128)(2,1)S(1)} %copy-done.2), channel_id=1, source_target_pairs={{0,50},{1,51},{16,0},{17,1},{32,16},{33,17},{48,32},{49,33},{2,48}... | collective-permute-start | bytes 786440 | tf_op jit(solution)/shard_map/p_up/ppermute | solution.py:37
  12.1 10.6 %collective-permute-start.4 = (bf16[2,64,1024]{2,1,0:T(8,128)(2,1)S(1)}, bf16[2,64,1024]{2,1,0:T(8,128)(2,1)S(1)}, u32[]{:S(2)}, u32[]{:S(2)}) collective-permute-start(bf16[2,64,1024]{2,1,0:T(8,128)(2,1)S(1)} %copy-done.2), channel_id=1, source_target_pairs={{0,34},{1,33},{16,50},{17,49},{32,0},{33,3},{48,16},{49,19},{2,32}... | collective-permute-start | bytes 786440 | tf_op jit(solution)/shard_map/p_far/ppermute | solution.py:37
  12.1 12.5 %collective-permute-start.5 = (bf16[2,64,1024]{2,1,0:T(8,128)(2,1)S(1)}, bf16[2,64,1024]{2,1,0:T(8,128)(2,1)S(1)}, u32[]{:S(2)}, u32[]{:S(2)}) collective-permute-start(bf16[2,64,1024]{2,1,0:T(8,128)(2,1)S(1)} %copy-done.2), channel_id=1, source_target_pairs={{0,16},{1,17},{16,32},{17,33},{32,48},{33,49},{48,2},{49,3},{2,18}... | collective-permute-start | bytes 786440 | tf_op jit(solution)/shard_map/p_down/ppermute | solution.py:37
  12.1 8.1 %collective-permute-start.1 = (bf16[32,2048]{1,0:T(8,128)(2,1)}, bf16[32,2048]{1,0:T(8,128)(2,1)S(1)}, u32[]{:S(2)}, u32[]{:S(2)}) collective-permute-start(bf16[32,2048]{1,0:T(8,128)(2,1)} %form.2.refs_0_), channel_id=1, source_target_pairs={{0,128},{1,129},{16,144},{17,145},{32,160},{33,161},{48,176},{49,1... | collective-permute-start | bytes 393224 | tf_op jit(solution)/shard_map/g_far/ppermute | solution.py:37
  12.6 7.6 %collective-permute-start.2 = (bf16[32,2048]{1,0:T(8,128)(2,1)}, bf16[32,2048]{1,0:T(8,128)(2,1)S(1)}, u32[]{:S(2)}, u32[]{:S(2)}) collective-permute-start(bf16[32,2048]{1,0:T(8,128)(2,1)} %form.2.refs_0_), channel_id=1, source_target_pairs={{0,64},{1,65},{16,80},{17,81},{32,96},{33,97},{48,112},{49,113},{2... | collective-permute-start | bytes 393224 | tf_op jit(solution)/shard_map/g_down/ppermute | solution.py:37
  20.1 30.1 %copy-start = (bf16[128,2048]{1,0:T(8,128)(2,1)S(1)}, bf16[128,2048]{1,0:T(8,128)(2,1)}, u32[]{:S(2)}) copy-start(bf16[128,2048]{1,0:T(8,128)(2,1)} %get-tuple-element.64.refs_4_) | copy-start | bytes 1572868
  20.1 31.7 %copy-start.3 = (bf16[64,2048]{1,0:T(8,128)(2,1)S(1)}, bf16[64,2048]{1,0:T(8,128)(2,1)}, u32[]{:S(2)}) copy-start(bf16[64,2048]{1,0:T(8,128)(2,1)} %get-tuple-element.70) | copy-start | bytes 786436
  24.6 24.1 %collective-permute-start.10 = (bf16[128,2048]{1,0:T(8,128)(2,1)}, bf16[128,2048]{1,0:T(8,128)(2,1)S(1)}, u32[]{:S(2)}, u32[]{:S(2)}) collective-permute-start(bf16[128,2048]{1,0:T(8,128)(2,1)} %get-tuple-element.64.refs_4_), channel_id=1, source_target_pairs={{0,4},{1,5},{16,20},{17,21},{32,36},{33,37},{48,52},{49,53},{2,6},... | collective-permute-start | bytes 1572872 | tf_op jit(solution)/shard_map/n_down/ppermute | solution.py:37
  25.9 22.8 %collective-permute-start.9 = (bf16[128,2048]{1,0:T(8,128)(2,1)}, bf16[128,2048]{1,0:T(8,128)(2,1)S(1)}, u32[]{:S(2)}, u32[]{:S(2)}) collective-permute-start(bf16[128,2048]{1,0:T(8,128)(2,1)} %get-tuple-element.64.refs_4_), channel_id=1, source_target_pairs={{0,12},{1,13},{16,28},{17,29},{32,44},{33,45},{48,60},{49,61},{2,1... | collective-permute-start | bytes 1572872 | tf_op jit(solution)/shard_map/n_up/ppermute | solution.py:37
  29.3 5.1 %collective-permute-start.6 = (bf16[128,512]{1,0:T(8,128)(2,1)S(1)}, bf16[128,512]{1,0:T(8,128)(2,1)S(1)}, u32[]{:S(2)}, u32[]{:S(2)}) collective-permute-start(bf16[128,512]{1,0:T(8,128)(2,1)S(1)} %apply.1.refs_0_), channel_id=1, source_target_pairs={{0,48},{1,49},{16,0},{17,1},{32,16},{33,17},{48,32},{49,33},{2,50}... | collective-permute-start | bytes 393224 | tf_op jit(solution)/shard_map/low1/ppermute | solution.py:37
  31.4 12.3 %collective-permute-start.7 = (bf16[128,512]{1,0:T(8,128)(2,1)S(1)}, bf16[128,512]{1,0:T(8,128)(2,1)S(1)}, u32[]{:S(2)}, u32[]{:S(2)}) collective-permute-start(bf16[128,512]{1,0:T(8,128)(2,1)S(1)} %apply.1.refs_0_), channel_id=1, source_target_pairs={{0,32},{1,33},{16,48},{17,49},{32,0},{33,1},{48,16},{49,17},{2,34}... | collective-permute-start | bytes 393224 | tf_op jit(solution)/shard_map/low2/ppermute | solution.py:37
  31.7 12.0 %collective-permute-start.8 = (bf16[128,512]{1,0:T(8,128)(2,1)S(1)}, bf16[128,512]{1,0:T(8,128)(2,1)S(1)}, u32[]{:S(2)}, u32[]{:S(2)}) collective-permute-start(bf16[128,512]{1,0:T(8,128)(2,1)S(1)} %apply.1.refs_0_), channel_id=1, source_target_pairs={{0,16},{1,17},{16,32},{17,33},{32,48},{33,49},{48,0},{49,1},{2,18}... | collective-permute-start | bytes 393224 | tf_op jit(solution)/shard_map/low3/ppermute | solution.py:37
  43.7 13.0 %collective-permute-start.14 = (bf16[64,2048]{1,0:T(8,128)(2,1)}, bf16[64,2048]{1,0:T(8,128)(2,1)S(1)}, u32[]{:S(2)}, u32[]{:S(2)}) collective-permute-start(bf16[64,2048]{1,0:T(8,128)(2,1)} %get-tuple-element.65), channel_id=1, source_target_pairs={{0,2},{1,3},{16,18},{17,19},{32,34},{33,35},{48,50},{49,51},{2,0},... | collective-permute-start | bytes 786440 | tf_op jit(solution)/shard_map/far1/ppermute | solution.py:37
  48.7 12.7 %collective-permute-start.11 = (bf16[512,512]{1,0:T(8,128)(2,1)S(1)}, bf16[512,512]{1,0:T(8,128)(2,1)S(1)}, u32[]{:S(2)}, u32[]{:S(2)}) collective-permute-start(bf16[512,512]{1,0:T(8,128)(2,1)S(1)} %bitcast.7), channel_id=1, source_target_pairs={{0,192},{1,193},{16,208},{17,209},{32,224},{33,225},{48,240},{49,2... | collective-permute-start | bytes 1572872 | tf_op jit(solution)/shard_map/r_up/ppermute | solution.py:37
  48.8 13.5 %collective-permute-start.12 = (bf16[512,512]{1,0:T(8,128)(2,1)S(1)}, bf16[512,512]{1,0:T(8,128)(2,1)S(1)}, u32[]{:S(2)}, u32[]{:S(2)}) collective-permute-start(bf16[512,512]{1,0:T(8,128)(2,1)S(1)} %bitcast.8), channel_id=1, source_target_pairs={{0,64},{1,65},{16,80},{17,81},{32,96},{33,97},{48,112},{49,113},{2... | collective-permute-start | bytes 1572872 | tf_op jit(solution)/shard_map/r_down/ppermute | solution.py:37
  50.3 13.5 %collective-permute-start.13 = (bf16[128,2048]{1,0:T(8,128)(2,1)S(1)}, bf16[128,2048]{1,0:T(8,128)(2,1)S(1)}, u32[]{:S(2)}, u32[]{:S(2)}) collective-permute-start(bf16[128,2048]{1,0:T(8,128)(2,1)S(1)} %copy-done), channel_id=1, source_target_pairs={{0,8},{1,9},{16,24},{17,25},{32,40},{33,41},{48,56},{49,57},{2,10}... | collective-permute-start | bytes 1572872 | tf_op jit(solution)/shard_map/n_two/ppermute | solution.py:37
  51.9 15.8 %collective-permute-start.19 = (bf16[64,2048]{1,0:T(8,128)(2,1)S(1)}, bf16[64,2048]{1,0:T(8,128)(2,1)S(1)}, u32[]{:S(2)}, u32[]{:S(2)}) collective-permute-start(bf16[64,2048]{1,0:T(8,128)(2,1)S(1)} %copy-done.3), channel_id=1, source_target_pairs={{0,2},{1,3},{16,18},{17,19},{32,34},{33,35},{48,50},{49,51},{2,0},... | collective-permute-start | bytes 786440 | tf_op jit(solution)/shard_map/far2/ppermute | solution.py:37
  63.8 5.7 %collective-permute-start.16 = (bf16[64,2048]{1,0:T(8,128)(2,1)S(1)}, bf16[64,2048]{1,0:T(8,128)(2,1)S(1)}, u32[]{:S(2)}, u32[]{:S(2)}) collective-permute-start(bf16[64,2048]{1,0:T(8,128)(2,1)S(1)} %collective-permute-done.14._.refs_0_), channel_id=1, source_target_pairs={{0,12},{1,13},{16,28},{17,29},{32,44},{33,45},{48,60},{49,61},{2,1... | collective-permute-start | bytes 786440 | tf_op jit(solution)/shard_map/a1/ppermute | solution.py:37
  65.2 6.8 %collective-permute-start.17 = (bf16[64,2048]{1,0:T(8,128)(2,1)S(1)}, bf16[64,2048]{1,0:T(8,128)(2,1)S(1)}, u32[]{:S(2)}, u32[]{:S(2)}) collective-permute-start(bf16[64,2048]{1,0:T(8,128)(2,1)S(1)} %collective-permute-done.14._.refs_0_), channel_id=1, source_target_pairs={{0,8},{1,9},{16,24},{17,25},{32,40},{33,41},{48,56},{49,57},{2,10}... | collective-permute-start | bytes 786440 | tf_op jit(solution)/shard_map/a2/ppermute | solution.py:37
  65.5 17.0 %collective-permute-start.18 = (bf16[64,2048]{1,0:T(8,128)(2,1)S(1)}, bf16[64,2048]{1,0:T(8,128)(2,1)S(1)}, u32[]{:S(2)}, u32[]{:S(2)}) collective-permute-start(bf16[64,2048]{1,0:T(8,128)(2,1)S(1)} %collective-permute-done.14._.refs_0_), channel_id=1, source_target_pairs={{0,4},{1,5},{16,20},{17,21},{32,36},{33,37},{48,52},{49,53},{2,6},... | collective-permute-start | bytes 786440 | tf_op jit(solution)/shard_map/a3/ppermute | solution.py:37
  66.2 17.5 %collective-permute-start.15 = (bf16[512,512]{1,0:T(8,128)(2,1)S(1)}, bf16[512,512]{1,0:T(8,128)(2,1)S(1)}, u32[]{:S(2)}, u32[]{:S(2)}) collective-permute-start(bf16[512,512]{1,0:T(8,128)(2,1)S(1)} %collective-permute-done.11.refs_1_), channel_id=1, source_target_pairs={{0,192},{1,193},{16,208},{17,209},{32,224},{33,225},{48,240},{49,2... | collective-permute-start | bytes 1572872 | tf_op jit(solution)/shard_map/r_next/ppermute | solution.py:37
  67.7 20.5 %collective-permute-start.20 = (bf16[64,2048]{1,0:T(8,128)(2,1)S(1)}, bf16[64,2048]{1,0:T(8,128)(2,1)S(1)}, u32[]{:S(2)}, u32[]{:S(2)}) collective-permute-start(bf16[64,2048]{1,0:T(8,128)(2,1)S(1)} %collective-permute-done.19._.refs_4_), channel_id=1, source_target_pairs={{0,12},{1,13},{16,28},{17,29},{32,44},{33,45},{48,60},{49,61},{2,1... | collective-permute-start | bytes 786440 | tf_op jit(solution)/shard_map/b1/ppermute | solution.py:37
  69.4 18.8 %collective-permute-start.21 = (bf16[64,2048]{1,0:T(8,128)(2,1)S(1)}, bf16[64,2048]{1,0:T(8,128)(2,1)S(1)}, u32[]{:S(2)}, u32[]{:S(2)}) collective-permute-start(bf16[64,2048]{1,0:T(8,128)(2,1)S(1)} %collective-permute-done.19._.refs_4_), channel_id=1, source_target_pairs={{0,8},{1,9},{16,24},{17,25},{32,40},{33,41},{48,56},{49,57},{2,10}... | collective-permute-start | bytes 786440 | tf_op jit(solution)/shard_map/b2/ppermute | solution.py:37
  72.0 18.9 %collective-permute-start.22 = (bf16[64,2048]{1,0:T(8,128)(2,1)S(1)}, bf16[64,2048]{1,0:T(8,128)(2,1)S(1)}, u32[]{:S(2)}, u32[]{:S(2)}) collective-permute-start(bf16[64,2048]{1,0:T(8,128)(2,1)S(1)} %collective-permute-done.19._.refs_4_), channel_id=1, source_target_pairs={{0,4},{1,5},{16,20},{17,21},{32,36},{33,37},{48,52},{49,53},{2,6},... | collective-permute-start | bytes 786440 | tf_op jit(solution)/shard_map/b3/ppermute | solution.py:37
  86.2 8.3 %collective-permute-start.24 = (bf16[512,512]{1,0:T(8,128)(2,1)S(1)}, bf16[512,512]{1,0:T(8,128)(2,1)S(1)}, u32[]{:S(2)}, u32[]{:S(2)}) collective-permute-start(bf16[512,512]{1,0:T(8,128)(2,1)S(1)} %get-tuple-element.82.own_ref), channel_id=1, source_target_pairs={{0,1},{1,0},{16,17},{17,16},{32,33},{33,32},{48,49},{49,48},{2,3},... | collective-permute-start | bytes 1572872 | tf_op jit(solution)/shard_map/swap_near/ppermute | solution.py:37
  93.0 3.0 %collective-permute-start.23 = (bf16[512,512]{1,0:T(8,128)(2,1)S(1)}, bf16[512,512]{1,0:T(8,128)(2,1)S(1)}, u32[]{:S(2)}, u32[]{:S(2)}) collective-permute-start(bf16[512,512]{1,0:T(8,128)(2,1)S(1)} %far.1.own_ref), channel_id=1, source_target_pairs={{0,1},{1,0},{16,17},{17,16},{32,33},{33,32},{48,49},{49,48},{2,3},... | collective-permute-start | bytes 1572872 | tf_op jit(solution)/shard_map/swap_far/ppermute | solution.py:37

commit v3 on v2

--- a/solution.py
+++ b/solution.py
@@ -97,14 +97,12 @@
             )
         for group in range(width // 4):
             held = [prod_ref[layer, pl.ds(group * 4 + s, count, stride=width), :] for s in range(4)]
-            tile = None
-            for r in range(4):
-                value = held[r]
-                for n in range(1, 4):
-                    value = jnp.where(row == n, held[(n + r) % 4], value)
-                if r > 0:
-                    value = pltpu.roll(value, r * width, 1)
-                tile = value if tile is None else jnp.where(turn == r, value, tile)
+            half = [jnp.where(row % 2 == 1, held[(r + 1) % 4], held[r]) for r in range(4)]
+            full = [jnp.where(row >= 2, half[(r + 2) % 4], half[r]) for r in range(4)]
+            full = [full[0]] + [pltpu.roll(full[r], r * width, 1) for r in range(1, 4)]
+            low = jnp.where(turn == 1, full[1], full[0])
+            high = jnp.where(turn == 3, full[3], full[2])
+            tile = jnp.where(turn >= 2, high, low)
             at = layer * width * width + group * 128
             value = (tile * scale).astype(outs[0].dtype)
             for out_ref in outs:
@@ -141,7 +139,7 @@
         lax.fori_loop(first, first + steps // max(len(outs) - 1, 1), step, 0)
 
 
-def form_grads(acts, backs, cuts=0, block=16):
+def form_grads(acts, backs, cuts=0, block=32):
     count, layers, width, toks = acts.shape
     entries = layers * width * width
     shapes = [jax.ShapeDtypeStruct((rows, entries), jnp.bfloat16) for rows in [count] + [count // max(cuts, 1)] * cuts]
@@ -227,7 +225,7 @@
         out_shape=jax.ShapeDtypeStruct((NX, NZL * count // NX, width), jnp.bfloat16),
         scratch_shapes=[pltpu.SemaphoreType.DMA((NZL * NX,))],
         compiler_params=pltpu.CompilerParams(vmem_limit_bytes=16 * MIB),
-        cost_estimate=FREE,
+        cost_estimate=pl.CostEstimate(flops=20 * 10**9, bytes_accessed=0, transcendentals=0),
         name="join",
     )(pos, *parts)
     return out.reshape(NZL * count, width)
@@ -356,21 +354,23 @@
     near = [train_grad, send(train_grad, "n_up", dy=-1), None, send(train_grad, "n_down", dy=1)]
     part = apply_rows(pos, got[:NX], got[NX:])
     parts = [part] + [send(part, "low%d" % s, dzl=-s) for s in (1, 2, 3)]
-    first, second, *parts = after(first, second, *parts)
+    near[1], near[3] = after(near[1], near[3])
+    near[2] = send(near[1], "n_two", dy=-1)
+    first, second, parts[1], parts[2] = after(first, second, parts[1], parts[2])
     first = send(first, "far1", dz=NZL)
     second = send(second, "far2", dz=NZL)
     mine = join_queries(pos, parts)
-    mine, again, near[1], near[3] = after(mine, train_grad, near[1], near[3])
     queries = [mine, send(mine, "r_up", dx=-1), None, send(mine, "r_down", dx=1)]
-    near[2] = send(again, "n_two", dy=2)
     later = pass_on(pos, first)
     queries[1], queries[3], near[2], first, later = after(queries[1], queries[3], near[2], first, later)
-    firsts = [first] + [send(first, "a%d" % s, dy=-s) for s in (1, 2, 3)]
+    firsts = [first, send(first, "a1", dy=-1), None, send(first, "a3", dy=1)]
     queries[2] = send(queries[1], "r_next", dx=-1)
-    seconds = [second] + [send(second, "b%d" % s, dy=-s) for s in (1, 2, 3)]
+    second, firsts[1], firsts[3] = after(second, firsts[1], firsts[3])
+    firsts[2] = send(firsts[3], "a2", dy=1)
+    seconds = [second, send(second, "b1", dy=-1), None, send(second, "b3", dy=1)]
+    seconds[2] = send(seconds[1], "b2", dy=-1)
     later, *firsts = after(later, *firsts)
-    last = pass_on(later, second)
-    queries[2], last = after(queries[2], last)
+    last = later
     near_terms, packed = score_near(last, queries, near, scale)
     near_other = send(near_terms, "swap_near", dcore=1)
     far_terms = score_far(pos, packed, firsts, seconds, scale)

time: 98.4 us -> 94.9 us (0.964)
  waiting for transfers between devices: 36.5 us -> 31.5 us
  starting transfers between devices: 37.6 us -> 41.3 us
  Pallas kernels: 23.2 us -> 21.6 us
    ppermute x25, waiting for transfers between devices: 36.5 us -> 31.5 us  [send(): return lax.ppermute(value, AXES, pairs(move))]
    ppermute x25, starting transfers between devices: 37.6 us -> 41.3 us  [send(): return lax.ppermute(value, AXES, pairs(move))]
    pallas_call x2 -> x1, Pallas kernels: 2.27 us -> 1.14 us  [pass_on(): pl.pallas_call(pass_kernel, in_specs=[scalars(), anywhere()], out_specs=s...]
  transfers between devices with their start and end apart: 25 -> 25, of which waited for: 12 -> 10; matrix products, arithmetic and copies ran while one was open for 0% -> 0% of each run, Pallas kernels for 19% -> 16%
where the time goes in v3:
time: 94.9 us; the launch traced here: 94.8 us
  starting transfers between devices  41.3 us (44%)
  waiting for transfers between devices  31.5 us (33%)
  Pallas kernels  21.6 us (23%)
    ppermute x25, starting transfers between devices, send(): return lax.ppermute(value, AXES, pairs(move))  41.3 us
    ppermute x25, waiting for transfers between devices, send(): return lax.ppermute(value, AXES, pairs(move))  31.5 us
    pallas_call x2, Pallas kernels, form_grads(): pl.pallas_call(functools.partial(form_kernel, block), in_specs=[anywhere(...  9.5 us
    pallas_call x2, Pallas kernels, add_terms(): pl.pallas_call(add_kernel, in_specs=[scalars(), whole(), whole()] + [anyw...  3.15 us
    pallas_call x1, Pallas kernels, score_near(): pl.pallas_call(functools.partial(near_kernel, scale), in_specs=[scalars()...  2.42 us
    pallas_call x1, Pallas kernels, score_far(): pl.pallas_call(functools.partial(far_kernel, scale), in_specs=[scalars()]...  2.08 us
  transfers between devices with their start and end apart: 25, of which 10 were waited for; matrix products, arithmetic and copies ran while one was open for 0% of the time, Pallas kernels for 16%

profile of v3, /device:TPU:1, one launch (start us, length us, event | category | flops | bytes accessed | tf_op | source)
XLA Modules:
  0.0 94.8 jit_solution(11583724035321848172)
XLA Ops:
  0.0 3.2 %form.2.refs_0_ = bf16[32,2048]{1,0:T(8,128)(2,1)} custom-call(bf16[32,2,32,256]{3,2,1,0:T(8,128)(2,1)} %bitcast.10, bf16[32,2,32,256]{3,2,1,0:T(8,128)(2,1)} %bitcast.11), custom_call_target="tpu_custom_call" | custom-call | tf_op jit(solution)/shard_map/form/pallas_call | solution.py:146
  3.2 3.4 %collective-permute-start = (bf16[32,2048]{1,0:T(8,128)(2,1)}, bf16[32,2048]{1,0:T(8,128)(2,1)S(1)}, u32[]{:S(2)}, u32[]{:S(2)}) collective-permute-start(bf16[32,2048]{1,0:T(8,128)(2,1)} %form.2.refs_0_), channel_id=1, source_target_pairs={{0,192},{1,193},{16,208},{17,209},{32,224},{33,225},{48,240},{49,2... | collective-permute-start | bytes 393224 | tf_op jit(solution)/shard_map/g_up/ppermute | solution.py:37
  6.6 0.0 copy-done.2
  6.6 5.6 %collective-permute-start.3 = (bf16[2,64,1024]{2,1,0:T(8,128)(2,1)S(1)}, bf16[2,64,1024]{2,1,0:T(8,128)(2,1)S(1)}, u32[]{:S(2)}, u32[]{:S(2)}) collective-permute-start(bf16[2,64,1024]{2,1,0:T(8,128)(2,1)S(1)} %copy-done.2), channel_id=1, source_target_pairs={{0,50},{1,51},{16,0},{17,1},{32,16},{33,17},{48,32},{49,33},{2,48}... | collective-permute-start | bytes 786440 | tf_op jit(solution)/shard_map/p_up/ppermute | solution.py:37
  12.2 0.0 collective-permute-start.4
  12.2 0.0 collective-permute-start.5
  12.2 0.5 collective-permute-start.1
  12.7 0.0 collective-permute-done.refs_1_
  12.7 0.6 collective-permute-start.2
  13.3 6.3 %form.3 = (bf16[128,2048]{1,0:T(8,128)(2,1)}, bf16[64,2048]{1,0:T(8,128)(2,1)}, bf16[64,2048]{1,0:T(8,128)(2,1)}) custom-call(bf16[128,2,32,256]{3,2,1,0:T(8,128)(2,1)} %acts_hbm, bf16[128,2,32,256]{3,2,1,0:T(8,128)(2,1)} %backs_hbm.1), custom_call_target="tpu_custom_call" | custom-call | tf_op jit(solution)/shard_map/form/pallas_call | solution.py:146
  19.6 0.1 pad_add_fusion.pos_ref
  19.7 0.0 collective-permute-done.1.refs_2_
  19.7 0.0 collective-permute-done.2.refs_3_
  19.7 0.0 collective-permute-done.3.refs_5_
  19.7 3.0 %collective-permute-done.4.refs_6_ = bf16[2,64,1024]{2,1,0:T(8,128)(2,1)S(1)} collective-permute-done((bf16[2,64,1024]{2,1,0:T(8,128)(2,1)S(1)}, bf16[2,64,1024]{2,1,0:T(8,128)(2,1)S(1)}, u32[]{:S(2)}, u32[]{:S(2)}) %collective-permute-start.4) | collective-permute-done | bytes 262176 | tf_op jit(solution)/shard_map/p_far/ppermute | solution.py:37
  22.8 1.9 %collective-permute-done.5.refs_7_ = bf16[2,64,1024]{2,1,0:T(8,128)(2,1)S(1)} collective-permute-done((bf16[2,64,1024]{2,1,0:T(8,128)(2,1)S(1)}, bf16[2,64,1024]{2,1,0:T(8,128)(2,1)S(1)}, u32[]{:S(2)}, u32[]{:S(2)}) %collective-permute-start.5) | collective-permute-done | bytes 262176 | tf_op jit(solution)/shard_map/p_down/ppermute | solution.py:37
  24.7 0.0 copy-done.1
  24.7 1.9 %apply.1.refs_0_ = bf16[128,512]{1,0:T(8,128)(2,1)S(1)} custom-call(s32[4]{0:T(128)S(1)} %pad_add_fusion.pos_ref, bf16[32,2048]{1,0:T(8,128)(2,1)S(1)} %copy-done.1, bf16[32,2048]{1,0:T(8,128)(2,1)S(1)} %collective-permute-done.refs_1_, bf16[32,2048]{1,0:T(8,128)(2,1)S(1)} %collective-permute-done.1.refs_2_, ...), custom_call_target="tpu_custom_call" | custom-call | tf_op jit(solution)/shard_map/apply/pallas_call | solution.py:191
  26.6 2.1 %collective-permute-start.6 = (bf16[128,512]{1,0:T(8,128)(2,1)S(1)}, bf16[128,512]{1,0:T(8,128)(2,1)S(1)}, u32[]{:S(2)}, u32[]{:S(2)}) collective-permute-start(bf16[128,512]{1,0:T(8,128)(2,1)S(1)} %apply.1.refs_0_), channel_id=1, source_target_pairs={{0,48},{1,49},{16,0},{17,1},{32,16},{33,17},{48,32},{49,33},{2,50}... | collective-permute-start | bytes 393224 | tf_op jit(solution)/shard_map/low1/ppermute | solution.py:37
  28.7 0.3 collective-permute-start.7
  29.0 0.1 collective-permute-start.8
  29.0 2.7 %collective-permute-start.11 = (bf16[128,2048]{1,0:T(8,128)(2,1)}, bf16[128,2048]{1,0:T(8,128)(2,1)S(1)}, u32[]{:S(2)}, u32[]{:S(2)}) collective-permute-start(bf16[128,2048]{1,0:T(8,128)(2,1)} %get-tuple-element.57.refs_4_), channel_id=1, source_target_pairs={{0,12},{1,13},{16,28},{17,29},{32,44},{33,45},{48,60},{49,61},{2,1... | collective-permute-start | bytes 1572872 | tf_op jit(solution)/shard_map/n_up/ppermute | solution.py:37
  31.8 0.0 collective-permute-start.12
  31.8 0.2 collective-permute-done.6.refs_1_
  32.0 9.3 %collective-permute-done.7.refs_2_ = bf16[128,512]{1,0:T(8,128)(2,1)S(1)} collective-permute-done((bf16[128,512]{1,0:T(8,128)(2,1)S(1)}, bf16[128,512]{1,0:T(8,128)(2,1)S(1)}, u32[]{:S(2)}, u32[]{:S(2)}) %collective-permute-start.7) | collective-permute-done | bytes 131104 | tf_op jit(solution)/shard_map/low2/ppermute | solution.py:37
  41.3 3.5 %collective-permute-start.14 = (bf16[64,2048]{1,0:T(8,128)(2,1)}, bf16[64,2048]{1,0:T(8,128)(2,1)S(1)}, u32[]{:S(2)}, u32[]{:S(2)}) collective-permute-start(bf16[64,2048]{1,0:T(8,128)(2,1)} %get-tuple-element.59), channel_id=1, source_target_pairs={{0,2},{1,3},{16,18},{17,19},{32,34},{33,35},{48,50},{49,51},{2,0},... | collective-permute-start | bytes 786440 | tf_op jit(solution)/shard_map/far1/ppermute | solution.py:37
  44.7 0.0 collective-permute-done.8.refs_3_
  44.8 1.4 %join.1 = bf16[4,128,512]{2,1,0:T(8,128)(2,1)S(1)} custom-call(s32[4]{0:T(128)S(1)} %pad_add_fusion.pos_ref, bf16[128,512]{1,0:T(8,128)(2,1)S(1)} %apply.1.refs_0_, bf16[128,512]{1,0:T(8,128)(2,1)S(1)} %collective-permute-done.6.refs_1_, bf16[128,512]{1,0:T(8,128)(2,1)S(1)} %collective-permute-done.7.refs_2_, bf16[128,512]{1,0:T(8,128)(2,1)S(1)} %collective-permute-done.8.refs_3_), custom_call_target="tpu_custom_call" | custom-call | flops 20000000000 | tf_op jit(solution)/shard_map/join/pallas_call | solution.py:221
  46.2 0.0 copy-start
  46.2 0.3 collective-permute-start.10
  46.4 2.7 %collective-permute-start.9 = (bf16[512,512]{1,0:T(8,128)(2,1)S(1)}, bf16[512,512]{1,0:T(8,128)(2,1)S(1)}, u32[]{:S(2)}, u32[]{:S(2)}) collective-permute-start(bf16[512,512]{1,0:T(8,128)(2,1)S(1)} %bitcast.8), channel_id=1, source_target_pairs={{0,192},{1,193},{16,208},{17,209},{32,224},{33,225},{48,240},{49,2... | collective-permute-start | bytes 1572872 | tf_op jit(solution)/shard_map/r_up/ppermute | solution.py:37
  49.1 0.0 collective-permute-done.11.refs_5_
  49.1 0.0 collective-permute-done.12.refs_7_
  49.1 2.7 %collective-permute-start.13 = (bf16[128,2048]{1,0:T(8,128)(2,1)S(1)}, bf16[128,2048]{1,0:T(8,128)(2,1)S(1)}, u32[]{:S(2)}, u32[]{:S(2)}) collective-permute-start(bf16[128,2048]{1,0:T(8,128)(2,1)S(1)} %collective-permute-done.11.refs_5_), channel_id=1, source_target_pairs={{0,12},{1,13},{16,28},{17,29},{32,44},{33,45},{48,60},{49,61},{2,1... | collective-permute-start | bytes 1572872 | tf_op jit(solution)/shard_map/n_two/ppermute | solution.py:37
  51.8 1.9 %collective-permute-start.15 = (bf16[64,2048]{1,0:T(8,128)(2,1)S(1)}, bf16[64,2048]{1,0:T(8,128)(2,1)S(1)}, u32[]{:S(2)}, u32[]{:S(2)}) collective-permute-start(bf16[64,2048]{1,0:T(8,128)(2,1)S(1)} %copy-done.3), channel_id=1, source_target_pairs={{0,2},{1,3},{16,18},{17,19},{32,34},{33,35},{48,50},{49,51},{2,0},... | collective-permute-start | bytes 786440 | tf_op jit(solution)/shard_map/far2/ppermute | solution.py:37
  53.8 5.3 %collective-permute-done.14._.refs_0_ = bf16[64,2048]{1,0:T(8,128)(2,1)S(1)} collective-permute-done((bf16[64,2048]{1,0:T(8,128)(2,1)}, bf16[64,2048]{1,0:T(8,128)(2,1)S(1)}, u32[]{:S(2)}, u32[]{:S(2)}) %collective-permute-start.14) | collective-permute-done | bytes 262176 | tf_op jit(solution)/shard_map/far1/ppermute | solution.py:37
  59.0 1.1 %pass.1.pos_ref = s32[4]{0:T(128)S(1)} custom-call(s32[4]{0:T(128)S(1)} %pad_add_fusion.pos_ref, bf16[64,2048]{1,0:T(8,128)(2,1)S(1)} %collective-permute-done.14._.refs_0_), custom_call_target="tpu_custom_call" | custom-call | flops 4000000000 | tf_op jit(solution)/shard_map/pass/pallas_call | solution.py:49
  60.2 0.3 collective-permute-done.10.refs_3_
  60.5 0.0 collective-permute-done.9.refs_1_
  60.5 1.4 %collective-permute-done.13.refs_6_ = bf16[128,2048]{1,0:T(8,128)(2,1)S(1)} collective-permute-done((bf16[128,2048]{1,0:T(8,128)(2,1)S(1)}, bf16[128,2048]{1,0:T(8,128)(2,1)S(1)}, u32[]{:S(2)}, u32[]{:S(2)}) %collective-permute-start.13) | collective-permute-done | bytes 524320 | tf_op jit(solution)/shard_map/n_two/ppermute | solution.py:37
  61.8 3.4 %collective-permute-start.16 = (bf16[64,2048]{1,0:T(8,128)(2,1)S(1)}, bf16[64,2048]{1,0:T(8,128)(2,1)S(1)}, u32[]{:S(2)}, u32[]{:S(2)}) collective-permute-start(bf16[64,2048]{1,0:T(8,128)(2,1)S(1)} %collective-permute-done.14._.refs_0_), channel_id=1, source_target_pairs={{0,12},{1,13},{16,28},{17,29},{32,44},{33,45},{48,60},{49,61},{2,1... | collective-permute-start | bytes 786440 | tf_op jit(solution)/shard_map/a1/ppermute | solution.py:37
  65.3 0.0 collective-permute-start.17
  65.3 0.4 collective-permute-start.19
  65.6 0.0 collective-permute-done.15.refs_4_
  65.6 2.9 %collective-permute-done.16.refs_1_ = bf16[64,2048]{1,0:T(8,128)(2,1)S(1)} collective-permute-done((bf16[64,2048]{1,0:T(8,128)(2,1)S(1)}, bf16[64,2048]{1,0:T(8,128)(2,1)S(1)}, u32[]{:S(2)}, u32[]{:S(2)}) %collective-permute-start.16) | collective-permute-done | bytes 262176 | tf_op jit(solution)/shard_map/a1/ppermute | solution.py:37
  68.6 3.1 %collective-permute-done.17.refs_3_ = bf16[64,2048]{1,0:T(8,128)(2,1)S(1)} collective-permute-done((bf16[64,2048]{1,0:T(8,128)(2,1)S(1)}, bf16[64,2048]{1,0:T(8,128)(2,1)S(1)}, u32[]{:S(2)}, u32[]{:S(2)}) %collective-permute-start.17) | collective-permute-done | bytes 262176 | tf_op jit(solution)/shard_map/a3/ppermute | solution.py:37
  71.7 1.4 %collective-permute-start.20 = (bf16[64,2048]{1,0:T(8,128)(2,1)S(1)}, bf16[64,2048]{1,0:T(8,128)(2,1)S(1)}, u32[]{:S(2)}, u32[]{:S(2)}) collective-permute-start(bf16[64,2048]{1,0:T(8,128)(2,1)S(1)} %collective-permute-done.15.refs_4_), channel_id=1, source_target_pairs={{0,12},{1,13},{16,28},{17,29},{32,44},{33,45},{48,60},{49,61},{2,1... | collective-permute-start | bytes 786440 | tf_op jit(solution)/shard_map/b1/ppermute | solution.py:37
  73.0 0.1 collective-permute-start.18
  73.2 0.0 collective-permute-start.22
  73.2 4.0 %collective-permute-done.20.refs_5_ = bf16[64,2048]{1,0:T(8,128)(2,1)S(1)} collective-permute-done((bf16[64,2048]{1,0:T(8,128)(2,1)S(1)}, bf16[64,2048]{1,0:T(8,128)(2,1)S(1)}, u32[]{:S(2)}, u32[]{:S(2)}) %collective-permute-start.20) | collective-permute-done | bytes 262176 | tf_op jit(solution)/shard_map/b1/ppermute | solution.py:37
  77.2 2.3 %collective-permute-start.21 = (bf16[64,2048]{1,0:T(8,128)(2,1)S(1)}, bf16[64,2048]{1,0:T(8,128)(2,1)S(1)}, u32[]{:S(2)}, u32[]{:S(2)}) collective-permute-start(bf16[64,2048]{1,0:T(8,128)(2,1)S(1)} %collective-permute-done.20.refs_5_), channel_id=1, source_target_pairs={{0,12},{1,13},{16,28},{17,29},{32,44},{33,45},{48,60},{49,61},{2,1... | collective-permute-start | bytes 786440 | tf_op jit(solution)/shard_map/b2/ppermute | solution.py:37
  79.5 0.0 collective-permute-done.18.refs_2_
  79.5 0.0 collective-permute-done.19.refs_2_
  79.5 0.0 copy-done
  79.5 2.4 %near.1 = (bf16[512,512]{1,0:T(8,128)(2,1)S(1)}, bf16[512,2048]{1,0:T(8,128)(2,1)S(1)}) custom-call(s32[4]{0:T(128)S(1)} %pass.1.pos_ref, bf16[512,512]{1,0:T(8,128)(2,1)S(1)} %bitcast.9, bf16[512,512]{1,0:T(8,128)(2,1)S(1)} %collective-permute-done.9.refs_1_, bf16[512,512]{1,0:T(8,128)(2,1)S(1)} %collective-permute-done.19.refs_2_, ...), custom_call_target="tpu_custom_call" | custom-call | tf_op jit(solution)/shard_map/near/pallas_call | solution.py:267
  81.9 6.4 %collective-permute-start.24 = (bf16[512,512]{1,0:T(8,128)(2,1)S(1)}, bf16[512,512]{1,0:T(8,128)(2,1)S(1)}, u32[]{:S(2)}, u32[]{:S(2)}) collective-permute-start(bf16[512,512]{1,0:T(8,128)(2,1)S(1)} %get-tuple-element.76.own_ref), channel_id=1, source_target_pairs={{0,1},{1,0},{16,17},{17,16},{32,33},{33,32},{48,49},{49,48},{2,3},... | collective-permute-start | bytes 1572872 | tf_op jit(solution)/shard_map/swap_near/ppermute | solution.py:37
  88.3 0.0 collective-permute-done.22.refs_7_
  88.3 0.0 collective-permute-done.21.refs_6_
  88.3 2.1 %far.1.own_ref = bf16[512,512]{1,0:T(8,128)(2,1)S(1)} custom-call(s32[4]{0:T(128)S(1)} %pad_add_fusion.pos_ref, bf16[512,2048]{1,0:T(8,128)(2,1)S(1)} %get-tuple-element.70.right_ref, bf16[64,2048]{1,0:T(8,128)(2,1)S(1)} %collective-permute-done.14._.refs_0_, bf16[64,2048]{1,0:T(8,128)(2,1)S(1)} %collective-permute-done.16.refs_1_, ...), custom_call_target="tpu_custom_call" | custom-call | tf_op jit(solution)/shard_map/far/pallas_call | solution.py:299
  90.4 1.0 %collective-permute-start.23 = (bf16[512,512]{1,0:T(8,128)(2,1)S(1)}, bf16[512,512]{1,0:T(8,128)(2,1)S(1)}, u32[]{:S(2)}, u32[]{:S(2)}) collective-permute-start(bf16[512,512]{1,0:T(8,128)(2,1)S(1)} %far.1.own_ref), channel_id=1, source_target_pairs={{0,1},{1,0},{16,17},{17,16},{32,33},{33,32},{48,49},{49,48},{2,3},... | collective-permute-start | bytes 1572872 | tf_op jit(solution)/shard_map/swap_far/ppermute | solution.py:37
  91.4 0.0 collective-permute-done.24.other_ref
  91.4 1.6 %add.30.refs_0_ = f32[1024,512]{1,0:T(8,128)} custom-call(s32[4]{0:T(128)S(1)} %get-tuple-element.78.places_ref, bf16[512,512]{1,0:T(8,128)(2,1)S(1)} %get-tuple-element.76.own_ref, bf16[512,512]{1,0:T(8,128)(2,1)S(1)} %collective-permute-done.24.other_ref), custom_call_target="tpu_custom_call" | custom-call | tf_op jit(solution)/shard_map/add/pallas_call | solution.py:328
  93.0 0.0 collective-permute-done.23.other_ref
  93.0 1.6 %add.31 = f32[1024,512]{1,0:T(8,128)} custom-call(s32[4]{0:T(128)S(1)} %get-tuple-element.77.places_ref, bf16[512,512]{1,0:T(8,128)(2,1)S(1)} %far.1.own_ref, bf16[512,512]{1,0:T(8,128)(2,1)S(1)} %collective-permute-done.23.other_ref, f32[1024,512]{1,0:T(8,128)} %add.30.refs_0_), custom_call_target="tpu_custom_call", output_to_operand_aliasing={{}: (3, {})} | custom-call | tf_op jit(solution)/shard_map/add/pallas_call | solution.py:328
  (5 shorter events, 0.0 us)
Async XLA Ops:
  0.0 6.6 %copy-start.2 = (bf16[2,64,1024]{2,1,0:T(8,128)(2,1)S(1)}, bf16[2,64,1024]{2,1,0:T(8,128)(2,1)}, u32[]{:S(2)}) copy-start(bf16[2,64,1024]{2,1,0:T(8,128)(2,1)} %refs_4_) | copy-start | bytes 786436
  3.2 9.5 %collective-permute-start = (bf16[32,2048]{1,0:T(8,128)(2,1)}, bf16[32,2048]{1,0:T(8,128)(2,1)S(1)}, u32[]{:S(2)}, u32[]{:S(2)}) collective-permute-start(bf16[32,2048]{1,0:T(8,128)(2,1)} %form.2.refs_0_), channel_id=1, source_target_pairs={{0,192},{1,193},{16,208},{17,209},{32,224},{33,225},{48,240},{49,2... | collective-permute-start | bytes 393224 | tf_op jit(solution)/shard_map/g_up/ppermute | solution.py:37
  6.6 13.1 %collective-permute-start.3 = (bf16[2,64,1024]{2,1,0:T(8,128)(2,1)S(1)}, bf16[2,64,1024]{2,1,0:T(8,128)(2,1)S(1)}, u32[]{:S(2)}, u32[]{:S(2)}) collective-permute-start(bf16[2,64,1024]{2,1,0:T(8,128)(2,1)S(1)} %copy-done.2), channel_id=1, source_target_pairs={{0,50},{1,51},{16,0},{17,1},{32,16},{33,17},{48,32},{49,33},{2,48}... | collective-permute-start | bytes 786440 | tf_op jit(solution)/shard_map/p_up/ppermute | solution.py:37
  12.2 10.6 %collective-permute-start.4 = (bf16[2,64,1024]{2,1,0:T(8,128)(2,1)S(1)}, bf16[2,64,1024]{2,1,0:T(8,128)(2,1)S(1)}, u32[]{:S(2)}, u32[]{:S(2)}) collective-permute-start(bf16[2,64,1024]{2,1,0:T(8,128)(2,1)S(1)} %copy-done.2), channel_id=1, source_target_pairs={{0,34},{1,33},{16,50},{17,49},{32,0},{33,3},{48,16},{49,19},{2,32}... | collective-permute-start | bytes 786440 | tf_op jit(solution)/shard_map/p_far/ppermute | solution.py:37
  12.2 12.5 %collective-permute-start.5 = (bf16[2,64,1024]{2,1,0:T(8,128)(2,1)S(1)}, bf16[2,64,1024]{2,1,0:T(8,128)(2,1)S(1)}, u32[]{:S(2)}, u32[]{:S(2)}) collective-permute-start(bf16[2,64,1024]{2,1,0:T(8,128)(2,1)S(1)} %copy-done.2), channel_id=1, source_target_pairs={{0,16},{1,17},{16,32},{17,33},{32,48},{33,49},{48,2},{49,3},{2,18}... | collective-permute-start | bytes 786440 | tf_op jit(solution)/shard_map/p_down/ppermute | solution.py:37
  12.2 7.5 %collective-permute-start.1 = (bf16[32,2048]{1,0:T(8,128)(2,1)}, bf16[32,2048]{1,0:T(8,128)(2,1)S(1)}, u32[]{:S(2)}, u32[]{:S(2)}) collective-permute-start(bf16[32,2048]{1,0:T(8,128)(2,1)} %form.2.refs_0_), channel_id=1, source_target_pairs={{0,128},{1,129},{16,144},{17,145},{32,160},{33,161},{48,176},{49,1... | collective-permute-start | bytes 393224 | tf_op jit(solution)/shard_map/g_far/ppermute | solution.py:37
  12.7 7.0 %collective-permute-start.2 = (bf16[32,2048]{1,0:T(8,128)(2,1)}, bf16[32,2048]{1,0:T(8,128)(2,1)S(1)}, u32[]{:S(2)}, u32[]{:S(2)}) collective-permute-start(bf16[32,2048]{1,0:T(8,128)(2,1)} %form.2.refs_0_), channel_id=1, source_target_pairs={{0,64},{1,65},{16,80},{17,81},{32,96},{33,97},{48,112},{49,113},{2... | collective-permute-start | bytes 393224 | tf_op jit(solution)/shard_map/g_down/ppermute | solution.py:37
  13.3 11.4 %copy-start.1 = (bf16[32,2048]{1,0:T(8,128)(2,1)S(1)}, bf16[32,2048]{1,0:T(8,128)(2,1)}, u32[]{:S(2)}) copy-start(bf16[32,2048]{1,0:T(8,128)(2,1)} %form.2.refs_0_) | copy-start | bytes 393220
  26.6 25.3 %copy-start.3 = (bf16[64,2048]{1,0:T(8,128)(2,1)S(1)}, bf16[64,2048]{1,0:T(8,128)(2,1)}, u32[]{:S(2)}) copy-start(bf16[64,2048]{1,0:T(8,128)(2,1)} %get-tuple-element.62) | copy-start | bytes 786436
  26.6 5.4 %collective-permute-start.6 = (bf16[128,512]{1,0:T(8,128)(2,1)S(1)}, bf16[128,512]{1,0:T(8,128)(2,1)S(1)}, u32[]{:S(2)}, u32[]{:S(2)}) collective-permute-start(bf16[128,512]{1,0:T(8,128)(2,1)S(1)} %apply.1.refs_0_), channel_id=1, source_target_pairs={{0,48},{1,49},{16,0},{17,1},{32,16},{33,17},{48,32},{49,33},{2,50}... | collective-permute-start | bytes 393224 | tf_op jit(solution)/shard_map/low1/ppermute | solution.py:37
  28.7 12.6 %collective-permute-start.7 = (bf16[128,512]{1,0:T(8,128)(2,1)S(1)}, bf16[128,512]{1,0:T(8,128)(2,1)S(1)}, u32[]{:S(2)}, u32[]{:S(2)}) collective-permute-start(bf16[128,512]{1,0:T(8,128)(2,1)S(1)} %apply.1.refs_0_), channel_id=1, source_target_pairs={{0,32},{1,33},{16,48},{17,49},{32,0},{33,1},{48,16},{49,17},{2,34}... | collective-permute-start | bytes 393224 | tf_op jit(solution)/shard_map/low2/ppermute | solution.py:37
  29.0 15.8 %collective-permute-start.8 = (bf16[128,512]{1,0:T(8,128)(2,1)S(1)}, bf16[128,512]{1,0:T(8,128)(2,1)S(1)}, u32[]{:S(2)}, u32[]{:S(2)}) collective-permute-start(bf16[128,512]{1,0:T(8,128)(2,1)S(1)} %apply.1.refs_0_), channel_id=1, source_target_pairs={{0,16},{1,17},{16,32},{17,33},{32,48},{33,49},{48,0},{49,1},{2,18}... | collective-permute-start | bytes 393224 | tf_op jit(solution)/shard_map/low3/ppermute | solution.py:37
  29.0 20.1 %collective-permute-start.11 = (bf16[128,2048]{1,0:T(8,128)(2,1)}, bf16[128,2048]{1,0:T(8,128)(2,1)S(1)}, u32[]{:S(2)}, u32[]{:S(2)}) collective-permute-start(bf16[128,2048]{1,0:T(8,128)(2,1)} %get-tuple-element.57.refs_4_), channel_id=1, source_target_pairs={{0,12},{1,13},{16,28},{17,29},{32,44},{33,45},{48,60},{49,61},{2,1... | collective-permute-start | bytes 1572872 | tf_op jit(solution)/shard_map/n_up/ppermute | solution.py:37
  31.8 17.3 %collective-permute-start.12 = (bf16[128,2048]{1,0:T(8,128)(2,1)}, bf16[128,2048]{1,0:T(8,128)(2,1)S(1)}, u32[]{:S(2)}, u32[]{:S(2)}) collective-permute-start(bf16[128,2048]{1,0:T(8,128)(2,1)} %get-tuple-element.57.refs_4_), channel_id=1, source_target_pairs={{0,4},{1,5},{16,20},{17,21},{32,36},{33,37},{48,52},{49,53},{2,6},... | collective-permute-start | bytes 1572872 | tf_op jit(solution)/shard_map/n_down/ppermute | solution.py:37
  41.3 17.7 %collective-permute-start.14 = (bf16[64,2048]{1,0:T(8,128)(2,1)}, bf16[64,2048]{1,0:T(8,128)(2,1)S(1)}, u32[]{:S(2)}, u32[]{:S(2)}) collective-permute-start(bf16[64,2048]{1,0:T(8,128)(2,1)} %get-tuple-element.59), channel_id=1, source_target_pairs={{0,2},{1,3},{16,18},{17,19},{32,34},{33,35},{48,50},{49,51},{2,0},... | collective-permute-start | bytes 786440 | tf_op jit(solution)/shard_map/far1/ppermute | solution.py:37
  46.2 33.3 %copy-start = (bf16[128,2048]{1,0:T(8,128)(2,1)S(1)}, bf16[128,2048]{1,0:T(8,128)(2,1)}, u32[]{:S(2)}) copy-start(bf16[128,2048]{1,0:T(8,128)(2,1)} %get-tuple-element.57.refs_4_) | copy-start | bytes 1572868
  46.2 14.3 %collective-permute-start.10 = (bf16[512,512]{1,0:T(8,128)(2,1)S(1)}, bf16[512,512]{1,0:T(8,128)(2,1)S(1)}, u32[]{:S(2)}, u32[]{:S(2)}) collective-permute-start(bf16[512,512]{1,0:T(8,128)(2,1)S(1)} %bitcast.7), channel_id=1, source_target_pairs={{0,64},{1,65},{16,80},{17,81},{32,96},{33,97},{48,112},{49,113},{2... | collective-permute-start | bytes 1572872 | tf_op jit(solution)/shard_map/r_down/ppermute | solution.py:37
  46.4 14.0 %collective-permute-start.9 = (bf16[512,512]{1,0:T(8,128)(2,1)S(1)}, bf16[512,512]{1,0:T(8,128)(2,1)S(1)}, u32[]{:S(2)}, u32[]{:S(2)}) collective-permute-start(bf16[512,512]{1,0:T(8,128)(2,1)S(1)} %bitcast.8), channel_id=1, source_target_pairs={{0,192},{1,193},{16,208},{17,209},{32,224},{33,225},{48,240},{49,2... | collective-permute-start | bytes 1572872 | tf_op jit(solution)/shard_map/r_up/ppermute | solution.py:37
  49.1 12.7 %collective-permute-start.13 = (bf16[128,2048]{1,0:T(8,128)(2,1)S(1)}, bf16[128,2048]{1,0:T(8,128)(2,1)S(1)}, u32[]{:S(2)}, u32[]{:S(2)}) collective-permute-start(bf16[128,2048]{1,0:T(8,128)(2,1)S(1)} %collective-permute-done.11.refs_5_), channel_id=1, source_target_pairs={{0,12},{1,13},{16,28},{17,29},{32,44},{33,45},{48,60},{49,61},{2,1... | collective-permute-start | bytes 1572872 | tf_op jit(solution)/shard_map/n_two/ppermute | solution.py:37
  51.8 13.8 %collective-permute-start.15 = (bf16[64,2048]{1,0:T(8,128)(2,1)S(1)}, bf16[64,2048]{1,0:T(8,128)(2,1)S(1)}, u32[]{:S(2)}, u32[]{:S(2)}) collective-permute-start(bf16[64,2048]{1,0:T(8,128)(2,1)S(1)} %copy-done.3), channel_id=1, source_target_pairs={{0,2},{1,3},{16,18},{17,19},{32,34},{33,35},{48,50},{49,51},{2,0},... | collective-permute-start | bytes 786440 | tf_op jit(solution)/shard_map/far2/ppermute | solution.py:37
  61.8 6.7 %collective-permute-start.16 = (bf16[64,2048]{1,0:T(8,128)(2,1)S(1)}, bf16[64,2048]{1,0:T(8,128)(2,1)S(1)}, u32[]{:S(2)}, u32[]{:S(2)}) collective-permute-start(bf16[64,2048]{1,0:T(8,128)(2,1)S(1)} %collective-permute-done.14._.refs_0_), channel_id=1, source_target_pairs={{0,12},{1,13},{16,28},{17,29},{32,44},{33,45},{48,60},{49,61},{2,1... | collective-permute-start | bytes 786440 | tf_op jit(solution)/shard_map/a1/ppermute | solution.py:37
  65.3 6.4 %collective-permute-start.17 = (bf16[64,2048]{1,0:T(8,128)(2,1)S(1)}, bf16[64,2048]{1,0:T(8,128)(2,1)S(1)}, u32[]{:S(2)}, u32[]{:S(2)}) collective-permute-start(bf16[64,2048]{1,0:T(8,128)(2,1)S(1)} %collective-permute-done.14._.refs_0_), channel_id=1, source_target_pairs={{0,4},{1,5},{16,20},{17,21},{32,36},{33,37},{48,52},{49,53},{2,6},... | collective-permute-start | bytes 786440 | tf_op jit(solution)/shard_map/a3/ppermute | solution.py:37
  65.3 14.2 %collective-permute-start.19 = (bf16[512,512]{1,0:T(8,128)(2,1)S(1)}, bf16[512,512]{1,0:T(8,128)(2,1)S(1)}, u32[]{:S(2)}, u32[]{:S(2)}) collective-permute-start(bf16[512,512]{1,0:T(8,128)(2,1)S(1)} %collective-permute-done.9.refs_1_), channel_id=1, source_target_pairs={{0,192},{1,193},{16,208},{17,209},{32,224},{33,225},{48,240},{49,2... | collective-permute-start | bytes 1572872 | tf_op jit(solution)/shard_map/r_next/ppermute | solution.py:37
  71.7 5.5 %collective-permute-start.20 = (bf16[64,2048]{1,0:T(8,128)(2,1)S(1)}, bf16[64,2048]{1,0:T(8,128)(2,1)S(1)}, u32[]{:S(2)}, u32[]{:S(2)}) collective-permute-start(bf16[64,2048]{1,0:T(8,128)(2,1)S(1)} %collective-permute-done.15.refs_4_), channel_id=1, source_target_pairs={{0,12},{1,13},{16,28},{17,29},{32,44},{33,45},{48,60},{49,61},{2,1... | collective-permute-start | bytes 786440 | tf_op jit(solution)/shard_map/b1/ppermute | solution.py:37
  73.0 6.4 %collective-permute-start.18 = (bf16[64,2048]{1,0:T(8,128)(2,1)S(1)}, bf16[64,2048]{1,0:T(8,128)(2,1)S(1)}, u32[]{:S(2)}, u32[]{:S(2)}) collective-permute-start(bf16[64,2048]{1,0:T(8,128)(2,1)S(1)} %collective-permute-done.17.refs_3_), channel_id=1, source_target_pairs={{0,4},{1,5},{16,20},{17,21},{32,36},{33,37},{48,52},{49,53},{2,6},... | collective-permute-start | bytes 786440 | tf_op jit(solution)/shard_map/a2/ppermute | solution.py:37
  73.2 15.2 %collective-permute-start.22 = (bf16[64,2048]{1,0:T(8,128)(2,1)S(1)}, bf16[64,2048]{1,0:T(8,128)(2,1)S(1)}, u32[]{:S(2)}, u32[]{:S(2)}) collective-permute-start(bf16[64,2048]{1,0:T(8,128)(2,1)S(1)} %collective-permute-done.15.refs_4_), channel_id=1, source_target_pairs={{0,4},{1,5},{16,20},{17,21},{32,36},{33,37},{48,52},{49,53},{2,6},... | collective-permute-start | bytes 786440 | tf_op jit(solution)/shard_map/b3/ppermute | solution.py:37
  77.2 11.1 %collective-permute-start.21 = (bf16[64,2048]{1,0:T(8,128)(2,1)S(1)}, bf16[64,2048]{1,0:T(8,128)(2,1)S(1)}, u32[]{:S(2)}, u32[]{:S(2)}) collective-permute-start(bf16[64,2048]{1,0:T(8,128)(2,1)S(1)} %collective-permute-done.20.refs_5_), channel_id=1, source_target_pairs={{0,12},{1,13},{16,28},{17,29},{32,44},{33,45},{48,60},{49,61},{2,1... | collective-permute-start | bytes 786440 | tf_op jit(solution)/shard_map/b2/ppermute | solution.py:37
  81.9 9.5 %collective-permute-start.24 = (bf16[512,512]{1,0:T(8,128)(2,1)S(1)}, bf16[512,512]{1,0:T(8,128)(2,1)S(1)}, u32[]{:S(2)}, u32[]{:S(2)}) collective-permute-start(bf16[512,512]{1,0:T(8,128)(2,1)S(1)} %get-tuple-element.76.own_ref), channel_id=1, source_target_pairs={{0,1},{1,0},{16,17},{17,16},{32,33},{33,32},{48,49},{49,48},{2,3},... | collective-permute-start | bytes 1572872 | tf_op jit(solution)/shard_map/swap_near/ppermute | solution.py:37
  90.4 2.6 %collective-permute-start.23 = (bf16[512,512]{1,0:T(8,128)(2,1)S(1)}, bf16[512,512]{1,0:T(8,128)(2,1)S(1)}, u32[]{:S(2)}, u32[]{:S(2)}) collective-permute-start(bf16[512,512]{1,0:T(8,128)(2,1)S(1)} %far.1.own_ref), channel_id=1, source_target_pairs={{0,1},{1,0},{16,17},{17,16},{32,33},{33,32},{48,49},{49,48},{2,3},... | collective-permute-start | bytes 1572872 | tf_op jit(solution)/shard_map/swap_far/ppermute | solution.py:37

commit v4 on v3

--- a/solution.py
+++ b/solution.py
@@ -236,22 +236,22 @@
     out_ref[...] = (prod * scale).astype(out_ref.dtype)
 
 
-def place_trains(y, trains, left_ref):
+def place_trains(y, trains, left_ref, first=0):
     count = trains[0].shape[0]
     moves = []
     for s in range(NY):
-        at = pl.multiple_of(lax.rem(y + s, NY) * count, count)
+        at = pl.multiple_of(first + lax.rem(y + s, NY) * count, count)
         moves.append((trains[s], left_ref.at[pl.ds(at, count)]))
     return moves
 
 
 def near_kernel(scale, pos_ref, *refs):
-    queries, trains = refs[:NX], refs[NX : NX + NY]
-    out_ref, right_ref, left_ref, sems = refs[NX + NY :]
-    x = pos_ref[0]
+    queries, trains, firsts = refs[:NX], refs[NX : NX + NY], refs[NX + NY : NX + 2 * NY]
+    out_ref, right_ref, left_ref, sems = refs[NX + 2 * NY :]
+    x, y = pos_ref[0], pos_ref[2]
     layers = 2
     rows = queries[0].shape[1] // layers
-    moves = place_trains(pos_ref[2], trains, left_ref)
+    moves = place_trains(y, trains, left_ref) + place_trains(y, firsts, left_ref, NY * trains[0].shape[0])
     for s in range(NX):
         for layer in range(layers):
             at = pl.multiple_of(layer * NX * rows + lax.rem(x + s, NX) * rows, rows)
@@ -260,77 +260,71 @@
     dot_terms(scale, left_ref, right_ref, out_ref)
 
 
-def score_near(pos, queries, trains, scale):
+def score_near(pos, queries, trains, firsts, scale):
     count, entries = trains[0].shape
-    total = NY * count
+    total = NY * (count + firsts[0].shape[0])
     columns = queries[0].shape[0]
     return pl.pallas_call(
         functools.partial(near_kernel, scale),
-        in_specs=[scalars()] + [whole()] * (NX + NY),
+        in_specs=[scalars()] + [whole()] * (NX + 2 * NY),
         out_specs=[whole(), whole()],
         out_shape=[
             jax.ShapeDtypeStruct((total, columns), jnp.bfloat16),
             jax.ShapeDtypeStruct((columns, entries), jnp.bfloat16),
         ],
-        scratch_shapes=[pltpu.VMEM((total, entries), jnp.bfloat16), pltpu.SemaphoreType.DMA((2 * NX + NY,))],
-        compiler_params=pltpu.CompilerParams(vmem_limit_bytes=16 * MIB),
+        scratch_shapes=[pltpu.VMEM((total, entries), jnp.bfloat16), pltpu.SemaphoreType.DMA((2 * NX + 2 * NY,))],
+        compiler_params=pltpu.CompilerParams(vmem_limit_bytes=24 * MIB),
         cost_estimate=FREE,
         name="near",
-    )(pos, *queries, *trains)
+    )(pos, *queries, *trains, *firsts)
 
 
 def far_kernel(scale, pos_ref, right_ref, *refs):
-    firsts, seconds, (out_ref, left_ref, sems) = refs[:NY], refs[NY : 2 * NY], refs[2 * NY :]
-    y = pos_ref[2]
-    count = firsts[0].shape[0]
-    moves = []
-    for s in range(NY):
-        at = lax.rem(y + s, NY) * 2 * count
-        moves.append((firsts[s], left_ref.at[pl.ds(pl.multiple_of(at, count), count)]))
-        moves.append((seconds[s], left_ref.at[pl.ds(pl.multiple_of(at + count, count), count)]))
-    move_all(moves, sems)
+    trains, (out_ref, left_ref, sems) = refs[:NY], refs[NY:]
+    move_all(place_trains(pos_ref[2], trains, left_ref), sems)
     dot_terms(scale, left_ref, right_ref, out_ref)
 
 
-def score_far(pos, packed, firsts, seconds, scale):
-    count, entries = firsts[0].shape
-    total = 2 * NY * count
+def score_far(pos, packed, trains, scale):
+    count, entries = trains[0].shape
+    total = NY * count
     columns = packed.shape[0]
     return pl.pallas_call(
         functools.partial(far_kernel, scale),
-        in_specs=[scalars()] + [whole()] * (1 + 2 * NY),
+        in_specs=[scalars()] + [whole()] * (1 + NY),
         out_specs=whole(),
         out_shape=jax.ShapeDtypeStruct((total, columns), jnp.bfloat16),
-        scratch_shapes=[pltpu.VMEM((total, entries), jnp.bfloat16), pltpu.SemaphoreType.DMA((2 * NY,))],
+        scratch_shapes=[pltpu.VMEM((total, entries), jnp.bfloat16), pltpu.SemaphoreType.DMA((NY,))],
         compiler_params=pltpu.CompilerParams(vmem_limit_bytes=16 * MIB),
-        cost_estimate=FREE,
+        cost_estimate=pl.CostEstimate(flops=20 * 10**9, bytes_accessed=0, transcendentals=0),
         name="far",
-    )(pos, packed, *firsts, *seconds)
-
-
-def add_kernel(places_ref, own_ref, other_ref, *refs):
+    )(pos, packed, *trains)
+
+
+def add_kernel(sizes, places_ref, own_ref, other_ref, *refs):
     out_ref, sum_ref, sems = refs[-3:]
-    count = own_ref.shape[0] // NY
     copies = []
-    for s in range(NY):
-        rows = pl.ds(s * count, count)
+    first = 0
+    for i, size in enumerate(sizes):
+        rows = pl.ds(first, size)
+        first += size
         sum_ref[rows, :] = own_ref[rows, :].astype(jnp.float32) + other_ref[rows, :].astype(jnp.float32)
-        at = pl.multiple_of(places_ref[s] * count, count)
-        copies.append(pltpu.make_async_copy(sum_ref.at[rows], out_ref.at[pl.ds(at, count)], sems.at[s]))
+        at = pl.multiple_of(places_ref[i] * 16, 16)
+        copies.append(pltpu.make_async_copy(sum_ref.at[rows], out_ref.at[pl.ds(at, size)], sems.at[i]))
         copies[-1].start()
     for copy in copies:
         copy.wait()
 
 
-def add_terms(places, own, other, total, held=None):
+def add_terms(places, sizes, own, other, total, held=None):
     columns = own.shape[1]
     extra = [] if held is None else [held]
     return pl.pallas_call(
-        add_kernel,
+        functools.partial(add_kernel, sizes),
         in_specs=[scalars(), whole(), whole()] + [anywhere()] * len(extra),
         out_specs=anywhere(),
         out_shape=jax.ShapeDtypeStruct((total, columns), jnp.float32),
-        scratch_shapes=[pltpu.VMEM(own.shape, jnp.float32), pltpu.SemaphoreType.DMA((NY,))],
+        scratch_shapes=[pltpu.VMEM(own.shape, jnp.float32), pltpu.SemaphoreType.DMA((len(sizes),))],
         input_output_aliases={} if held is None else {3: 0},
         compiler_params=pltpu.CompilerParams(vmem_limit_bytes=16 * MIB),
         cost_estimate=FREE,
@@ -348,7 +342,7 @@
     precs = [precond, send(precond, "p_up", dz=-1), send(precond, "p_far", split=2), send(precond, "p_down", dz=1)]
     (query_grad,) = form_grads(query_acts[0], query_backs[0])
     grads = [query_grad, send(query_grad, "g_up", dx=-1), send(query_grad, "g_far", dx=2), send(query_grad, "g_down", dx=1)]
-    train_acts, query_grad = after(train_acts, query_grad)
+    train_acts, query_grad, precs[1] = after(train_acts, query_grad, precs[1])
     train_grad, first, second = form_grads(train_acts, train_backs, 2)
     train_grad, first, second, *got = after(train_grad, first, second, *grads, *precs)
     near = [train_grad, send(train_grad, "n_up", dy=-1), None, send(train_grad, "n_down", dy=1)]
@@ -356,14 +350,14 @@
     parts = [part] + [send(part, "low%d" % s, dzl=-s) for s in (1, 2, 3)]
     near[1], near[3] = after(near[1], near[3])
     near[2] = send(near[1], "n_two", dy=-1)
-    first, second, parts[1], parts[2] = after(first, second, parts[1], parts[2])
+    first, second, *parts = after(first, second, *parts)
     first = send(first, "far1", dz=NZL)
     second = send(second, "far2", dz=NZL)
     mine = join_queries(pos, parts)
     queries = [mine, send(mine, "r_up", dx=-1), None, send(mine, "r_down", dx=1)]
     later = pass_on(pos, first)
-    queries[1], queries[3], near[2], first, later = after(queries[1], queries[3], near[2], first, later)
-    firsts = [first, send(first, "a1", dy=-1), None, send(first, "a3", dy=1)]
+    queries[1], queries[3], near[2], again, later = after(queries[1], queries[3], near[2], first, later)
+    firsts = [first, send(again, "a1", dy=-1), None, send(first, "a3", dy=1)]
     queries[2] = send(queries[1], "r_next", dx=-1)
     second, firsts[1], firsts[3] = after(second, firsts[1], firsts[3])
     firsts[2] = send(firsts[3], "a2", dy=1)
@@ -371,13 +365,17 @@
     seconds[2] = send(seconds[1], "b2", dy=-1)
     later, *firsts = after(later, *firsts)
     last = later
-    near_terms, packed = score_near(last, queries, near, scale)
-    near_other = send(near_terms, "swap_near", dcore=1)
-    far_terms = score_far(pos, packed, firsts, seconds, scale)
-    far_other = send(far_terms, "swap_far", dcore=1)
+    terms, packed = score_near(last, queries, near, firsts, scale)
+    other = send(terms, "swap", dcore=1)
+    last_terms = score_far(pos, packed, seconds, scale)
+    last_other = send(last_terms, "swap_last", dcore=1)
+    count, cut, rest = near[0].shape[0], firsts[0].shape[0], seconds[0].shape[0]
     ys = jnp.arange(NY, dtype=jnp.int32) * NZH
-    out = add_terms((ys + zh).astype(jnp.int32), near_terms, near_other, total)
-    return add_terms((ys + 1 - zh).astype(jnp.int32), far_terms, far_other, total, out)
+    near_rows, far_rows = (ys + zh) * (count // 16), (ys + 1 - zh) * (count // 16)
+    places = jnp.concatenate([near_rows, far_rows]).astype(jnp.int32)
+    out = add_terms(places, (count,) * NY + (cut,) * NY, terms, other, total)
+    places = (far_rows + cut // 16).astype(jnp.int32)
+    return add_terms(places, (rest,) * NY, last_terms, last_other, total, out)
 
 
 def solution(mesh):

time: 94.9 us -> 94 us (level)
  the two profiles are of different devices: /device:TPU:1 before, /device:TPU:65 now
where the time goes in v4:
time: 94 us; the launch traced here: 93.9 us
  starting transfers between devices  45.6 us (49%)
  waiting for transfers between devices  26.2 us (28%)
  Pallas kernels  21.5 us (23%)
    ppermute x25, starting transfers between devices, send(): return lax.ppermute(value, AXES, pairs(move))  45.6 us
    ppermute x25, waiting for transfers between devices, send(): return lax.ppermute(value, AXES, pairs(move))  26.2 us
    pallas_call x2, Pallas kernels, form_grads(): pl.pallas_call(functools.partial(form_kernel, block), in_specs=[anywhere(...  9.47 us
    pallas_call x2, Pallas kernels, add_terms(): pl.pallas_call(functools.partial(add_kernel, sizes), in_specs=[scalars(),...  3.14 us
    pallas_call x1, Pallas kernels, score_near(): pl.pallas_call(functools.partial(near_kernel, scale), in_specs=[scalars()...  3.1 us
    pallas_call x1, Pallas kernels, apply_rows(): pl.pallas_call(apply_kernel, in_specs=[scalars()] + [whole()] * (NX + NZL...  1.89 us
  transfers between devices with their start and end apart: 25, of which 8 were waited for; matrix products, arithmetic and copies ran while one was open for 0% of the time, Pallas kernels for 19%

profile of v4, /device:TPU:65, one launch (start us, length us, event | category | flops | bytes accessed | tf_op | source)
XLA Modules:
  0.0 93.9 jit_solution(18034195758908896959)
XLA Ops:
  0.0 0.0 collective-permute-start
  0.0 4.2 %collective-permute-start.4 = (bf16[2,64,1024]{2,1,0:T(8,128)(2,1)}, bf16[2,64,1024]{2,1,0:T(8,128)(2,1)S(1)}, u32[]{:S(2)}, u32[]{:S(2)}) collective-permute-start(bf16[2,64,1024]{2,1,0:T(8,128)(2,1)} %refs_4_), channel_id=1, source_target_pairs={{0,34},{1,33},{16,50},{17,49},{32,0},{33,3},{48,16},{49,19},{2,32}... | collective-permute-start | bytes 786440 | tf_op jit(solution)/shard_map/p_far/ppermute | solution.py:37
  4.2 1.5 %collective-permute-start.5 = (bf16[2,64,1024]{2,1,0:T(8,128)(2,1)}, bf16[2,64,1024]{2,1,0:T(8,128)(2,1)S(1)}, u32[]{:S(2)}, u32[]{:S(2)}) collective-permute-start(bf16[2,64,1024]{2,1,0:T(8,128)(2,1)} %refs_4_), channel_id=1, source_target_pairs={{0,16},{1,17},{16,32},{17,33},{32,48},{33,49},{48,2},{49,3},{2,18}... | collective-permute-start | bytes 786440 | tf_op jit(solution)/shard_map/p_down/ppermute | solution.py:37
  5.7 3.1 %form.2.refs_0_ = bf16[32,2048]{1,0:T(8,128)(2,1)} custom-call(bf16[32,2,32,256]{3,2,1,0:T(8,128)(2,1)} %bitcast.10, bf16[32,2,32,256]{3,2,1,0:T(8,128)(2,1)} %bitcast.11), custom_call_target="tpu_custom_call" | custom-call | tf_op jit(solution)/shard_map/form/pallas_call | solution.py:146
  8.8 2.6 %collective-permute-start.1 = (bf16[32,2048]{1,0:T(8,128)(2,1)}, bf16[32,2048]{1,0:T(8,128)(2,1)S(1)}, u32[]{:S(2)}, u32[]{:S(2)}) collective-permute-start(bf16[32,2048]{1,0:T(8,128)(2,1)} %form.2.refs_0_), channel_id=1, source_target_pairs={{0,192},{1,193},{16,208},{17,209},{32,224},{33,225},{48,240},{49,2... | collective-permute-start | bytes 393224 | tf_op jit(solution)/shard_map/g_up/ppermute | solution.py:37
  11.4 0.5 collective-permute-start.2
  11.9 0.0 collective-permute-done.refs_5_
  11.9 0.6 collective-permute-start.3
  12.5 0.1 pad_add_fusion.pos_ref
  12.6 6.3 %form.3 = (bf16[128,2048]{1,0:T(8,128)(2,1)}, bf16[64,2048]{1,0:T(8,128)(2,1)}, bf16[64,2048]{1,0:T(8,128)(2,1)}) custom-call(bf16[128,2,32,256]{3,2,1,0:T(8,128)(2,1)} %acts_hbm, bf16[128,2,32,256]{3,2,1,0:T(8,128)(2,1)} %backs_hbm.1), custom_call_target="tpu_custom_call" | custom-call | tf_op jit(solution)/shard_map/form/pallas_call | solution.py:146
  18.9 0.0 collective-permute-done.1.refs_1_
  18.9 0.0 collective-permute-done.2.refs_2_
  18.9 2.3 %collective-permute-done.3.refs_3_ = bf16[32,2048]{1,0:T(8,128)(2,1)S(1)} collective-permute-done((bf16[32,2048]{1,0:T(8,128)(2,1)}, bf16[32,2048]{1,0:T(8,128)(2,1)S(1)}, u32[]{:S(2)}, u32[]{:S(2)}) %collective-permute-start.3) | collective-permute-done | bytes 131104 | tf_op jit(solution)/shard_map/g_down/ppermute | solution.py:37
  21.3 0.0 collective-permute-done.4.refs_6_
  21.3 0.0 collective-permute-done.5.refs_7_
  21.3 0.0 copy-done
  21.3 0.0 copy-done.2
  21.3 1.9 %apply.1.refs_0_ = bf16[128,512]{1,0:T(8,128)(2,1)S(1)} custom-call(s32[4]{0:T(128)S(1)} %pad_add_fusion.pos_ref, bf16[32,2048]{1,0:T(8,128)(2,1)S(1)} %copy-done, bf16[32,2048]{1,0:T(8,128)(2,1)S(1)} %collective-permute-done.1.refs_1_, bf16[32,2048]{1,0:T(8,128)(2,1)S(1)} %collective-permute-done.2.refs_2_, ...), custom_call_target="tpu_custom_call" | custom-call | tf_op jit(solution)/shard_map/apply/pallas_call | solution.py:191
  23.2 0.1 collective-permute-start.6
  23.3 2.8 %collective-permute-start.7 = (bf16[128,512]{1,0:T(8,128)(2,1)S(1)}, bf16[128,512]{1,0:T(8,128)(2,1)S(1)}, u32[]{:S(2)}, u32[]{:S(2)}) collective-permute-start(bf16[128,512]{1,0:T(8,128)(2,1)S(1)} %apply.1.refs_0_), channel_id=1, source_target_pairs={{0,32},{1,33},{16,48},{17,49},{32,0},{33,1},{48,16},{49,17},{2,34}... | collective-permute-start | bytes 393224 | tf_op jit(solution)/shard_map/low2/ppermute | solution.py:37
  26.1 0.0 collective-permute-start.8
  26.1 2.7 %collective-permute-start.11 = (bf16[128,2048]{1,0:T(8,128)(2,1)}, bf16[128,2048]{1,0:T(8,128)(2,1)S(1)}, u32[]{:S(2)}, u32[]{:S(2)}) collective-permute-start(bf16[128,2048]{1,0:T(8,128)(2,1)} %get-tuple-element.63.refs_4_), channel_id=1, source_target_pairs={{0,12},{1,13},{16,28},{17,29},{32,44},{33,45},{48,60},{49,61},{2,1... | collective-permute-start | bytes 1572872 | tf_op jit(solution)/shard_map/n_up/ppermute | solution.py:37
  28.8 0.0 collective-permute-start.12
  28.9 0.0 collective-permute-done.6.refs_1_
  28.9 5.5 %collective-permute-done.7.refs_2_ = bf16[128,512]{1,0:T(8,128)(2,1)S(1)} collective-permute-done((bf16[128,512]{1,0:T(8,128)(2,1)S(1)}, bf16[128,512]{1,0:T(8,128)(2,1)S(1)}, u32[]{:S(2)}, u32[]{:S(2)}) %collective-permute-start.7) | collective-permute-done | bytes 131104 | tf_op jit(solution)/shard_map/low2/ppermute | solution.py:37
  34.4 3.8 %collective-permute-done.8.refs_3_ = bf16[128,512]{1,0:T(8,128)(2,1)S(1)} collective-permute-done((bf16[128,512]{1,0:T(8,128)(2,1)S(1)}, bf16[128,512]{1,0:T(8,128)(2,1)S(1)}, u32[]{:S(2)}, u32[]{:S(2)}) %collective-permute-start.8) | collective-permute-done | bytes 131104 | tf_op jit(solution)/shard_map/low3/ppermute | solution.py:37
  38.2 1.6 %collective-permute-start.14 = (bf16[64,2048]{1,0:T(8,128)(2,1)}, bf16[64,2048]{1,0:T(8,128)(2,1)S(1)}, u32[]{:S(2)}, u32[]{:S(2)}) collective-permute-start(bf16[64,2048]{1,0:T(8,128)(2,1)} %get-tuple-element.65), channel_id=1, source_target_pairs={{0,2},{1,3},{16,18},{17,19},{32,34},{33,35},{48,50},{49,51},{2,0},... | collective-permute-start | bytes 786440 | tf_op jit(solution)/shard_map/far1/ppermute | solution.py:37
  39.8 1.4 %join.1 = bf16[4,128,512]{2,1,0:T(8,128)(2,1)S(1)} custom-call(s32[4]{0:T(128)S(1)} %pad_add_fusion.pos_ref, bf16[128,512]{1,0:T(8,128)(2,1)S(1)} %apply.1.refs_0_, bf16[128,512]{1,0:T(8,128)(2,1)S(1)} %collective-permute-done.6.refs_1_, bf16[128,512]{1,0:T(8,128)(2,1)S(1)} %collective-permute-done.7.refs_2_, bf16[128,512]{1,0:T(8,128)(2,1)S(1)} %collective-permute-done.8.refs_3_), custom_call_target="tpu_custom_call" | custom-call | flops 20000000000 | tf_op jit(solution)/shard_map/join/pallas_call | solution.py:221
  41.2 0.0 copy-start.1
  41.2 1.5 %collective-permute-start.10 = (bf16[512,512]{1,0:T(8,128)(2,1)S(1)}, bf16[512,512]{1,0:T(8,128)(2,1)S(1)}, u32[]{:S(2)}, u32[]{:S(2)}) collective-permute-start(bf16[512,512]{1,0:T(8,128)(2,1)S(1)} %bitcast.7), channel_id=1, source_target_pairs={{0,64},{1,65},{16,80},{17,81},{32,96},{33,97},{48,112},{49,113},{2... | collective-permute-start | bytes 1572872 | tf_op jit(solution)/shard_map/r_down/ppermute | solution.py:37
  42.7 1.5 %collective-permute-start.9 = (bf16[512,512]{1,0:T(8,128)(2,1)S(1)}, bf16[512,512]{1,0:T(8,128)(2,1)S(1)}, u32[]{:S(2)}, u32[]{:S(2)}) collective-permute-start(bf16[512,512]{1,0:T(8,128)(2,1)S(1)} %bitcast.8), channel_id=1, source_target_pairs={{0,192},{1,193},{16,208},{17,209},{32,224},{33,225},{48,240},{49,2... | collective-permute-start | bytes 1572872 | tf_op jit(solution)/shard_map/r_up/ppermute | solution.py:37
  44.1 0.0 collective-permute-done.11.refs_5_
  44.1 0.0 collective-permute-done.12.refs_7_
  44.1 2.7 %collective-permute-start.13 = (bf16[128,2048]{1,0:T(8,128)(2,1)S(1)}, bf16[128,2048]{1,0:T(8,128)(2,1)S(1)}, u32[]{:S(2)}, u32[]{:S(2)}) collective-permute-start(bf16[128,2048]{1,0:T(8,128)(2,1)S(1)} %collective-permute-done.11.refs_5_), channel_id=1, source_target_pairs={{0,12},{1,13},{16,28},{17,29},{32,44},{33,45},{48,60},{49,61},{2,1... | collective-permute-start | bytes 1572872 | tf_op jit(solution)/shard_map/n_two/ppermute | solution.py:37
  46.9 3.8 %collective-permute-start.15 = (bf16[64,2048]{1,0:T(8,128)(2,1)S(1)}, bf16[64,2048]{1,0:T(8,128)(2,1)S(1)}, u32[]{:S(2)}, u32[]{:S(2)}) collective-permute-start(bf16[64,2048]{1,0:T(8,128)(2,1)S(1)} %copy-done.3), channel_id=1, source_target_pairs={{0,2},{1,3},{16,18},{17,19},{32,34},{33,35},{48,50},{49,51},{2,0},... | collective-permute-start | bytes 786440 | tf_op jit(solution)/shard_map/far2/ppermute | solution.py:37
  50.6 4.7 %collective-permute-done.14._.refs_8_ = bf16[64,2048]{1,0:T(8,128)(2,1)S(1)} collective-permute-done((bf16[64,2048]{1,0:T(8,128)(2,1)}, bf16[64,2048]{1,0:T(8,128)(2,1)S(1)}, u32[]{:S(2)}, u32[]{:S(2)}) %collective-permute-start.14) | collective-permute-done | bytes 262176 | tf_op jit(solution)/shard_map/far1/ppermute | solution.py:37
  55.4 6.7 %collective-permute-start.17 = (bf16[64,2048]{1,0:T(8,128)(2,1)S(1)}, bf16[64,2048]{1,0:T(8,128)(2,1)S(1)}, u32[]{:S(2)}, u32[]{:S(2)}) collective-permute-start(bf16[64,2048]{1,0:T(8,128)(2,1)S(1)} %collective-permute-done.14._.refs_8_), channel_id=1, source_target_pairs={{0,4},{1,5},{16,20},{17,21},{32,36},{33,37},{48,52},{49,53},{2,6},... | collective-permute-start | bytes 786440 | tf_op jit(solution)/shard_map/a3/ppermute | solution.py:37
  62.1 1.1 %pass.1.pos_ref = s32[4]{0:T(128)S(1)} custom-call(s32[4]{0:T(128)S(1)} %pad_add_fusion.pos_ref, bf16[64,2048]{1,0:T(8,128)(2,1)S(1)} %collective-permute-done.14._.refs_8_), custom_call_target="tpu_custom_call" | custom-call | flops 4000000000 | tf_op jit(solution)/shard_map/pass/pallas_call | solution.py:49
  63.2 0.0 collective-permute-done.10.refs_3_
  63.2 0.0 collective-permute-done.9.refs_1_
  63.2 0.0 collective-permute-done.13.refs_6_
  63.2 1.5 %collective-permute-start.16 = (bf16[64,2048]{1,0:T(8,128)(2,1)S(1)}, bf16[64,2048]{1,0:T(8,128)(2,1)S(1)}, u32[]{:S(2)}, u32[]{:S(2)}) collective-permute-start(bf16[64,2048]{1,0:T(8,128)(2,1)S(1)} %collective-permute-done.14._.refs_8_), channel_id=1, source_target_pairs={{0,12},{1,13},{16,28},{17,29},{32,44},{33,45},{48,60},{49,61},{2,1... | collective-permute-start | bytes 786440 | tf_op jit(solution)/shard_map/a1/ppermute | solution.py:37
  64.8 0.0 collective-permute-start.19
  64.8 0.0 collective-permute-done.15.refs_0_
  64.8 4.9 %collective-permute-done.17.refs_11_ = bf16[64,2048]{1,0:T(8,128)(2,1)S(1)} collective-permute-done((bf16[64,2048]{1,0:T(8,128)(2,1)S(1)}, bf16[64,2048]{1,0:T(8,128)(2,1)S(1)}, u32[]{:S(2)}, u32[]{:S(2)}) %collective-permute-start.17) | collective-permute-done | bytes 262176 | tf_op jit(solution)/shard_map/a3/ppermute | solution.py:37
  69.6 0.6 collective-permute-done.16.refs_9_
  70.3 3.0 %collective-permute-start.20 = (bf16[64,2048]{1,0:T(8,128)(2,1)S(1)}, bf16[64,2048]{1,0:T(8,128)(2,1)S(1)}, u32[]{:S(2)}, u32[]{:S(2)}) collective-permute-start(bf16[64,2048]{1,0:T(8,128)(2,1)S(1)} %collective-permute-done.15.refs_0_), channel_id=1, source_target_pairs={{0,12},{1,13},{16,28},{17,29},{32,44},{33,45},{48,60},{49,61},{2,1... | collective-permute-start | bytes 786440 | tf_op jit(solution)/shard_map/b1/ppermute | solution.py:37
  73.2 0.0 collective-permute-start.18
  73.2 0.0 collective-permute-start.22
  73.2 4.1 %collective-permute-done.20.refs_1_ = bf16[64,2048]{1,0:T(8,128)(2,1)S(1)} collective-permute-done((bf16[64,2048]{1,0:T(8,128)(2,1)S(1)}, bf16[64,2048]{1,0:T(8,128)(2,1)S(1)}, u32[]{:S(2)}, u32[]{:S(2)}) %collective-permute-start.20) | collective-permute-done | bytes 262176 | tf_op jit(solution)/shard_map/b1/ppermute | solution.py:37
  77.4 3.4 %collective-permute-start.21 = (bf16[64,2048]{1,0:T(8,128)(2,1)S(1)}, bf16[64,2048]{1,0:T(8,128)(2,1)S(1)}, u32[]{:S(2)}, u32[]{:S(2)}) collective-permute-start(bf16[64,2048]{1,0:T(8,128)(2,1)S(1)} %collective-permute-done.20.refs_1_), channel_id=1, source_target_pairs={{0,12},{1,13},{16,28},{17,29},{32,44},{33,45},{48,60},{49,61},{2,1... | collective-permute-start | bytes 786440 | tf_op jit(solution)/shard_map/b2/ppermute | solution.py:37
  80.8 0.0 collective-permute-done.18.refs_10_
  80.8 0.0 collective-permute-done.19.refs_2_
  80.8 3.1 %near.1 = (bf16[768,512]{1,0:T(8,128)(2,1)S(1)}, bf16[512,2048]{1,0:T(8,128)(2,1)S(1)}) custom-call(s32[4]{0:T(128)S(1)} %pass.1.pos_ref, bf16[512,512]{1,0:T(8,128)(2,1)S(1)} %bitcast.9, bf16[512,512]{1,0:T(8,128)(2,1)S(1)} %collective-permute-done.9.refs_1_, bf16[512,512]{1,0:T(8,128)(2,1)S(1)} %collective-permute-done.19.refs_2_, ...), custom_call_target="tpu_custom_call" | custom-call | tf_op jit(solution)/shard_map/near/pallas_call | solution.py:267
  83.9 4.7 %collective-permute-start.24 = (bf16[768,512]{1,0:T(8,128)(2,1)S(1)}, bf16[768,512]{1,0:T(8,128)(2,1)S(1)}, u32[]{:S(2)}, u32[]{:S(2)}) collective-permute-start(bf16[768,512]{1,0:T(8,128)(2,1)S(1)} %get-tuple-element.82.own_ref), channel_id=1, source_target_pairs={{0,1},{1,0},{16,17},{17,16},{32,33},{33,32},{48,49},{49,48},{2,3},... | collective-permute-start | bytes 2359304 | tf_op jit(solution)/shard_map/swap/ppermute | solution.py:37
  88.6 0.0 collective-permute-done.22.refs_3_
  88.6 0.0 collective-permute-done.21.refs_2_
  88.6 1.4 %far.1.own_ref = bf16[256,512]{1,0:T(8,128)(2,1)S(1)} custom-call(s32[4]{0:T(128)S(1)} %pad_add_fusion.pos_ref, bf16[512,2048]{1,0:T(8,128)(2,1)S(1)} %get-tuple-element.80.right_ref, bf16[64,2048]{1,0:T(8,128)(2,1)S(1)} %collective-permute-done.15.refs_0_, bf16[64,2048]{1,0:T(8,128)(2,1)S(1)} %collective-permute-done.20.refs_1_, ...), custom_call_target="tpu_custom_call" | custom-call | flops 20000000000 | tf_op jit(solution)/shard_map/far/pallas_call | solution.py:292
  90.0 0.3 collective-permute-start.23
  90.3 0.1 pad_add_fusion.1.places_ref
  90.4 0.1 collective-permute-done.24.other_ref
  90.5 1.8 %add.39.refs_0_ = f32[1024,512]{1,0:T(8,128)} custom-call(s32[8]{0:T(128)S(1)} %pad_add_fusion.1.places_ref, bf16[768,512]{1,0:T(8,128)(2,1)S(1)} %get-tuple-element.82.own_ref, bf16[768,512]{1,0:T(8,128)(2,1)S(1)} %collective-permute-done.24.other_ref), custom_call_target="tpu_custom_call" | custom-call | tf_op jit(solution)/shard_map/add/pallas_call | solution.py:322
  92.3 0.0 collective-permute-done.23.other_ref
  92.3 1.4 %add.40 = f32[1024,512]{1,0:T(8,128)} custom-call(s32[4]{0:T(128)S(1)} %broadcast_add_fusion.places_ref, bf16[256,512]{1,0:T(8,128)(2,1)S(1)} %far.1.own_ref, bf16[256,512]{1,0:T(8,128)(2,1)S(1)} %collective-permute-done.23.other_ref, f32[1024,512]{1,0:T(8,128)} %add.39.refs_0_), custom_call_target="tpu_custom_call", output_to_operand_aliasing={{}: (3, {})} | custom-call | tf_op jit(solution)/shard_map/add/pallas_call | solution.py:322
  (7 shorter events, 0.0 us)
Async XLA Ops:
  0.0 11.9 %collective-permute-start = (bf16[2,64,1024]{2,1,0:T(8,128)(2,1)}, bf16[2,64,1024]{2,1,0:T(8,128)(2,1)S(1)}, u32[]{:S(2)}, u32[]{:S(2)}) collective-permute-start(bf16[2,64,1024]{2,1,0:T(8,128)(2,1)} %refs_4_), channel_id=1, source_target_pairs={{0,50},{1,51},{16,0},{17,1},{32,16},{33,17},{48,32},{49,33},{2,48}... | collective-permute-start | bytes 786440 | tf_op jit(solution)/shard_map/p_up/ppermute | solution.py:37
  0.0 21.3 %collective-permute-start.4 = (bf16[2,64,1024]{2,1,0:T(8,128)(2,1)}, bf16[2,64,1024]{2,1,0:T(8,128)(2,1)S(1)}, u32[]{:S(2)}, u32[]{:S(2)}) collective-permute-start(bf16[2,64,1024]{2,1,0:T(8,128)(2,1)} %refs_4_), channel_id=1, source_target_pairs={{0,34},{1,33},{16,50},{17,49},{32,0},{33,3},{48,16},{49,19},{2,32}... | collective-permute-start | bytes 786440 | tf_op jit(solution)/shard_map/p_far/ppermute | solution.py:37
  4.2 17.1 %collective-permute-start.5 = (bf16[2,64,1024]{2,1,0:T(8,128)(2,1)}, bf16[2,64,1024]{2,1,0:T(8,128)(2,1)S(1)}, u32[]{:S(2)}, u32[]{:S(2)}) collective-permute-start(bf16[2,64,1024]{2,1,0:T(8,128)(2,1)} %refs_4_), channel_id=1, source_target_pairs={{0,16},{1,17},{16,32},{17,33},{32,48},{33,49},{48,2},{49,3},{2,18}... | collective-permute-start | bytes 786440 | tf_op jit(solution)/shard_map/p_down/ppermute | solution.py:37
  8.8 10.1 %collective-permute-start.1 = (bf16[32,2048]{1,0:T(8,128)(2,1)}, bf16[32,2048]{1,0:T(8,128)(2,1)S(1)}, u32[]{:S(2)}, u32[]{:S(2)}) collective-permute-start(bf16[32,2048]{1,0:T(8,128)(2,1)} %form.2.refs_0_), channel_id=1, source_target_pairs={{0,192},{1,193},{16,208},{17,209},{32,224},{33,225},{48,240},{49,2... | collective-permute-start | bytes 393224 | tf_op jit(solution)/shard_map/g_up/ppermute | solution.py:37
  11.4 7.6 %collective-permute-start.2 = (bf16[32,2048]{1,0:T(8,128)(2,1)}, bf16[32,2048]{1,0:T(8,128)(2,1)S(1)}, u32[]{:S(2)}, u32[]{:S(2)}) collective-permute-start(bf16[32,2048]{1,0:T(8,128)(2,1)} %form.2.refs_0_), channel_id=1, source_target_pairs={{0,128},{1,129},{16,144},{17,145},{32,160},{33,161},{48,176},{49,1... | collective-permute-start | bytes 393224 | tf_op jit(solution)/shard_map/g_far/ppermute | solution.py:37
  11.9 9.4 %collective-permute-start.3 = (bf16[32,2048]{1,0:T(8,128)(2,1)}, bf16[32,2048]{1,0:T(8,128)(2,1)S(1)}, u32[]{:S(2)}, u32[]{:S(2)}) collective-permute-start(bf16[32,2048]{1,0:T(8,128)(2,1)} %form.2.refs_0_), channel_id=1, source_target_pairs={{0,64},{1,65},{16,80},{17,81},{32,96},{33,97},{48,112},{49,113},{2... | collective-permute-start | bytes 393224 | tf_op jit(solution)/shard_map/g_down/ppermute | solution.py:37
  12.6 8.7 %copy-start = (bf16[32,2048]{1,0:T(8,128)(2,1)S(1)}, bf16[32,2048]{1,0:T(8,128)(2,1)}, u32[]{:S(2)}) copy-start(bf16[32,2048]{1,0:T(8,128)(2,1)} %form.2.refs_0_) | copy-start | bytes 393220
  12.6 8.7 %copy-start.2 = (bf16[2,64,1024]{2,1,0:T(8,128)(2,1)S(1)}, bf16[2,64,1024]{2,1,0:T(8,128)(2,1)}, u32[]{:S(2)}) copy-start(bf16[2,64,1024]{2,1,0:T(8,128)(2,1)} %refs_4_) | copy-start | bytes 786436
  23.2 23.7 %copy-start.3 = (bf16[64,2048]{1,0:T(8,128)(2,1)S(1)}, bf16[64,2048]{1,0:T(8,128)(2,1)}, u32[]{:S(2)}) copy-start(bf16[64,2048]{1,0:T(8,128)(2,1)} %get-tuple-element.67) | copy-start | bytes 786436
  23.2 5.6 %collective-permute-start.6 = (bf16[128,512]{1,0:T(8,128)(2,1)S(1)}, bf16[128,512]{1,0:T(8,128)(2,1)S(1)}, u32[]{:S(2)}, u32[]{:S(2)}) collective-permute-start(bf16[128,512]{1,0:T(8,128)(2,1)S(1)} %apply.1.refs_0_), channel_id=1, source_target_pairs={{0,48},{1,49},{16,0},{17,1},{32,16},{33,17},{48,32},{49,33},{2,50}... | collective-permute-start | bytes 393224 | tf_op jit(solution)/shard_map/low1/ppermute | solution.py:37
  23.3 11.0 %collective-permute-start.7 = (bf16[128,512]{1,0:T(8,128)(2,1)S(1)}, bf16[128,512]{1,0:T(8,128)(2,1)S(1)}, u32[]{:S(2)}, u32[]{:S(2)}) collective-permute-start(bf16[128,512]{1,0:T(8,128)(2,1)S(1)} %apply.1.refs_0_), channel_id=1, source_target_pairs={{0,32},{1,33},{16,48},{17,49},{32,0},{33,1},{48,16},{49,17},{2,34}... | collective-permute-start | bytes 393224 | tf_op jit(solution)/shard_map/low2/ppermute | solution.py:37
  26.1 12.1 %collective-permute-start.8 = (bf16[128,512]{1,0:T(8,128)(2,1)S(1)}, bf16[128,512]{1,0:T(8,128)(2,1)S(1)}, u32[]{:S(2)}, u32[]{:S(2)}) collective-permute-start(bf16[128,512]{1,0:T(8,128)(2,1)S(1)} %apply.1.refs_0_), channel_id=1, source_target_pairs={{0,16},{1,17},{16,32},{17,33},{32,48},{33,49},{48,0},{49,1},{2,18}... | collective-permute-start | bytes 393224 | tf_op jit(solution)/shard_map/low3/ppermute | solution.py:37
  26.1 18.0 %collective-permute-start.11 = (bf16[128,2048]{1,0:T(8,128)(2,1)}, bf16[128,2048]{1,0:T(8,128)(2,1)S(1)}, u32[]{:S(2)}, u32[]{:S(2)}) collective-permute-start(bf16[128,2048]{1,0:T(8,128)(2,1)} %get-tuple-element.63.refs_4_), channel_id=1, source_target_pairs={{0,12},{1,13},{16,28},{17,29},{32,44},{33,45},{48,60},{49,61},{2,1... | collective-permute-start | bytes 1572872 | tf_op jit(solution)/shard_map/n_up/ppermute | solution.py:37
  28.8 15.3 %collective-permute-start.12 = (bf16[128,2048]{1,0:T(8,128)(2,1)}, bf16[128,2048]{1,0:T(8,128)(2,1)S(1)}, u32[]{:S(2)}, u32[]{:S(2)}) collective-permute-start(bf16[128,2048]{1,0:T(8,128)(2,1)} %get-tuple-element.63.refs_4_), channel_id=1, source_target_pairs={{0,4},{1,5},{16,20},{17,21},{32,36},{33,37},{48,52},{49,53},{2,6},... | collective-permute-start | bytes 1572872 | tf_op jit(solution)/shard_map/n_down/ppermute | solution.py:37
  38.2 17.2 %collective-permute-start.14 = (bf16[64,2048]{1,0:T(8,128)(2,1)}, bf16[64,2048]{1,0:T(8,128)(2,1)S(1)}, u32[]{:S(2)}, u32[]{:S(2)}) collective-permute-start(bf16[64,2048]{1,0:T(8,128)(2,1)} %get-tuple-element.65), channel_id=1, source_target_pairs={{0,2},{1,3},{16,18},{17,19},{32,34},{33,35},{48,50},{49,51},{2,0},... | collective-permute-start | bytes 786440 | tf_op jit(solution)/shard_map/far1/ppermute | solution.py:37
  41.2 39.6 %copy-start.1 = (bf16[128,2048]{1,0:T(8,128)(2,1)S(1)}, bf16[128,2048]{1,0:T(8,128)(2,1)}, u32[]{:S(2)}) copy-start(bf16[128,2048]{1,0:T(8,128)(2,1)} %get-tuple-element.63.refs_4_) | copy-start | bytes 1572868
  41.2 22.0 %collective-permute-start.10 = (bf16[512,512]{1,0:T(8,128)(2,1)S(1)}, bf16[512,512]{1,0:T(8,128)(2,1)S(1)}, u32[]{:S(2)}, u32[]{:S(2)}) collective-permute-start(bf16[512,512]{1,0:T(8,128)(2,1)S(1)} %bitcast.7), channel_id=1, source_target_pairs={{0,64},{1,65},{16,80},{17,81},{32,96},{33,97},{48,112},{49,113},{2... | collective-permute-start | bytes 1572872 | tf_op jit(solution)/shard_map/r_down/ppermute | solution.py:37
  42.7 20.5 %collective-permute-start.9 = (bf16[512,512]{1,0:T(8,128)(2,1)S(1)}, bf16[512,512]{1,0:T(8,128)(2,1)S(1)}, u32[]{:S(2)}, u32[]{:S(2)}) collective-permute-start(bf16[512,512]{1,0:T(8,128)(2,1)S(1)} %bitcast.8), channel_id=1, source_target_pairs={{0,192},{1,193},{16,208},{17,209},{32,224},{33,225},{48,240},{49,2... | collective-permute-start | bytes 1572872 | tf_op jit(solution)/shard_map/r_up/ppermute | solution.py:37
  44.1 19.1 %collective-permute-start.13 = (bf16[128,2048]{1,0:T(8,128)(2,1)S(1)}, bf16[128,2048]{1,0:T(8,128)(2,1)S(1)}, u32[]{:S(2)}, u32[]{:S(2)}) collective-permute-start(bf16[128,2048]{1,0:T(8,128)(2,1)S(1)} %collective-permute-done.11.refs_5_), channel_id=1, source_target_pairs={{0,12},{1,13},{16,28},{17,29},{32,44},{33,45},{48,60},{49,61},{2,1... | collective-permute-start | bytes 1572872 | tf_op jit(solution)/shard_map/n_two/ppermute | solution.py:37
  46.9 17.9 %collective-permute-start.15 = (bf16[64,2048]{1,0:T(8,128)(2,1)S(1)}, bf16[64,2048]{1,0:T(8,128)(2,1)S(1)}, u32[]{:S(2)}, u32[]{:S(2)}) collective-permute-start(bf16[64,2048]{1,0:T(8,128)(2,1)S(1)} %copy-done.3), channel_id=1, source_target_pairs={{0,2},{1,3},{16,18},{17,19},{32,34},{33,35},{48,50},{49,51},{2,0},... | collective-permute-start | bytes 786440 | tf_op jit(solution)/shard_map/far2/ppermute | solution.py:37
  55.4 14.3 %collective-permute-start.17 = (bf16[64,2048]{1,0:T(8,128)(2,1)S(1)}, bf16[64,2048]{1,0:T(8,128)(2,1)S(1)}, u32[]{:S(2)}, u32[]{:S(2)}) collective-permute-start(bf16[64,2048]{1,0:T(8,128)(2,1)S(1)} %collective-permute-done.14._.refs_8_), channel_id=1, source_target_pairs={{0,4},{1,5},{16,20},{17,21},{32,36},{33,37},{48,52},{49,53},{2,6},... | collective-permute-start | bytes 786440 | tf_op jit(solution)/shard_map/a3/ppermute | solution.py:37
  63.2 7.0 %collective-permute-start.16 = (bf16[64,2048]{1,0:T(8,128)(2,1)S(1)}, bf16[64,2048]{1,0:T(8,128)(2,1)S(1)}, u32[]{:S(2)}, u32[]{:S(2)}) collective-permute-start(bf16[64,2048]{1,0:T(8,128)(2,1)S(1)} %collective-permute-done.14._.refs_8_), channel_id=1, source_target_pairs={{0,12},{1,13},{16,28},{17,29},{32,44},{33,45},{48,60},{49,61},{2,1... | collective-permute-start | bytes 786440 | tf_op jit(solution)/shard_map/a1/ppermute | solution.py:37
  64.8 16.1 %collective-permute-start.19 = (bf16[512,512]{1,0:T(8,128)(2,1)S(1)}, bf16[512,512]{1,0:T(8,128)(2,1)S(1)}, u32[]{:S(2)}, u32[]{:S(2)}) collective-permute-start(bf16[512,512]{1,0:T(8,128)(2,1)S(1)} %collective-permute-done.9.refs_1_), channel_id=1, source_target_pairs={{0,192},{1,193},{16,208},{17,209},{32,224},{33,225},{48,240},{49,2... | collective-permute-start | bytes 1572872 | tf_op jit(solution)/shard_map/r_next/ppermute | solution.py:37
  70.3 7.1 %collective-permute-start.20 = (bf16[64,2048]{1,0:T(8,128)(2,1)S(1)}, bf16[64,2048]{1,0:T(8,128)(2,1)S(1)}, u32[]{:S(2)}, u32[]{:S(2)}) collective-permute-start(bf16[64,2048]{1,0:T(8,128)(2,1)S(1)} %collective-permute-done.15.refs_0_), channel_id=1, source_target_pairs={{0,12},{1,13},{16,28},{17,29},{32,44},{33,45},{48,60},{49,61},{2,1... | collective-permute-start | bytes 786440 | tf_op jit(solution)/shard_map/b1/ppermute | solution.py:37
  73.2 7.6 %collective-permute-start.18 = (bf16[64,2048]{1,0:T(8,128)(2,1)S(1)}, bf16[64,2048]{1,0:T(8,128)(2,1)S(1)}, u32[]{:S(2)}, u32[]{:S(2)}) collective-permute-start(bf16[64,2048]{1,0:T(8,128)(2,1)S(1)} %collective-permute-done.17.refs_11_), channel_id=1, source_target_pairs={{0,4},{1,5},{16,20},{17,21},{32,36},{33,37},{48,52},{49,53},{2,6},... | collective-permute-start | bytes 786440 | tf_op jit(solution)/shard_map/a2/ppermute | solution.py:37
  73.2 15.4 %collective-permute-start.22 = (bf16[64,2048]{1,0:T(8,128)(2,1)S(1)}, bf16[64,2048]{1,0:T(8,128)(2,1)S(1)}, u32[]{:S(2)}, u32[]{:S(2)}) collective-permute-start(bf16[64,2048]{1,0:T(8,128)(2,1)S(1)} %collective-permute-done.15.refs_0_), channel_id=1, source_target_pairs={{0,4},{1,5},{16,20},{17,21},{32,36},{33,37},{48,52},{49,53},{2,6},... | collective-permute-start | bytes 786440 | tf_op jit(solution)/shard_map/b3/ppermute | solution.py:37
  77.4 11.2 %collective-permute-start.21 = (bf16[64,2048]{1,0:T(8,128)(2,1)S(1)}, bf16[64,2048]{1,0:T(8,128)(2,1)S(1)}, u32[]{:S(2)}, u32[]{:S(2)}) collective-permute-start(bf16[64,2048]{1,0:T(8,128)(2,1)S(1)} %collective-permute-done.20.refs_1_), channel_id=1, source_target_pairs={{0,12},{1,13},{16,28},{17,29},{32,44},{33,45},{48,60},{49,61},{2,1... | collective-permute-start | bytes 786440 | tf_op jit(solution)/shard_map/b2/ppermute | solution.py:37
  83.9 6.6 %collective-permute-start.24 = (bf16[768,512]{1,0:T(8,128)(2,1)S(1)}, bf16[768,512]{1,0:T(8,128)(2,1)S(1)}, u32[]{:S(2)}, u32[]{:S(2)}) collective-permute-start(bf16[768,512]{1,0:T(8,128)(2,1)S(1)} %get-tuple-element.82.own_ref), channel_id=1, source_target_pairs={{0,1},{1,0},{16,17},{17,16},{32,33},{33,32},{48,49},{49,48},{2,3},... | collective-permute-start | bytes 2359304 | tf_op jit(solution)/shard_map/swap/ppermute | solution.py:37
  90.0 2.3 %collective-permute-start.23 = (bf16[256,512]{1,0:T(8,128)(2,1)S(1)}, bf16[256,512]{1,0:T(8,128)(2,1)S(1)}, u32[]{:S(2)}, u32[]{:S(2)}) collective-permute-start(bf16[256,512]{1,0:T(8,128)(2,1)S(1)} %far.1.own_ref), channel_id=1, source_target_pairs={{0,1},{1,0},{16,17},{17,16},{32,33},{33,32},{48,49},{49,48},{2,3},... | collective-permute-start | bytes 786440 | tf_op jit(solution)/shard_map/swap_last/ppermute | solution.py:37

commit v5 on v4

--- a/solution.py
+++ b/solution.py
@@ -40,17 +40,13 @@
 LONG = pl.CostEstimate(flops=4000000000, bytes_accessed=0, transcendentals=0)
 
 
-def pass_kernel(pos_ref, _, out_ref):
-    for i in range(out_ref.shape[0]):
-        out_ref[i] = pos_ref[i]
-
-
 def pass_on(pos, held):
     return pl.pallas_call(
-        pass_kernel,
-        in_specs=[scalars(), anywhere()],
-        out_specs=scalars(),
+        lambda pos_ref, held_ref, out_ref: None,
+        in_specs=[pl.BlockSpec(memory_space=pl.ANY)] * 2,
+        out_specs=pl.BlockSpec(memory_space=pl.ANY),
         out_shape=jax.ShapeDtypeStruct(pos.shape, pos.dtype),
+        input_output_aliases={0: 0},
         compiler_params=pltpu.CompilerParams(vmem_limit_bytes=MIB),
         cost_estimate=LONG,
         name="pass",
@@ -73,12 +69,9 @@
     return pl.BlockSpec(memory_space=pltpu.SMEM)
 
 
-def move_all(moves, sems):
-    copies = [pltpu.make_async_copy(source, target, sems.at[i]) for i, (source, target) in enumerate(moves)]
-    for copy in copies:
-        copy.start()
-    for copy in copies:
-        copy.wait()
+def move_all(moves):
+    for source, target in moves:
+        target[...] = source[...]
 
 
 def form_block(acts_ref, backs_ref, outs, prod_ref):
@@ -162,7 +155,7 @@
 
 def apply_kernel(pos_ref, *refs):
     grads, precs = refs[:NX], refs[NX : NX + NZL]
-    out_ref, query_ref, rows_ref, sems = refs[NX + NZL :]
+    out_ref, query_ref, rows_ref = refs[NX + NZL :]
     x, zl = pos_ref[0], pos_ref[1]
     moves = []
     for s in range(NX):
@@ -173,7 +166,7 @@
         count = precs[s].shape[1]
         at = pl.multiple_of(lax.rem(zl + s, NZL) * count, count)
         moves.append((precs[s], rows_ref.at[:, pl.ds(at, count)]))
-    move_all(moves, sems)
+    move_all(moves)
     layers, rows, grad = rows_ref.shape
     for layer in range(layers):
         prod = lax.dot_general(
@@ -196,7 +189,6 @@
         scratch_shapes=[
             pltpu.VMEM((NX * count, entries), jnp.bfloat16),
             pltpu.VMEM((layers, NZL * rows, grad), jnp.bfloat16),
-            pltpu.SemaphoreType.DMA((NX + NZL,)),
         ],
         compiler_params=pltpu.CompilerParams(vmem_limit_bytes=16 * MIB),
         cost_estimate=FREE,
@@ -205,7 +197,7 @@
 
 
 def join_kernel(pos_ref, *refs):
-    parts, (out_ref, sems) = refs[:NZL], refs[NZL:]
+    parts, out_ref = refs[:NZL], refs[NZL]
     zl = pos_ref[1]
     count = parts[0].shape[0] // NX
     moves = []
@@ -213,7 +205,7 @@
         at = pl.multiple_of(lax.rem(zl + s, NZL) * count, count)
         for x in range(NX):
             moves.append((parts[s].at[pl.ds(x * count, count)], out_ref.at[x, pl.ds(at, count)]))
-    move_all(moves, sems)
+    move_all(moves)
 
 
 def join_queries(pos, parts):
@@ -223,7 +215,6 @@
         in_specs=[scalars()] + [whole()] * NZL,
         out_specs=whole(),
         out_shape=jax.ShapeDtypeStruct((NX, NZL * count // NX, width), jnp.bfloat16),
-        scratch_shapes=[pltpu.SemaphoreType.DMA((NZL * NX,))],
         compiler_params=pltpu.CompilerParams(vmem_limit_bytes=16 * MIB),
         cost_estimate=pl.CostEstimate(flops=20 * 10**9, bytes_accessed=0, transcendentals=0),
         name="join",
@@ -247,7 +238,7 @@
 
 def near_kernel(scale, pos_ref, *refs):
     queries, trains, firsts = refs[:NX], refs[NX : NX + NY], refs[NX + NY : NX + 2 * NY]
-    out_ref, right_ref, left_ref, sems = refs[NX + 2 * NY :]
+    out_ref, right_ref, left_ref = refs[NX + 2 * NY :]
     x, y = pos_ref[0], pos_ref[2]
     layers = 2
     rows = queries[0].shape[1] // layers
@@ -256,7 +247,7 @@
         for layer in range(layers):
             at = pl.multiple_of(layer * NX * rows + lax.rem(x + s, NX) * rows, rows)
             moves.append((queries[s].at[:, pl.ds(layer * rows, rows)], right_ref.at[:, pl.ds(at, rows)]))
-    move_all(moves, sems)
+    move_all(moves)
     dot_terms(scale, left_ref, right_ref, out_ref)
 
 
@@ -272,7 +263,7 @@
             jax.ShapeDtypeStruct((total, columns), jnp.bfloat16),
             jax.ShapeDtypeStruct((columns, entries), jnp.bfloat16),
         ],
-        scratch_shapes=[pltpu.VMEM((total, entries), jnp.bfloat16), pltpu.SemaphoreType.DMA((2 * NX + 2 * NY,))],
+        scratch_shapes=[pltpu.VMEM((total, entries), jnp.bfloat16)],
         compiler_params=pltpu.CompilerParams(vmem_limit_bytes=24 * MIB),
         cost_estimate=FREE,
         name="near",
@@ -280,8 +271,8 @@
 
 
 def far_kernel(scale, pos_ref, right_ref, *refs):
-    trains, (out_ref, left_ref, sems) = refs[:NY], refs[NY:]
-    move_all(place_trains(pos_ref[2], trains, left_ref), sems)
+    trains, (out_ref, left_ref) = refs[:NY], refs[NY:]
+    move_all(place_trains(pos_ref[2], trains, left_ref))
     dot_terms(scale, left_ref, right_ref, out_ref)
 
 
@@ -294,7 +285,7 @@
         in_specs=[scalars()] + [whole()] * (1 + NY),
         out_specs=whole(),
         out_shape=jax.ShapeDtypeStruct((total, columns), jnp.bfloat16),
-        scratch_shapes=[pltpu.VMEM((total, entries), jnp.bfloat16), pltpu.SemaphoreType.DMA((NY,))],
+        scratch_shapes=[pltpu.VMEM((total, entries), jnp.bfloat16)],
         compiler_params=pltpu.CompilerParams(vmem_limit_bytes=16 * MIB),
         cost_estimate=pl.CostEstimate(flops=20 * 10**9, bytes_accessed=0, transcendentals=0),
         name="far",
@@ -355,7 +346,7 @@
     second = send(second, "far2", dz=NZL)
     mine = join_queries(pos, parts)
     queries = [mine, send(mine, "r_up", dx=-1), None, send(mine, "r_down", dx=1)]
-    later = pass_on(pos, first)
+    later = pass_on(jnp.stack([x, zl, y]).astype(jnp.int32), first)
     queries[1], queries[3], near[2], again, later = after(queries[1], queries[3], near[2], first, later)
     firsts = [first, send(again, "a1", dy=-1), None, send(first, "a3", dy=1)]
     queries[2] = send(queries[1], "r_next", dx=-1)

time: 94 us -> 91.8 us (0.977)
  Pallas kernels: 21.5 us -> 18.2 us
  waiting for transfers between devices: 26.2 us -> 28.5 us
  starting transfers between devices: 45.6 us -> 44.4 us
    ppermute x25, waiting for transfers between devices: 26.2 us -> 28.5 us  [send(): return lax.ppermute(value, AXES, pairs(move))]
    ppermute x25, starting transfers between devices: 45.6 us -> 44.4 us  [send(): return lax.ppermute(value, AXES, pairs(move))]
    pallas_call x1, Pallas kernels: 1.14 us -> 0.01 us  [pass_on(): pl.pallas_call(lambda pos_ref, held_ref, out_ref: None, in_specs=[pl.Bloc...]
  transfers between devices with their start and end apart: 25 -> 25, of which waited for: 8 -> 7; matrix products, arithmetic and copies ran while one was open for 0% -> 0% of each run, Pallas kernels for 19% -> 17%
where the time goes in v5:
time: 91.8 us; the launch traced here: 91.7 us
  starting transfers between devices  44.4 us (48%)
  waiting for transfers between devices  28.5 us (31%)
  Pallas kernels  18.2 us (20%)
    ppermute x25, starting transfers between devices, send(): return lax.ppermute(value, AXES, pairs(move))  44.4 us
    ppermute x25, waiting for transfers between devices, send(): return lax.ppermute(value, AXES, pairs(move))  28.5 us
    pallas_call x2, Pallas kernels, form_grads(): pl.pallas_call(functools.partial(form_kernel, block), in_specs=[anywhere(...  9.47 us
    pallas_call x2, Pallas kernels, add_terms(): pl.pallas_call(functools.partial(add_kernel, sizes), in_specs=[scalars(),...  3.15 us
    pallas_call x1, Pallas kernels, score_near(): pl.pallas_call(functools.partial(near_kernel, scale), in_specs=[scalars()...  2.59 us
  transfers between devices with their start and end apart: 25, of which 7 were waited for; matrix products, arithmetic and copies ran while one was open for 0% of the time, Pallas kernels for 17%

profile of v5, /device:TPU:65, one launch (start us, length us, event | category | flops | bytes accessed | tf_op | source)
XLA Modules:
  0.0 91.7 jit_solution(9429928027096450671)
XLA Ops:
  0.0 0.0 collective-permute-start
  0.0 4.2 %collective-permute-start.4 = (bf16[2,64,1024]{2,1,0:T(8,128)(2,1)}, bf16[2,64,1024]{2,1,0:T(8,128)(2,1)S(1)}, u32[]{:S(2)}, u32[]{:S(2)}) collective-permute-start(bf16[2,64,1024]{2,1,0:T(8,128)(2,1)} %refs_4_), channel_id=1, source_target_pairs={{0,34},{1,33},{16,50},{17,49},{32,0},{33,3},{48,16},{49,19},{2,32}... | collective-permute-start | bytes 786440 | tf_op jit(solution)/shard_map/p_far/ppermute | solution.py:37
  4.2 1.5 %collective-permute-start.5 = (bf16[2,64,1024]{2,1,0:T(8,128)(2,1)}, bf16[2,64,1024]{2,1,0:T(8,128)(2,1)S(1)}, u32[]{:S(2)}, u32[]{:S(2)}) collective-permute-start(bf16[2,64,1024]{2,1,0:T(8,128)(2,1)} %refs_4_), channel_id=1, source_target_pairs={{0,16},{1,17},{16,32},{17,33},{32,48},{33,49},{48,2},{49,3},{2,18}... | collective-permute-start | bytes 786440 | tf_op jit(solution)/shard_map/p_down/ppermute | solution.py:37
  5.7 3.1 %form.2.refs_0_ = bf16[32,2048]{1,0:T(8,128)(2,1)} custom-call(bf16[32,2,32,256]{3,2,1,0:T(8,128)(2,1)} %bitcast.10, bf16[32,2,32,256]{3,2,1,0:T(8,128)(2,1)} %bitcast.11), custom_call_target="tpu_custom_call" | custom-call | tf_op jit(solution)/shard_map/form/pallas_call | solution.py:139
  8.8 2.6 %collective-permute-start.1 = (bf16[32,2048]{1,0:T(8,128)(2,1)}, bf16[32,2048]{1,0:T(8,128)(2,1)S(1)}, u32[]{:S(2)}, u32[]{:S(2)}) collective-permute-start(bf16[32,2048]{1,0:T(8,128)(2,1)} %form.2.refs_0_), channel_id=1, source_target_pairs={{0,192},{1,193},{16,208},{17,209},{32,224},{33,225},{48,240},{49,2... | collective-permute-start | bytes 393224 | tf_op jit(solution)/shard_map/g_up/ppermute | solution.py:37
  11.4 0.5 collective-permute-start.2
  11.9 0.0 collective-permute-done.refs_5_
  11.9 0.6 collective-permute-start.3
  12.5 0.1 pad_add_fusion.pos_ref
  12.6 6.3 %form.3 = (bf16[128,2048]{1,0:T(8,128)(2,1)}, bf16[64,2048]{1,0:T(8,128)(2,1)}, bf16[64,2048]{1,0:T(8,128)(2,1)}) custom-call(bf16[128,2,32,256]{3,2,1,0:T(8,128)(2,1)} %acts_hbm, bf16[128,2,32,256]{3,2,1,0:T(8,128)(2,1)} %backs_hbm.1), custom_call_target="tpu_custom_call" | custom-call | tf_op jit(solution)/shard_map/form/pallas_call | solution.py:139
  18.9 0.0 collective-permute-done.1.refs_1_
  18.9 0.0 collective-permute-done.2.refs_2_
  18.9 2.3 %collective-permute-done.3.refs_3_ = bf16[32,2048]{1,0:T(8,128)(2,1)S(1)} collective-permute-done((bf16[32,2048]{1,0:T(8,128)(2,1)}, bf16[32,2048]{1,0:T(8,128)(2,1)S(1)}, u32[]{:S(2)}, u32[]{:S(2)}) %collective-permute-start.3) | collective-permute-done | bytes 131104 | tf_op jit(solution)/shard_map/g_down/ppermute | solution.py:37
  21.3 0.0 collective-permute-done.4.refs_6_
  21.3 0.0 collective-permute-done.5.refs_7_
  21.3 0.0 copy-done
  21.3 0.0 copy-done.2
  21.3 1.2 %apply.1.refs_0_ = bf16[128,512]{1,0:T(8,128)(2,1)S(1)} custom-call(s32[4]{0:T(128)S(1)} %pad_add_fusion.pos_ref, bf16[32,2048]{1,0:T(8,128)(2,1)S(1)} %copy-done, bf16[32,2048]{1,0:T(8,128)(2,1)S(1)} %collective-permute-done.1.refs_1_, bf16[32,2048]{1,0:T(8,128)(2,1)S(1)} %collective-permute-done.2.refs_2_, ...), custom_call_target="tpu_custom_call" | custom-call | tf_op jit(solution)/shard_map/apply/pallas_call | solution.py:184
  22.5 0.0 copy-start.3
  22.5 0.1 collective-permute-start.6
  22.6 2.8 %collective-permute-start.7 = (bf16[128,512]{1,0:T(8,128)(2,1)S(1)}, bf16[128,512]{1,0:T(8,128)(2,1)S(1)}, u32[]{:S(2)}, u32[]{:S(2)}) collective-permute-start(bf16[128,512]{1,0:T(8,128)(2,1)S(1)} %apply.1.refs_0_), channel_id=1, source_target_pairs={{0,32},{1,33},{16,48},{17,49},{32,0},{33,1},{48,16},{49,17},{2,34}... | collective-permute-start | bytes 393224 | tf_op jit(solution)/shard_map/low2/ppermute | solution.py:37
  25.4 0.0 collective-permute-start.8
  25.4 2.7 %collective-permute-start.11 = (bf16[128,2048]{1,0:T(8,128)(2,1)}, bf16[128,2048]{1,0:T(8,128)(2,1)S(1)}, u32[]{:S(2)}, u32[]{:S(2)}) collective-permute-start(bf16[128,2048]{1,0:T(8,128)(2,1)} %get-tuple-element.63.refs_4_), channel_id=1, source_target_pairs={{0,12},{1,13},{16,28},{17,29},{32,44},{33,45},{48,60},{49,61},{2,1... | collective-permute-start | bytes 1572872 | tf_op jit(solution)/shard_map/n_up/ppermute | solution.py:37
  28.1 0.0 collective-permute-start.12
  28.1 0.0 collective-permute-done.6.refs_1_
  28.1 5.5 %collective-permute-done.7.refs_2_ = bf16[128,512]{1,0:T(8,128)(2,1)S(1)} collective-permute-done((bf16[128,512]{1,0:T(8,128)(2,1)S(1)}, bf16[128,512]{1,0:T(8,128)(2,1)S(1)}, u32[]{:S(2)}, u32[]{:S(2)}) %collective-permute-start.7) | collective-permute-done | bytes 131104 | tf_op jit(solution)/shard_map/low2/ppermute | solution.py:37
  33.6 3.8 %collective-permute-done.8.refs_3_ = bf16[128,512]{1,0:T(8,128)(2,1)S(1)} collective-permute-done((bf16[128,512]{1,0:T(8,128)(2,1)S(1)}, bf16[128,512]{1,0:T(8,128)(2,1)S(1)}, u32[]{:S(2)}, u32[]{:S(2)}) %collective-permute-start.8) | collective-permute-done | bytes 131104 | tf_op jit(solution)/shard_map/low3/ppermute | solution.py:37
  37.4 1.6 %collective-permute-start.14 = (bf16[64,2048]{1,0:T(8,128)(2,1)}, bf16[64,2048]{1,0:T(8,128)(2,1)S(1)}, u32[]{:S(2)}, u32[]{:S(2)}) collective-permute-start(bf16[64,2048]{1,0:T(8,128)(2,1)} %get-tuple-element.65), channel_id=1, source_target_pairs={{0,2},{1,3},{16,18},{17,19},{32,34},{33,35},{48,50},{49,51},{2,0},... | collective-permute-start | bytes 786440 | tf_op jit(solution)/shard_map/far1/ppermute | solution.py:37
  39.0 0.6 join.1
  39.6 1.5 %collective-permute-start.10 = (bf16[512,512]{1,0:T(8,128)(2,1)S(1)}, bf16[512,512]{1,0:T(8,128)(2,1)S(1)}, u32[]{:S(2)}, u32[]{:S(2)}) collective-permute-start(bf16[512,512]{1,0:T(8,128)(2,1)S(1)} %bitcast.7), channel_id=1, source_target_pairs={{0,64},{1,65},{16,80},{17,81},{32,96},{33,97},{48,112},{49,113},{2... | collective-permute-start | bytes 1572872 | tf_op jit(solution)/shard_map/r_down/ppermute | solution.py:37
  41.1 1.5 %collective-permute-start.9 = (bf16[512,512]{1,0:T(8,128)(2,1)S(1)}, bf16[512,512]{1,0:T(8,128)(2,1)S(1)}, u32[]{:S(2)}, u32[]{:S(2)}) collective-permute-start(bf16[512,512]{1,0:T(8,128)(2,1)S(1)} %bitcast.8), channel_id=1, source_target_pairs={{0,192},{1,193},{16,208},{17,209},{32,224},{33,225},{48,240},{49,2... | collective-permute-start | bytes 1572872 | tf_op jit(solution)/shard_map/r_up/ppermute | solution.py:37
  42.6 0.0 collective-permute-done.11.refs_5_
  42.6 0.0 collective-permute-done.12.refs_7_
  42.6 2.7 %collective-permute-start.13 = (bf16[128,2048]{1,0:T(8,128)(2,1)S(1)}, bf16[128,2048]{1,0:T(8,128)(2,1)S(1)}, u32[]{:S(2)}, u32[]{:S(2)}) collective-permute-start(bf16[128,2048]{1,0:T(8,128)(2,1)S(1)} %collective-permute-done.11.refs_5_), channel_id=1, source_target_pairs={{0,12},{1,13},{16,28},{17,29},{32,44},{33,45},{48,60},{49,61},{2,1... | collective-permute-start | bytes 1572872 | tf_op jit(solution)/shard_map/n_two/ppermute | solution.py:37
  45.3 0.1 pad_add_fusion.1.pos_ref
  45.4 3.8 %collective-permute-start.15 = (bf16[64,2048]{1,0:T(8,128)(2,1)S(1)}, bf16[64,2048]{1,0:T(8,128)(2,1)S(1)}, u32[]{:S(2)}, u32[]{:S(2)}) collective-permute-start(bf16[64,2048]{1,0:T(8,128)(2,1)S(1)} %copy-done.3), channel_id=1, source_target_pairs={{0,2},{1,3},{16,18},{17,19},{32,34},{33,35},{48,50},{49,51},{2,0},... | collective-permute-start | bytes 786440 | tf_op jit(solution)/shard_map/far2/ppermute | solution.py:37
  49.2 6.8 %collective-permute-done.14.held_ref.refs_8_ = bf16[64,2048]{1,0:T(8,128)(2,1)S(1)} collective-permute-done((bf16[64,2048]{1,0:T(8,128)(2,1)}, bf16[64,2048]{1,0:T(8,128)(2,1)S(1)}, u32[]{:S(2)}, u32[]{:S(2)}) %collective-permute-start.14) | collective-permute-done | bytes 262176 | tf_op jit(solution)/shard_map/far1/ppermute | solution.py:37
  56.0 5.3 %collective-permute-start.17 = (bf16[64,2048]{1,0:T(8,128)(2,1)S(1)}, bf16[64,2048]{1,0:T(8,128)(2,1)S(1)}, u32[]{:S(2)}, u32[]{:S(2)}) collective-permute-start(bf16[64,2048]{1,0:T(8,128)(2,1)S(1)} %collective-permute-done.14.held_ref.refs_8_), channel_id=1, source_target_pairs={{0,4},{1,5},{16,20},{17,21},{32,36},{33,37},{48,52},{49,53},{2,6},... | collective-permute-start | bytes 786440 | tf_op jit(solution)/shard_map/a3/ppermute | solution.py:37
  61.3 0.0 collective-permute-done.10.refs_3_
  61.3 0.0 collective-permute-done.9.refs_1_
  61.3 0.0 collective-permute-done.13.refs_6_
  61.3 1.5 %collective-permute-start.16 = (bf16[64,2048]{1,0:T(8,128)(2,1)S(1)}, bf16[64,2048]{1,0:T(8,128)(2,1)S(1)}, u32[]{:S(2)}, u32[]{:S(2)}) collective-permute-start(bf16[64,2048]{1,0:T(8,128)(2,1)S(1)} %collective-permute-done.14.held_ref.refs_8_), channel_id=1, source_target_pairs={{0,12},{1,13},{16,28},{17,29},{32,44},{33,45},{48,60},{49,61},{2,1... | collective-permute-start | bytes 786440 | tf_op jit(solution)/shard_map/a1/ppermute | solution.py:37
  62.9 0.2 collective-permute-start.19
  63.0 0.2 collective-permute-done.15.refs_0_
  63.2 5.7 %collective-permute-done.17.refs_11_ = bf16[64,2048]{1,0:T(8,128)(2,1)S(1)} collective-permute-done((bf16[64,2048]{1,0:T(8,128)(2,1)S(1)}, bf16[64,2048]{1,0:T(8,128)(2,1)S(1)}, u32[]{:S(2)}, u32[]{:S(2)}) %collective-permute-start.17) | collective-permute-done | bytes 262176 | tf_op jit(solution)/shard_map/a3/ppermute | solution.py:37
  68.9 0.0 collective-permute-done.16.refs_9_
  68.9 2.5 %collective-permute-start.20 = (bf16[64,2048]{1,0:T(8,128)(2,1)S(1)}, bf16[64,2048]{1,0:T(8,128)(2,1)S(1)}, u32[]{:S(2)}, u32[]{:S(2)}) collective-permute-start(bf16[64,2048]{1,0:T(8,128)(2,1)S(1)} %collective-permute-done.15.refs_0_), channel_id=1, source_target_pairs={{0,12},{1,13},{16,28},{17,29},{32,44},{33,45},{48,60},{49,61},{2,1... | collective-permute-start | bytes 786440 | tf_op jit(solution)/shard_map/b1/ppermute | solution.py:37
  71.3 0.0 collective-permute-start.18
  71.4 0.0 collective-permute-start.22
  71.4 4.1 %collective-permute-done.20.refs_1_ = bf16[64,2048]{1,0:T(8,128)(2,1)S(1)} collective-permute-done((bf16[64,2048]{1,0:T(8,128)(2,1)S(1)}, bf16[64,2048]{1,0:T(8,128)(2,1)S(1)}, u32[]{:S(2)}, u32[]{:S(2)}) %collective-permute-start.20) | collective-permute-done | bytes 262176 | tf_op jit(solution)/shard_map/b1/ppermute | solution.py:37
  75.5 3.4 %collective-permute-start.21 = (bf16[64,2048]{1,0:T(8,128)(2,1)S(1)}, bf16[64,2048]{1,0:T(8,128)(2,1)S(1)}, u32[]{:S(2)}, u32[]{:S(2)}) collective-permute-start(bf16[64,2048]{1,0:T(8,128)(2,1)S(1)} %collective-permute-done.20.refs_1_), channel_id=1, source_target_pairs={{0,12},{1,13},{16,28},{17,29},{32,44},{33,45},{48,60},{49,61},{2,1... | collective-permute-start | bytes 786440 | tf_op jit(solution)/shard_map/b2/ppermute | solution.py:37
  78.9 0.0 collective-permute-done.18.refs_10_
  78.9 0.0 collective-permute-done.19.refs_2_
  78.9 2.6 %near.1 = (bf16[768,512]{1,0:T(8,128)(2,1)S(1)}, bf16[512,2048]{1,0:T(8,128)(2,1)S(1)}) custom-call(s32[3]{0:T(128)S(1)} %pass.1.pos_ref, bf16[512,512]{1,0:T(8,128)(2,1)S(1)} %bitcast.9, bf16[512,512]{1,0:T(8,128)(2,1)S(1)} %collective-permute-done.9.refs_1_, bf16[512,512]{1,0:T(8,128)(2,1)S(1)} %collective-permute-done.19.refs_2_, ...), custom_call_target="tpu_custom_call" | custom-call | tf_op jit(solution)/shard_map/near/pallas_call | solution.py:258
  81.5 4.7 %collective-permute-start.24 = (bf16[768,512]{1,0:T(8,128)(2,1)S(1)}, bf16[768,512]{1,0:T(8,128)(2,1)S(1)}, u32[]{:S(2)}, u32[]{:S(2)}) collective-permute-start(bf16[768,512]{1,0:T(8,128)(2,1)S(1)} %get-tuple-element.82.own_ref), channel_id=1, source_target_pairs={{0,1},{1,0},{16,17},{17,16},{32,33},{33,32},{48,49},{49,48},{2,3},... | collective-permute-start | bytes 2359304 | tf_op jit(solution)/shard_map/swap/ppermute | solution.py:37
  86.2 0.0 collective-permute-done.22.refs_3_
  86.2 0.0 collective-permute-done.21.refs_2_
  86.2 1.3 %far.1.own_ref = bf16[256,512]{1,0:T(8,128)(2,1)S(1)} custom-call(s32[4]{0:T(128)S(1)} %pad_add_fusion.pos_ref, bf16[512,2048]{1,0:T(8,128)(2,1)S(1)} %get-tuple-element.80.right_ref, bf16[64,2048]{1,0:T(8,128)(2,1)S(1)} %collective-permute-done.15.refs_0_, bf16[64,2048]{1,0:T(8,128)(2,1)S(1)} %collective-permute-done.20.refs_1_, ...), custom_call_target="tpu_custom_call" | custom-call | flops 20000000000 | tf_op jit(solution)/shard_map/far/pallas_call | solution.py:283
  87.5 0.8 collective-permute-start.23
  88.3 0.1 pad_add_fusion.2.places_ref
  88.4 0.0 collective-permute-done.24.other_ref
  88.4 1.8 %add.43.refs_0_ = f32[1024,512]{1,0:T(8,128)} custom-call(s32[8]{0:T(128)S(1)} %pad_add_fusion.2.places_ref, bf16[768,512]{1,0:T(8,128)(2,1)S(1)} %get-tuple-element.82.own_ref, bf16[768,512]{1,0:T(8,128)(2,1)S(1)} %collective-permute-done.24.other_ref), custom_call_target="tpu_custom_call" | custom-call | tf_op jit(solution)/shard_map/add/pallas_call | solution.py:313
  90.2 0.0 collective-permute-done.23.other_ref
  90.2 1.4 %add.44 = f32[1024,512]{1,0:T(8,128)} custom-call(s32[4]{0:T(128)S(1)} %broadcast_add_fusion.places_ref, bf16[256,512]{1,0:T(8,128)(2,1)S(1)} %far.1.own_ref, bf16[256,512]{1,0:T(8,128)(2,1)S(1)} %collective-permute-done.23.other_ref, f32[1024,512]{1,0:T(8,128)} %add.43.refs_0_), custom_call_target="tpu_custom_call", output_to_operand_aliasing={{}: (3, {})} | custom-call | tf_op jit(solution)/shard_map/add/pallas_call | solution.py:313
  (8 shorter events, 0.0 us)
Async XLA Ops:
  0.0 11.9 %collective-permute-start = (bf16[2,64,1024]{2,1,0:T(8,128)(2,1)}, bf16[2,64,1024]{2,1,0:T(8,128)(2,1)S(1)}, u32[]{:S(2)}, u32[]{:S(2)}) collective-permute-start(bf16[2,64,1024]{2,1,0:T(8,128)(2,1)} %refs_4_), channel_id=1, source_target_pairs={{0,50},{1,51},{16,0},{17,1},{32,16},{33,17},{48,32},{49,33},{2,48}... | collective-permute-start | bytes 786440 | tf_op jit(solution)/shard_map/p_up/ppermute | solution.py:37
  0.0 21.3 %collective-permute-start.4 = (bf16[2,64,1024]{2,1,0:T(8,128)(2,1)}, bf16[2,64,1024]{2,1,0:T(8,128)(2,1)S(1)}, u32[]{:S(2)}, u32[]{:S(2)}) collective-permute-start(bf16[2,64,1024]{2,1,0:T(8,128)(2,1)} %refs_4_), channel_id=1, source_target_pairs={{0,34},{1,33},{16,50},{17,49},{32,0},{33,3},{48,16},{49,19},{2,32}... | collective-permute-start | bytes 786440 | tf_op jit(solution)/shard_map/p_far/ppermute | solution.py:37
  4.2 17.1 %collective-permute-start.5 = (bf16[2,64,1024]{2,1,0:T(8,128)(2,1)}, bf16[2,64,1024]{2,1,0:T(8,128)(2,1)S(1)}, u32[]{:S(2)}, u32[]{:S(2)}) collective-permute-start(bf16[2,64,1024]{2,1,0:T(8,128)(2,1)} %refs_4_), channel_id=1, source_target_pairs={{0,16},{1,17},{16,32},{17,33},{32,48},{33,49},{48,2},{49,3},{2,18}... | collective-permute-start | bytes 786440 | tf_op jit(solution)/shard_map/p_down/ppermute | solution.py:37
  8.8 10.1 %collective-permute-start.1 = (bf16[32,2048]{1,0:T(8,128)(2,1)}, bf16[32,2048]{1,0:T(8,128)(2,1)S(1)}, u32[]{:S(2)}, u32[]{:S(2)}) collective-permute-start(bf16[32,2048]{1,0:T(8,128)(2,1)} %form.2.refs_0_), channel_id=1, source_target_pairs={{0,192},{1,193},{16,208},{17,209},{32,224},{33,225},{48,240},{49,2... | collective-permute-start | bytes 393224 | tf_op jit(solution)/shard_map/g_up/ppermute | solution.py:37
  11.4 7.6 %collective-permute-start.2 = (bf16[32,2048]{1,0:T(8,128)(2,1)}, bf16[32,2048]{1,0:T(8,128)(2,1)S(1)}, u32[]{:S(2)}, u32[]{:S(2)}) collective-permute-start(bf16[32,2048]{1,0:T(8,128)(2,1)} %form.2.refs_0_), channel_id=1, source_target_pairs={{0,128},{1,129},{16,144},{17,145},{32,160},{33,161},{48,176},{49,1... | collective-permute-start | bytes 393224 | tf_op jit(solution)/shard_map/g_far/ppermute | solution.py:37
  11.9 9.4 %collective-permute-start.3 = (bf16[32,2048]{1,0:T(8,128)(2,1)}, bf16[32,2048]{1,0:T(8,128)(2,1)S(1)}, u32[]{:S(2)}, u32[]{:S(2)}) collective-permute-start(bf16[32,2048]{1,0:T(8,128)(2,1)} %form.2.refs_0_), channel_id=1, source_target_pairs={{0,64},{1,65},{16,80},{17,81},{32,96},{33,97},{48,112},{49,113},{2... | collective-permute-start | bytes 393224 | tf_op jit(solution)/shard_map/g_down/ppermute | solution.py:37
  12.6 8.7 %copy-start = (bf16[32,2048]{1,0:T(8,128)(2,1)S(1)}, bf16[32,2048]{1,0:T(8,128)(2,1)}, u32[]{:S(2)}) copy-start(bf16[32,2048]{1,0:T(8,128)(2,1)} %form.2.refs_0_) | copy-start | bytes 393220
  12.6 8.7 %copy-start.2 = (bf16[2,64,1024]{2,1,0:T(8,128)(2,1)S(1)}, bf16[2,64,1024]{2,1,0:T(8,128)(2,1)}, u32[]{:S(2)}) copy-start(bf16[2,64,1024]{2,1,0:T(8,128)(2,1)} %refs_4_) | copy-start | bytes 786436
  22.5 22.9 %copy-start.3 = (bf16[64,2048]{1,0:T(8,128)(2,1)S(1)}, bf16[64,2048]{1,0:T(8,128)(2,1)}, u32[]{:S(2)}) copy-start(bf16[64,2048]{1,0:T(8,128)(2,1)} %get-tuple-element.67) | copy-start | bytes 786436
  22.5 5.6 %collective-permute-start.6 = (bf16[128,512]{1,0:T(8,128)(2,1)S(1)}, bf16[128,512]{1,0:T(8,128)(2,1)S(1)}, u32[]{:S(2)}, u32[]{:S(2)}) collective-permute-start(bf16[128,512]{1,0:T(8,128)(2,1)S(1)} %apply.1.refs_0_), channel_id=1, source_target_pairs={{0,48},{1,49},{16,0},{17,1},{32,16},{33,17},{48,32},{49,33},{2,50}... | collective-permute-start | bytes 393224 | tf_op jit(solution)/shard_map/low1/ppermute | solution.py:37
  22.6 11.0 %collective-permute-start.7 = (bf16[128,512]{1,0:T(8,128)(2,1)S(1)}, bf16[128,512]{1,0:T(8,128)(2,1)S(1)}, u32[]{:S(2)}, u32[]{:S(2)}) collective-permute-start(bf16[128,512]{1,0:T(8,128)(2,1)S(1)} %apply.1.refs_0_), channel_id=1, source_target_pairs={{0,32},{1,33},{16,48},{17,49},{32,0},{33,1},{48,16},{49,17},{2,34}... | collective-permute-start | bytes 393224 | tf_op jit(solution)/shard_map/low2/ppermute | solution.py:37
  25.4 12.1 %collective-permute-start.8 = (bf16[128,512]{1,0:T(8,128)(2,1)S(1)}, bf16[128,512]{1,0:T(8,128)(2,1)S(1)}, u32[]{:S(2)}, u32[]{:S(2)}) collective-permute-start(bf16[128,512]{1,0:T(8,128)(2,1)S(1)} %apply.1.refs_0_), channel_id=1, source_target_pairs={{0,16},{1,17},{16,32},{17,33},{32,48},{33,49},{48,0},{49,1},{2,18}... | collective-permute-start | bytes 393224 | tf_op jit(solution)/shard_map/low3/ppermute | solution.py:37
  25.4 17.2 %collective-permute-start.11 = (bf16[128,2048]{1,0:T(8,128)(2,1)}, bf16[128,2048]{1,0:T(8,128)(2,1)S(1)}, u32[]{:S(2)}, u32[]{:S(2)}) collective-permute-start(bf16[128,2048]{1,0:T(8,128)(2,1)} %get-tuple-element.63.refs_4_), channel_id=1, source_target_pairs={{0,12},{1,13},{16,28},{17,29},{32,44},{33,45},{48,60},{49,61},{2,1... | collective-permute-start | bytes 1572872 | tf_op jit(solution)/shard_map/n_up/ppermute | solution.py:37
  28.1 14.5 %collective-permute-start.12 = (bf16[128,2048]{1,0:T(8,128)(2,1)}, bf16[128,2048]{1,0:T(8,128)(2,1)S(1)}, u32[]{:S(2)}, u32[]{:S(2)}) collective-permute-start(bf16[128,2048]{1,0:T(8,128)(2,1)} %get-tuple-element.63.refs_4_), channel_id=1, source_target_pairs={{0,4},{1,5},{16,20},{17,21},{32,36},{33,37},{48,52},{49,53},{2,6},... | collective-permute-start | bytes 1572872 | tf_op jit(solution)/shard_map/n_down/ppermute | solution.py:37
  37.4 18.6 %collective-permute-start.14 = (bf16[64,2048]{1,0:T(8,128)(2,1)}, bf16[64,2048]{1,0:T(8,128)(2,1)S(1)}, u32[]{:S(2)}, u32[]{:S(2)}) collective-permute-start(bf16[64,2048]{1,0:T(8,128)(2,1)} %get-tuple-element.65), channel_id=1, source_target_pairs={{0,2},{1,3},{16,18},{17,19},{32,34},{33,35},{48,50},{49,51},{2,0},... | collective-permute-start | bytes 786440 | tf_op jit(solution)/shard_map/far1/ppermute | solution.py:37
  39.6 21.7 %collective-permute-start.10 = (bf16[512,512]{1,0:T(8,128)(2,1)S(1)}, bf16[512,512]{1,0:T(8,128)(2,1)S(1)}, u32[]{:S(2)}, u32[]{:S(2)}) collective-permute-start(bf16[512,512]{1,0:T(8,128)(2,1)S(1)} %bitcast.7), channel_id=1, source_target_pairs={{0,64},{1,65},{16,80},{17,81},{32,96},{33,97},{48,112},{49,113},{2... | collective-permute-start | bytes 1572872 | tf_op jit(solution)/shard_map/r_down/ppermute | solution.py:37
  41.1 20.2 %collective-permute-start.9 = (bf16[512,512]{1,0:T(8,128)(2,1)S(1)}, bf16[512,512]{1,0:T(8,128)(2,1)S(1)}, u32[]{:S(2)}, u32[]{:S(2)}) collective-permute-start(bf16[512,512]{1,0:T(8,128)(2,1)S(1)} %bitcast.8), channel_id=1, source_target_pairs={{0,192},{1,193},{16,208},{17,209},{32,224},{33,225},{48,240},{49,2... | collective-permute-start | bytes 1572872 | tf_op jit(solution)/shard_map/r_up/ppermute | solution.py:37
  42.6 18.8 %collective-permute-start.13 = (bf16[128,2048]{1,0:T(8,128)(2,1)S(1)}, bf16[128,2048]{1,0:T(8,128)(2,1)S(1)}, u32[]{:S(2)}, u32[]{:S(2)}) collective-permute-start(bf16[128,2048]{1,0:T(8,128)(2,1)S(1)} %collective-permute-done.11.refs_5_), channel_id=1, source_target_pairs={{0,12},{1,13},{16,28},{17,29},{32,44},{33,45},{48,60},{49,61},{2,1... | collective-permute-start | bytes 1572872 | tf_op jit(solution)/shard_map/n_two/ppermute | solution.py:37
  45.4 33.5 %copy-start.1 = (bf16[128,2048]{1,0:T(8,128)(2,1)S(1)}, bf16[128,2048]{1,0:T(8,128)(2,1)}, u32[]{:S(2)}) copy-start(bf16[128,2048]{1,0:T(8,128)(2,1)} %get-tuple-element.63.refs_4_) | copy-start | bytes 1572868
  45.4 17.8 %collective-permute-start.15 = (bf16[64,2048]{1,0:T(8,128)(2,1)S(1)}, bf16[64,2048]{1,0:T(8,128)(2,1)S(1)}, u32[]{:S(2)}, u32[]{:S(2)}) collective-permute-start(bf16[64,2048]{1,0:T(8,128)(2,1)S(1)} %copy-done.3), channel_id=1, source_target_pairs={{0,2},{1,3},{16,18},{17,19},{32,34},{33,35},{48,50},{49,51},{2,0},... | collective-permute-start | bytes 786440 | tf_op jit(solution)/shard_map/far2/ppermute | solution.py:37
  56.0 12.9 %collective-permute-start.17 = (bf16[64,2048]{1,0:T(8,128)(2,1)S(1)}, bf16[64,2048]{1,0:T(8,128)(2,1)S(1)}, u32[]{:S(2)}, u32[]{:S(2)}) collective-permute-start(bf16[64,2048]{1,0:T(8,128)(2,1)S(1)} %collective-permute-done.14.held_ref.refs_8_), channel_id=1, source_target_pairs={{0,4},{1,5},{16,20},{17,21},{32,36},{33,37},{48,52},{49,53},{2,6},... | collective-permute-start | bytes 786440 | tf_op jit(solution)/shard_map/a3/ppermute | solution.py:37
  61.3 7.6 %collective-permute-start.16 = (bf16[64,2048]{1,0:T(8,128)(2,1)S(1)}, bf16[64,2048]{1,0:T(8,128)(2,1)S(1)}, u32[]{:S(2)}, u32[]{:S(2)}) collective-permute-start(bf16[64,2048]{1,0:T(8,128)(2,1)S(1)} %collective-permute-done.14.held_ref.refs_8_), channel_id=1, source_target_pairs={{0,12},{1,13},{16,28},{17,29},{32,44},{33,45},{48,60},{49,61},{2,1... | collective-permute-start | bytes 786440 | tf_op jit(solution)/shard_map/a1/ppermute | solution.py:37
  62.9 16.1 %collective-permute-start.19 = (bf16[512,512]{1,0:T(8,128)(2,1)S(1)}, bf16[512,512]{1,0:T(8,128)(2,1)S(1)}, u32[]{:S(2)}, u32[]{:S(2)}) collective-permute-start(bf16[512,512]{1,0:T(8,128)(2,1)S(1)} %collective-permute-done.9.refs_1_), channel_id=1, source_target_pairs={{0,192},{1,193},{16,208},{17,209},{32,224},{33,225},{48,240},{49,2... | collective-permute-start | bytes 1572872 | tf_op jit(solution)/shard_map/r_next/ppermute | solution.py:37
  68.9 6.6 %collective-permute-start.20 = (bf16[64,2048]{1,0:T(8,128)(2,1)S(1)}, bf16[64,2048]{1,0:T(8,128)(2,1)S(1)}, u32[]{:S(2)}, u32[]{:S(2)}) collective-permute-start(bf16[64,2048]{1,0:T(8,128)(2,1)S(1)} %collective-permute-done.15.refs_0_), channel_id=1, source_target_pairs={{0,12},{1,13},{16,28},{17,29},{32,44},{33,45},{48,60},{49,61},{2,1... | collective-permute-start | bytes 786440 | tf_op jit(solution)/shard_map/b1/ppermute | solution.py:37
  71.3 7.6 %collective-permute-start.18 = (bf16[64,2048]{1,0:T(8,128)(2,1)S(1)}, bf16[64,2048]{1,0:T(8,128)(2,1)S(1)}, u32[]{:S(2)}, u32[]{:S(2)}) collective-permute-start(bf16[64,2048]{1,0:T(8,128)(2,1)S(1)} %collective-permute-done.17.refs_11_), channel_id=1, source_target_pairs={{0,4},{1,5},{16,20},{17,21},{32,36},{33,37},{48,52},{49,53},{2,6},... | collective-permute-start | bytes 786440 | tf_op jit(solution)/shard_map/a2/ppermute | solution.py:37
  71.4 14.9 %collective-permute-start.22 = (bf16[64,2048]{1,0:T(8,128)(2,1)S(1)}, bf16[64,2048]{1,0:T(8,128)(2,1)S(1)}, u32[]{:S(2)}, u32[]{:S(2)}) collective-permute-start(bf16[64,2048]{1,0:T(8,128)(2,1)S(1)} %collective-permute-done.15.refs_0_), channel_id=1, source_target_pairs={{0,4},{1,5},{16,20},{17,21},{32,36},{33,37},{48,52},{49,53},{2,6},... | collective-permute-start | bytes 786440 | tf_op jit(solution)/shard_map/b3/ppermute | solution.py:37
  75.5 10.7 %collective-permute-start.21 = (bf16[64,2048]{1,0:T(8,128)(2,1)S(1)}, bf16[64,2048]{1,0:T(8,128)(2,1)S(1)}, u32[]{:S(2)}, u32[]{:S(2)}) collective-permute-start(bf16[64,2048]{1,0:T(8,128)(2,1)S(1)} %collective-permute-done.20.refs_1_), channel_id=1, source_target_pairs={{0,12},{1,13},{16,28},{17,29},{32,44},{33,45},{48,60},{49,61},{2,1... | collective-permute-start | bytes 786440 | tf_op jit(solution)/shard_map/b2/ppermute | solution.py:37
  81.5 6.9 %collective-permute-start.24 = (bf16[768,512]{1,0:T(8,128)(2,1)S(1)}, bf16[768,512]{1,0:T(8,128)(2,1)S(1)}, u32[]{:S(2)}, u32[]{:S(2)}) collective-permute-start(bf16[768,512]{1,0:T(8,128)(2,1)S(1)} %get-tuple-element.82.own_ref), channel_id=1, source_target_pairs={{0,1},{1,0},{16,17},{17,16},{32,33},{33,32},{48,49},{49,48},{2,3},... | collective-permute-start | bytes 2359304 | tf_op jit(solution)/shard_map/swap/ppermute | solution.py:37
  87.5 2.6 %collective-permute-start.23 = (bf16[256,512]{1,0:T(8,128)(2,1)S(1)}, bf16[256,512]{1,0:T(8,128)(2,1)S(1)}, u32[]{:S(2)}, u32[]{:S(2)}) collective-permute-start(bf16[256,512]{1,0:T(8,128)(2,1)S(1)} %far.1.own_ref), channel_id=1, source_target_pairs={{0,1},{1,0},{16,17},{17,16},{32,33},{33,32},{48,49},{49,48},{2,3},... | collective-permute-start | bytes 786440 | tf_op jit(solution)/shard_map/swap_last/ppermute | solution.py:37

commit v6 on v5

--- a/solution.py
+++ b/solution.py
@@ -11,6 +11,7 @@
 NX, NY, NZL, NZH = 4, 4, 4, 2
 NT = (((1,), (1,)), ((), ()))
 MIB = 1 << 20
+LOW_ORDER = (0, 2, 1, 3)
 FREE = pl.CostEstimate(flops=0, bytes_accessed=0, transcendentals=0)
 
 
@@ -201,8 +202,8 @@
     zl = pos_ref[1]
     count = parts[0].shape[0] // NX
     moves = []
-    for s in range(NZL):
-        at = pl.multiple_of(lax.rem(zl + s, NZL) * count, count)
+    for s, shift in enumerate(LOW_ORDER):
+        at = pl.multiple_of(lax.rem(zl + shift, NZL) * count, count)
         for x in range(NX):
             moves.append((parts[s].at[pl.ds(x * count, count)], out_ref.at[x, pl.ds(at, count)]))
     move_all(moves)
@@ -338,7 +339,7 @@
     train_grad, first, second, *got = after(train_grad, first, second, *grads, *precs)
     near = [train_grad, send(train_grad, "n_up", dy=-1), None, send(train_grad, "n_down", dy=1)]
     part = apply_rows(pos, got[:NX], got[NX:])
-    parts = [part] + [send(part, "low%d" % s, dzl=-s) for s in (1, 2, 3)]
+    parts = [part] + [send(part, "low%d" % s, dzl=-s) for s in LOW_ORDER[1:]]
     near[1], near[3] = after(near[1], near[3])
     near[2] = send(near[1], "n_two", dy=-1)
     first, second, *parts = after(first, second, *parts)

time: 91.8 us -> 91.3 us (level)
  the two profiles are of different devices: /device:TPU:65 before, /device:TPU:1 now
where the time goes in v6:
time: 91.3 us; the launch traced here: 90 us
  starting transfers between devices  43.6 us (48%)
  waiting for transfers between devices  27.6 us (30%)
  Pallas kernels  18.2 us (20%)
    ppermute x25, starting transfers between devices, send(): return lax.ppermute(value, AXES, pairs(move))  43.6 us
    ppermute x25, waiting for transfers between devices, send(): return lax.ppermute(value, AXES, pairs(move))  27.6 us
    pallas_call x2, Pallas kernels, form_grads(): pl.pallas_call(functools.partial(form_kernel, block), in_specs=[anywhere(...  9.47 us
    pallas_call x2, Pallas kernels, add_terms(): pl.pallas_call(functools.partial(add_kernel, sizes), in_specs=[scalars(),...  3.15 us
    pallas_call x1, Pallas kernels, score_near(): pl.pallas_call(functools.partial(near_kernel, scale), in_specs=[scalars()...  2.59 us
  transfers between devices with their start and end apart: 25, of which 8 were waited for; matrix products, arithmetic and copies ran while one was open for 0% of the time, Pallas kernels for 17%

profile of v6, /device:TPU:1, one launch (start us, length us, event | category | flops | bytes accessed | tf_op | source)
XLA Modules:
  0.0 90.0 jit_solution(8987727430518643971)
XLA Ops:
  0.0 6.4 %collective-permute-start = (bf16[2,64,1024]{2,1,0:T(8,128)(2,1)}, bf16[2,64,1024]{2,1,0:T(8,128)(2,1)S(1)}, u32[]{:S(2)}, u32[]{:S(2)}) collective-permute-start(bf16[2,64,1024]{2,1,0:T(8,128)(2,1)} %refs_4_), channel_id=1, source_target_pairs={{0,50},{1,51},{16,0},{17,1},{32,16},{33,17},{48,32},{49,33},{2,48}... | collective-permute-start | bytes 786440 | tf_op jit(solution)/shard_map/p_up/ppermute | solution.py:38
  6.4 0.0 collective-permute-start.4
  6.4 0.0 collective-permute-start.5
  6.4 3.1 %form.2.refs_0_ = bf16[32,2048]{1,0:T(8,128)(2,1)} custom-call(bf16[32,2,32,256]{3,2,1,0:T(8,128)(2,1)} %bitcast.10, bf16[32,2,32,256]{3,2,1,0:T(8,128)(2,1)} %bitcast.11), custom_call_target="tpu_custom_call" | custom-call | tf_op jit(solution)/shard_map/form/pallas_call | solution.py:140
  9.6 2.6 %collective-permute-start.1 = (bf16[32,2048]{1,0:T(8,128)(2,1)}, bf16[32,2048]{1,0:T(8,128)(2,1)S(1)}, u32[]{:S(2)}, u32[]{:S(2)}) collective-permute-start(bf16[32,2048]{1,0:T(8,128)(2,1)} %form.2.refs_0_), channel_id=1, source_target_pairs={{0,192},{1,193},{16,208},{17,209},{32,224},{33,225},{48,240},{49,2... | collective-permute-start | bytes 393224 | tf_op jit(solution)/shard_map/g_up/ppermute | solution.py:38
  12.1 0.5 collective-permute-start.2
  12.6 1.7 %collective-permute-done.refs_5_ = bf16[2,64,1024]{2,1,0:T(8,128)(2,1)S(1)} collective-permute-done((bf16[2,64,1024]{2,1,0:T(8,128)(2,1)}, bf16[2,64,1024]{2,1,0:T(8,128)(2,1)S(1)}, u32[]{:S(2)}, u32[]{:S(2)}) %collective-permute-start) | collective-permute-done | bytes 262176 | tf_op jit(solution)/shard_map/p_up/ppermute | solution.py:38
  14.4 1.2 %collective-permute-start.3 = (bf16[32,2048]{1,0:T(8,128)(2,1)}, bf16[32,2048]{1,0:T(8,128)(2,1)S(1)}, u32[]{:S(2)}, u32[]{:S(2)}) collective-permute-start(bf16[32,2048]{1,0:T(8,128)(2,1)} %form.2.refs_0_), channel_id=1, source_target_pairs={{0,64},{1,65},{16,80},{17,81},{32,96},{33,97},{48,112},{49,113},{2... | collective-permute-start | bytes 393224 | tf_op jit(solution)/shard_map/g_down/ppermute | solution.py:38
  15.6 0.1 pad_add_fusion.pos_ref
  15.7 6.3 %form.3 = (bf16[128,2048]{1,0:T(8,128)(2,1)}, bf16[64,2048]{1,0:T(8,128)(2,1)}, bf16[64,2048]{1,0:T(8,128)(2,1)}) custom-call(bf16[128,2,32,256]{3,2,1,0:T(8,128)(2,1)} %acts_hbm, bf16[128,2,32,256]{3,2,1,0:T(8,128)(2,1)} %backs_hbm.1), custom_call_target="tpu_custom_call" | custom-call | tf_op jit(solution)/shard_map/form/pallas_call | solution.py:140
  22.0 0.0 collective-permute-done.1.refs_1_
  22.0 0.0 collective-permute-done.2.refs_2_
  22.0 0.0 collective-permute-done.3.refs_3_
  22.0 0.0 collective-permute-done.4.refs_6_
  22.0 0.0 collective-permute-done.5.refs_7_
  22.0 0.0 copy-done
  22.1 1.2 %apply.1.refs_0_ = bf16[128,512]{1,0:T(8,128)(2,1)S(1)} custom-call(s32[4]{0:T(128)S(1)} %pad_add_fusion.pos_ref, bf16[32,2048]{1,0:T(8,128)(2,1)S(1)} %copy-done, bf16[32,2048]{1,0:T(8,128)(2,1)S(1)} %collective-permute-done.1.refs_1_, bf16[32,2048]{1,0:T(8,128)(2,1)S(1)} %collective-permute-done.2.refs_2_, ...), custom_call_target="tpu_custom_call" | custom-call | tf_op jit(solution)/shard_map/apply/pallas_call | solution.py:185
  23.2 0.0 copy-start.3
  23.2 3.2 %collective-permute-start.6 = (bf16[128,512]{1,0:T(8,128)(2,1)S(1)}, bf16[128,512]{1,0:T(8,128)(2,1)S(1)}, u32[]{:S(2)}, u32[]{:S(2)}) collective-permute-start(bf16[128,512]{1,0:T(8,128)(2,1)S(1)} %apply.1.refs_0_), channel_id=1, source_target_pairs={{0,32},{1,33},{16,48},{17,49},{32,0},{33,1},{48,16},{49,17},{2,34}... | collective-permute-start | bytes 393224 | tf_op jit(solution)/shard_map/low2/ppermute | solution.py:38
  26.4 0.5 collective-permute-start.7
  26.9 0.9 %collective-permute-start.8 = (bf16[128,512]{1,0:T(8,128)(2,1)S(1)}, bf16[128,512]{1,0:T(8,128)(2,1)S(1)}, u32[]{:S(2)}, u32[]{:S(2)}) collective-permute-start(bf16[128,512]{1,0:T(8,128)(2,1)S(1)} %apply.1.refs_0_), channel_id=1, source_target_pairs={{0,16},{1,17},{16,32},{17,33},{32,48},{33,49},{48,0},{49,1},{2,18}... | collective-permute-start | bytes 393224 | tf_op jit(solution)/shard_map/low3/ppermute | solution.py:38
  27.9 2.7 %collective-permute-start.11 = (bf16[128,2048]{1,0:T(8,128)(2,1)}, bf16[128,2048]{1,0:T(8,128)(2,1)S(1)}, u32[]{:S(2)}, u32[]{:S(2)}) collective-permute-start(bf16[128,2048]{1,0:T(8,128)(2,1)} %get-tuple-element.63.refs_4_), channel_id=1, source_target_pairs={{0,12},{1,13},{16,28},{17,29},{32,44},{33,45},{48,60},{49,61},{2,1... | collective-permute-start | bytes 1572872 | tf_op jit(solution)/shard_map/n_up/ppermute | solution.py:38
  30.6 0.0 collective-permute-start.12
  30.6 2.6 %collective-permute-done.6.refs_1_ = bf16[128,512]{1,0:T(8,128)(2,1)S(1)} collective-permute-done((bf16[128,512]{1,0:T(8,128)(2,1)S(1)}, bf16[128,512]{1,0:T(8,128)(2,1)S(1)}, u32[]{:S(2)}, u32[]{:S(2)}) %collective-permute-start.6) | collective-permute-done | bytes 131104 | tf_op jit(solution)/shard_map/low2/ppermute | solution.py:38
  33.2 0.5 collective-permute-done.7.refs_2_
  33.7 0.9 collective-permute-done.8.refs_3_
  34.6 5.7 %collective-permute-start.14 = (bf16[64,2048]{1,0:T(8,128)(2,1)}, bf16[64,2048]{1,0:T(8,128)(2,1)S(1)}, u32[]{:S(2)}, u32[]{:S(2)}) collective-permute-start(bf16[64,2048]{1,0:T(8,128)(2,1)} %get-tuple-element.65), channel_id=1, source_target_pairs={{0,2},{1,3},{16,18},{17,19},{32,34},{33,35},{48,50},{49,51},{2,0},... | collective-permute-start | bytes 786440 | tf_op jit(solution)/shard_map/far1/ppermute | solution.py:38
  40.3 0.6 join.1
  40.9 0.3 collective-permute-start.10
  41.2 2.7 %collective-permute-start.9 = (bf16[512,512]{1,0:T(8,128)(2,1)S(1)}, bf16[512,512]{1,0:T(8,128)(2,1)S(1)}, u32[]{:S(2)}, u32[]{:S(2)}) collective-permute-start(bf16[512,512]{1,0:T(8,128)(2,1)S(1)} %bitcast.8), channel_id=1, source_target_pairs={{0,192},{1,193},{16,208},{17,209},{32,224},{33,225},{48,240},{49,2... | collective-permute-start | bytes 1572872 | tf_op jit(solution)/shard_map/r_up/ppermute | solution.py:38
  43.8 0.0 collective-permute-done.11.refs_5_
  43.8 0.0 collective-permute-done.12.refs_7_
  43.8 2.7 %collective-permute-start.13 = (bf16[128,2048]{1,0:T(8,128)(2,1)S(1)}, bf16[128,2048]{1,0:T(8,128)(2,1)S(1)}, u32[]{:S(2)}, u32[]{:S(2)}) collective-permute-start(bf16[128,2048]{1,0:T(8,128)(2,1)S(1)} %collective-permute-done.11.refs_5_), channel_id=1, source_target_pairs={{0,12},{1,13},{16,28},{17,29},{32,44},{33,45},{48,60},{49,61},{2,1... | collective-permute-start | bytes 1572872 | tf_op jit(solution)/shard_map/n_two/ppermute | solution.py:38
  46.6 0.1 pad_add_fusion.1.pos_ref
  46.6 1.5 %collective-permute-start.15 = (bf16[64,2048]{1,0:T(8,128)(2,1)S(1)}, bf16[64,2048]{1,0:T(8,128)(2,1)S(1)}, u32[]{:S(2)}, u32[]{:S(2)}) collective-permute-start(bf16[64,2048]{1,0:T(8,128)(2,1)S(1)} %copy-done.3), channel_id=1, source_target_pairs={{0,2},{1,3},{16,18},{17,19},{32,34},{33,35},{48,50},{49,51},{2,0},... | collective-permute-start | bytes 786440 | tf_op jit(solution)/shard_map/far2/ppermute | solution.py:38
  48.1 0.0 collective-permute-done.14.held_ref.refs_8_
  48.1 1.2 %collective-permute-start.17 = (bf16[64,2048]{1,0:T(8,128)(2,1)S(1)}, bf16[64,2048]{1,0:T(8,128)(2,1)S(1)}, u32[]{:S(2)}, u32[]{:S(2)}) collective-permute-start(bf16[64,2048]{1,0:T(8,128)(2,1)S(1)} %collective-permute-done.14.held_ref.refs_8_), channel_id=1, source_target_pairs={{0,4},{1,5},{16,20},{17,21},{32,36},{33,37},{48,52},{49,53},{2,6},... | collective-permute-start | bytes 786440 | tf_op jit(solution)/shard_map/a3/ppermute | solution.py:38
  49.3 4.9 %collective-permute-done.10.refs_3_ = bf16[512,512]{1,0:T(8,128)(2,1)S(1)} collective-permute-done((bf16[512,512]{1,0:T(8,128)(2,1)S(1)}, bf16[512,512]{1,0:T(8,128)(2,1)S(1)}, u32[]{:S(2)}, u32[]{:S(2)}) %collective-permute-start.10) | collective-permute-done | bytes 524320 | tf_op jit(solution)/shard_map/r_down/ppermute | solution.py:38
  54.2 0.0 collective-permute-done.9.refs_1_
  54.2 1.4 %collective-permute-done.13.refs_6_ = bf16[128,2048]{1,0:T(8,128)(2,1)S(1)} collective-permute-done((bf16[128,2048]{1,0:T(8,128)(2,1)S(1)}, bf16[128,2048]{1,0:T(8,128)(2,1)S(1)}, u32[]{:S(2)}, u32[]{:S(2)}) %collective-permute-start.13) | collective-permute-done | bytes 524320 | tf_op jit(solution)/shard_map/n_two/ppermute | solution.py:38
  55.6 3.4 %collective-permute-start.16 = (bf16[64,2048]{1,0:T(8,128)(2,1)S(1)}, bf16[64,2048]{1,0:T(8,128)(2,1)S(1)}, u32[]{:S(2)}, u32[]{:S(2)}) collective-permute-start(bf16[64,2048]{1,0:T(8,128)(2,1)S(1)} %collective-permute-done.14.held_ref.refs_8_), channel_id=1, source_target_pairs={{0,12},{1,13},{16,28},{17,29},{32,44},{33,45},{48,60},{49,61},{2,1... | collective-permute-start | bytes 786440 | tf_op jit(solution)/shard_map/a1/ppermute | solution.py:38
  59.0 0.4 collective-permute-start.19
  59.4 9.8 %collective-permute-done.15.refs_0_ = bf16[64,2048]{1,0:T(8,128)(2,1)S(1)} collective-permute-done((bf16[64,2048]{1,0:T(8,128)(2,1)S(1)}, bf16[64,2048]{1,0:T(8,128)(2,1)S(1)}, u32[]{:S(2)}, u32[]{:S(2)}) %collective-permute-start.15) | collective-permute-done | bytes 262176 | tf_op jit(solution)/shard_map/far2/ppermute | solution.py:38
  69.1 0.0 collective-permute-done.17.refs_11_
  69.1 0.0 collective-permute-done.16.refs_9_
  69.1 0.0 collective-permute-start.20
  69.1 1.5 %collective-permute-start.18 = (bf16[64,2048]{1,0:T(8,128)(2,1)S(1)}, bf16[64,2048]{1,0:T(8,128)(2,1)S(1)}, u32[]{:S(2)}, u32[]{:S(2)}) collective-permute-start(bf16[64,2048]{1,0:T(8,128)(2,1)S(1)} %collective-permute-done.17.refs_11_), channel_id=1, source_target_pairs={{0,4},{1,5},{16,20},{17,21},{32,36},{33,37},{48,52},{49,53},{2,6},... | collective-permute-start | bytes 786440 | tf_op jit(solution)/shard_map/a2/ppermute | solution.py:38
  70.6 0.0 collective-permute-start.22
  70.6 5.8 %collective-permute-done.20.refs_1_ = bf16[64,2048]{1,0:T(8,128)(2,1)S(1)} collective-permute-done((bf16[64,2048]{1,0:T(8,128)(2,1)S(1)}, bf16[64,2048]{1,0:T(8,128)(2,1)S(1)}, u32[]{:S(2)}, u32[]{:S(2)}) %collective-permute-start.20) | collective-permute-done | bytes 262176 | tf_op jit(solution)/shard_map/b1/ppermute | solution.py:38
  76.5 0.0 collective-permute-start.21
  76.5 0.0 collective-permute-done.18.refs_10_
  76.5 0.0 collective-permute-done.19.refs_2_
  76.5 0.0 copy-done.1
  76.5 2.6 %near.1 = (bf16[768,512]{1,0:T(8,128)(2,1)S(1)}, bf16[512,2048]{1,0:T(8,128)(2,1)S(1)}) custom-call(s32[3]{0:T(128)S(1)} %pass.1.pos_ref, bf16[512,512]{1,0:T(8,128)(2,1)S(1)} %bitcast.9, bf16[512,512]{1,0:T(8,128)(2,1)S(1)} %collective-permute-done.9.refs_1_, bf16[512,512]{1,0:T(8,128)(2,1)S(1)} %collective-permute-done.19.refs_2_, ...), custom_call_target="tpu_custom_call" | custom-call | tf_op jit(solution)/shard_map/near/pallas_call | solution.py:259
  79.1 5.1 %collective-permute-start.24 = (bf16[768,512]{1,0:T(8,128)(2,1)S(1)}, bf16[768,512]{1,0:T(8,128)(2,1)S(1)}, u32[]{:S(2)}, u32[]{:S(2)}) collective-permute-start(bf16[768,512]{1,0:T(8,128)(2,1)S(1)} %get-tuple-element.82.own_ref), channel_id=1, source_target_pairs={{0,1},{1,0},{16,17},{17,16},{32,33},{33,32},{48,49},{49,48},{2,3},... | collective-permute-start | bytes 2359304 | tf_op jit(solution)/shard_map/swap/ppermute | solution.py:38
  84.2 0.0 collective-permute-done.22.refs_3_
  84.2 0.0 collective-permute-done.21.refs_2_
  84.2 1.3 %far.1.own_ref = bf16[256,512]{1,0:T(8,128)(2,1)S(1)} custom-call(s32[4]{0:T(128)S(1)} %pad_add_fusion.pos_ref, bf16[512,2048]{1,0:T(8,128)(2,1)S(1)} %get-tuple-element.80.right_ref, bf16[64,2048]{1,0:T(8,128)(2,1)S(1)} %collective-permute-done.15.refs_0_, bf16[64,2048]{1,0:T(8,128)(2,1)S(1)} %collective-permute-done.20.refs_1_, ...), custom_call_target="tpu_custom_call" | custom-call | flops 20000000000 | tf_op jit(solution)/shard_map/far/pallas_call | solution.py:284
  85.5 1.1 %collective-permute-start.23 = (bf16[256,512]{1,0:T(8,128)(2,1)S(1)}, bf16[256,512]{1,0:T(8,128)(2,1)S(1)}, u32[]{:S(2)}, u32[]{:S(2)}) collective-permute-start(bf16[256,512]{1,0:T(8,128)(2,1)S(1)} %far.1.own_ref), channel_id=1, source_target_pairs={{0,1},{1,0},{16,17},{17,16},{32,33},{33,32},{48,49},{49,48},{2,3},... | collective-permute-start | bytes 786440 | tf_op jit(solution)/shard_map/swap_last/ppermute | solution.py:38
  86.6 0.1 pad_add_fusion.2.places_ref
  86.7 0.0 collective-permute-done.24.other_ref
  86.7 1.8 %add.43.refs_0_ = f32[1024,512]{1,0:T(8,128)} custom-call(s32[8]{0:T(128)S(1)} %pad_add_fusion.2.places_ref, bf16[768,512]{1,0:T(8,128)(2,1)S(1)} %get-tuple-element.82.own_ref, bf16[768,512]{1,0:T(8,128)(2,1)S(1)} %collective-permute-done.24.other_ref), custom_call_target="tpu_custom_call" | custom-call | tf_op jit(solution)/shard_map/add/pallas_call | solution.py:314
  88.5 0.0 collective-permute-done.23.other_ref
  88.5 1.4 %add.44 = f32[1024,512]{1,0:T(8,128)} custom-call(s32[4]{0:T(128)S(1)} %broadcast_add_fusion.places_ref, bf16[256,512]{1,0:T(8,128)(2,1)S(1)} %far.1.own_ref, bf16[256,512]{1,0:T(8,128)(2,1)S(1)} %collective-permute-done.23.other_ref, f32[1024,512]{1,0:T(8,128)} %add.43.refs_0_), custom_call_target="tpu_custom_call", output_to_operand_aliasing={{}: (3, {})} | custom-call | tf_op jit(solution)/shard_map/add/pallas_call | solution.py:314
  (8 shorter events, 0.0 us)
Async XLA Ops:
  0.0 14.4 %collective-permute-start = (bf16[2,64,1024]{2,1,0:T(8,128)(2,1)}, bf16[2,64,1024]{2,1,0:T(8,128)(2,1)S(1)}, u32[]{:S(2)}, u32[]{:S(2)}) collective-permute-start(bf16[2,64,1024]{2,1,0:T(8,128)(2,1)} %refs_4_), channel_id=1, source_target_pairs={{0,50},{1,51},{16,0},{17,1},{32,16},{33,17},{48,32},{49,33},{2,48}... | collective-permute-start | bytes 786440 | tf_op jit(solution)/shard_map/p_up/ppermute | solution.py:38
  6.4 15.6 %collective-permute-start.4 = (bf16[2,64,1024]{2,1,0:T(8,128)(2,1)}, bf16[2,64,1024]{2,1,0:T(8,128)(2,1)S(1)}, u32[]{:S(2)}, u32[]{:S(2)}) collective-permute-start(bf16[2,64,1024]{2,1,0:T(8,128)(2,1)} %refs_4_), channel_id=1, source_target_pairs={{0,34},{1,33},{16,50},{17,49},{32,0},{33,3},{48,16},{49,19},{2,32}... | collective-permute-start | bytes 786440 | tf_op jit(solution)/shard_map/p_far/ppermute | solution.py:38
  6.4 15.6 %collective-permute-start.5 = (bf16[2,64,1024]{2,1,0:T(8,128)(2,1)}, bf16[2,64,1024]{2,1,0:T(8,128)(2,1)S(1)}, u32[]{:S(2)}, u32[]{:S(2)}) collective-permute-start(bf16[2,64,1024]{2,1,0:T(8,128)(2,1)} %refs_4_), channel_id=1, source_target_pairs={{0,16},{1,17},{16,32},{17,33},{32,48},{33,49},{48,2},{49,3},{2,18}... | collective-permute-start | bytes 786440 | tf_op jit(solution)/shard_map/p_down/ppermute | solution.py:38
  9.6 12.4 %collective-permute-start.1 = (bf16[32,2048]{1,0:T(8,128)(2,1)}, bf16[32,2048]{1,0:T(8,128)(2,1)S(1)}, u32[]{:S(2)}, u32[]{:S(2)}) collective-permute-start(bf16[32,2048]{1,0:T(8,128)(2,1)} %form.2.refs_0_), channel_id=1, source_target_pairs={{0,192},{1,193},{16,208},{17,209},{32,224},{33,225},{48,240},{49,2... | collective-permute-start | bytes 393224 | tf_op jit(solution)/shard_map/g_up/ppermute | solution.py:38
  12.1 9.9 %collective-permute-start.2 = (bf16[32,2048]{1,0:T(8,128)(2,1)}, bf16[32,2048]{1,0:T(8,128)(2,1)S(1)}, u32[]{:S(2)}, u32[]{:S(2)}) collective-permute-start(bf16[32,2048]{1,0:T(8,128)(2,1)} %form.2.refs_0_), channel_id=1, source_target_pairs={{0,128},{1,129},{16,144},{17,145},{32,160},{33,161},{48,176},{49,1... | collective-permute-start | bytes 393224 | tf_op jit(solution)/shard_map/g_far/ppermute | solution.py:38
  14.4 7.7 %collective-permute-start.3 = (bf16[32,2048]{1,0:T(8,128)(2,1)}, bf16[32,2048]{1,0:T(8,128)(2,1)S(1)}, u32[]{:S(2)}, u32[]{:S(2)}) collective-permute-start(bf16[32,2048]{1,0:T(8,128)(2,1)} %form.2.refs_0_), channel_id=1, source_target_pairs={{0,64},{1,65},{16,80},{17,81},{32,96},{33,97},{48,112},{49,113},{2... | collective-permute-start | bytes 393224 | tf_op jit(solution)/shard_map/g_down/ppermute | solution.py:38
  15.7 6.4 %copy-start = (bf16[32,2048]{1,0:T(8,128)(2,1)S(1)}, bf16[32,2048]{1,0:T(8,128)(2,1)}, u32[]{:S(2)}) copy-start(bf16[32,2048]{1,0:T(8,128)(2,1)} %form.2.refs_0_) | copy-start | bytes 393220
  15.7 6.4 %copy-start.2 = (bf16[2,64,1024]{2,1,0:T(8,128)(2,1)S(1)}, bf16[2,64,1024]{2,1,0:T(8,128)(2,1)}, u32[]{:S(2)}) copy-start(bf16[2,64,1024]{2,1,0:T(8,128)(2,1)} %refs_4_) | copy-start | bytes 786436
  23.2 23.4 %copy-start.3 = (bf16[64,2048]{1,0:T(8,128)(2,1)S(1)}, bf16[64,2048]{1,0:T(8,128)(2,1)}, u32[]{:S(2)}) copy-start(bf16[64,2048]{1,0:T(8,128)(2,1)} %get-tuple-element.67) | copy-start | bytes 786436
  23.2 10.0 %collective-permute-start.6 = (bf16[128,512]{1,0:T(8,128)(2,1)S(1)}, bf16[128,512]{1,0:T(8,128)(2,1)S(1)}, u32[]{:S(2)}, u32[]{:S(2)}) collective-permute-start(bf16[128,512]{1,0:T(8,128)(2,1)S(1)} %apply.1.refs_0_), channel_id=1, source_target_pairs={{0,32},{1,33},{16,48},{17,49},{32,0},{33,1},{48,16},{49,17},{2,34}... | collective-permute-start | bytes 393224 | tf_op jit(solution)/shard_map/low2/ppermute | solution.py:38
  26.4 7.3 %collective-permute-start.7 = (bf16[128,512]{1,0:T(8,128)(2,1)S(1)}, bf16[128,512]{1,0:T(8,128)(2,1)S(1)}, u32[]{:S(2)}, u32[]{:S(2)}) collective-permute-start(bf16[128,512]{1,0:T(8,128)(2,1)S(1)} %apply.1.refs_0_), channel_id=1, source_target_pairs={{0,48},{1,49},{16,0},{17,1},{32,16},{33,17},{48,32},{49,33},{2,50}... | collective-permute-start | bytes 393224 | tf_op jit(solution)/shard_map/low1/ppermute | solution.py:38
  26.9 7.6 %collective-permute-start.8 = (bf16[128,512]{1,0:T(8,128)(2,1)S(1)}, bf16[128,512]{1,0:T(8,128)(2,1)S(1)}, u32[]{:S(2)}, u32[]{:S(2)}) collective-permute-start(bf16[128,512]{1,0:T(8,128)(2,1)S(1)} %apply.1.refs_0_), channel_id=1, source_target_pairs={{0,16},{1,17},{16,32},{17,33},{32,48},{33,49},{48,0},{49,1},{2,18}... | collective-permute-start | bytes 393224 | tf_op jit(solution)/shard_map/low3/ppermute | solution.py:38
  27.9 16.0 %collective-permute-start.11 = (bf16[128,2048]{1,0:T(8,128)(2,1)}, bf16[128,2048]{1,0:T(8,128)(2,1)S(1)}, u32[]{:S(2)}, u32[]{:S(2)}) collective-permute-start(bf16[128,2048]{1,0:T(8,128)(2,1)} %get-tuple-element.63.refs_4_), channel_id=1, source_target_pairs={{0,12},{1,13},{16,28},{17,29},{32,44},{33,45},{48,60},{49,61},{2,1... | collective-permute-start | bytes 1572872 | tf_op jit(solution)/shard_map/n_up/ppermute | solution.py:38
  30.6 13.2 %collective-permute-start.12 = (bf16[128,2048]{1,0:T(8,128)(2,1)}, bf16[128,2048]{1,0:T(8,128)(2,1)S(1)}, u32[]{:S(2)}, u32[]{:S(2)}) collective-permute-start(bf16[128,2048]{1,0:T(8,128)(2,1)} %get-tuple-element.63.refs_4_), channel_id=1, source_target_pairs={{0,4},{1,5},{16,20},{17,21},{32,36},{33,37},{48,52},{49,53},{2,6},... | collective-permute-start | bytes 1572872 | tf_op jit(solution)/shard_map/n_down/ppermute | solution.py:38
  34.6 13.6 %collective-permute-start.14 = (bf16[64,2048]{1,0:T(8,128)(2,1)}, bf16[64,2048]{1,0:T(8,128)(2,1)S(1)}, u32[]{:S(2)}, u32[]{:S(2)}) collective-permute-start(bf16[64,2048]{1,0:T(8,128)(2,1)} %get-tuple-element.65), channel_id=1, source_target_pairs={{0,2},{1,3},{16,18},{17,19},{32,34},{33,35},{48,50},{49,51},{2,0},... | collective-permute-start | bytes 786440 | tf_op jit(solution)/shard_map/far1/ppermute | solution.py:38
  40.9 13.3 %collective-permute-start.10 = (bf16[512,512]{1,0:T(8,128)(2,1)S(1)}, bf16[512,512]{1,0:T(8,128)(2,1)S(1)}, u32[]{:S(2)}, u32[]{:S(2)}) collective-permute-start(bf16[512,512]{1,0:T(8,128)(2,1)S(1)} %bitcast.7), channel_id=1, source_target_pairs={{0,64},{1,65},{16,80},{17,81},{32,96},{33,97},{48,112},{49,113},{2... | collective-permute-start | bytes 1572872 | tf_op jit(solution)/shard_map/r_down/ppermute | solution.py:38
  41.2 13.0 %collective-permute-start.9 = (bf16[512,512]{1,0:T(8,128)(2,1)S(1)}, bf16[512,512]{1,0:T(8,128)(2,1)S(1)}, u32[]{:S(2)}, u32[]{:S(2)}) collective-permute-start(bf16[512,512]{1,0:T(8,128)(2,1)S(1)} %bitcast.8), channel_id=1, source_target_pairs={{0,192},{1,193},{16,208},{17,209},{32,224},{33,225},{48,240},{49,2... | collective-permute-start | bytes 1572872 | tf_op jit(solution)/shard_map/r_up/ppermute | solution.py:38
  43.8 11.8 %collective-permute-start.13 = (bf16[128,2048]{1,0:T(8,128)(2,1)S(1)}, bf16[128,2048]{1,0:T(8,128)(2,1)S(1)}, u32[]{:S(2)}, u32[]{:S(2)}) collective-permute-start(bf16[128,2048]{1,0:T(8,128)(2,1)S(1)} %collective-permute-done.11.refs_5_), channel_id=1, source_target_pairs={{0,12},{1,13},{16,28},{17,29},{32,44},{33,45},{48,60},{49,61},{2,1... | collective-permute-start | bytes 1572872 | tf_op jit(solution)/shard_map/n_two/ppermute | solution.py:38
  46.6 29.9 %copy-start.1 = (bf16[128,2048]{1,0:T(8,128)(2,1)S(1)}, bf16[128,2048]{1,0:T(8,128)(2,1)}, u32[]{:S(2)}) copy-start(bf16[128,2048]{1,0:T(8,128)(2,1)} %get-tuple-element.63.refs_4_) | copy-start | bytes 1572868
  46.6 22.5 %collective-permute-start.15 = (bf16[64,2048]{1,0:T(8,128)(2,1)S(1)}, bf16[64,2048]{1,0:T(8,128)(2,1)S(1)}, u32[]{:S(2)}, u32[]{:S(2)}) collective-permute-start(bf16[64,2048]{1,0:T(8,128)(2,1)S(1)} %copy-done.3), channel_id=1, source_target_pairs={{0,2},{1,3},{16,18},{17,19},{32,34},{33,35},{48,50},{49,51},{2,0},... | collective-permute-start | bytes 786440 | tf_op jit(solution)/shard_map/far2/ppermute | solution.py:38
  48.1 21.0 %collective-permute-start.17 = (bf16[64,2048]{1,0:T(8,128)(2,1)S(1)}, bf16[64,2048]{1,0:T(8,128)(2,1)S(1)}, u32[]{:S(2)}, u32[]{:S(2)}) collective-permute-start(bf16[64,2048]{1,0:T(8,128)(2,1)S(1)} %collective-permute-done.14.held_ref.refs_8_), channel_id=1, source_target_pairs={{0,4},{1,5},{16,20},{17,21},{32,36},{33,37},{48,52},{49,53},{2,6},... | collective-permute-start | bytes 786440 | tf_op jit(solution)/shard_map/a3/ppermute | solution.py:38
  55.6 13.5 %collective-permute-start.16 = (bf16[64,2048]{1,0:T(8,128)(2,1)S(1)}, bf16[64,2048]{1,0:T(8,128)(2,1)S(1)}, u32[]{:S(2)}, u32[]{:S(2)}) collective-permute-start(bf16[64,2048]{1,0:T(8,128)(2,1)S(1)} %collective-permute-done.14.held_ref.refs_8_), channel_id=1, source_target_pairs={{0,12},{1,13},{16,28},{17,29},{32,44},{33,45},{48,60},{49,61},{2,1... | collective-permute-start | bytes 786440 | tf_op jit(solution)/shard_map/a1/ppermute | solution.py:38
  59.0 17.5 %collective-permute-start.19 = (bf16[512,512]{1,0:T(8,128)(2,1)S(1)}, bf16[512,512]{1,0:T(8,128)(2,1)S(1)}, u32[]{:S(2)}, u32[]{:S(2)}) collective-permute-start(bf16[512,512]{1,0:T(8,128)(2,1)S(1)} %collective-permute-done.9.refs_1_), channel_id=1, source_target_pairs={{0,192},{1,193},{16,208},{17,209},{32,224},{33,225},{48,240},{49,2... | collective-permute-start | bytes 1572872 | tf_op jit(solution)/shard_map/r_next/ppermute | solution.py:38
  69.1 7.3 %collective-permute-start.20 = (bf16[64,2048]{1,0:T(8,128)(2,1)S(1)}, bf16[64,2048]{1,0:T(8,128)(2,1)S(1)}, u32[]{:S(2)}, u32[]{:S(2)}) collective-permute-start(bf16[64,2048]{1,0:T(8,128)(2,1)S(1)} %collective-permute-done.15.refs_0_), channel_id=1, source_target_pairs={{0,12},{1,13},{16,28},{17,29},{32,44},{33,45},{48,60},{49,61},{2,1... | collective-permute-start | bytes 786440 | tf_op jit(solution)/shard_map/b1/ppermute | solution.py:38
  69.1 7.4 %collective-permute-start.18 = (bf16[64,2048]{1,0:T(8,128)(2,1)S(1)}, bf16[64,2048]{1,0:T(8,128)(2,1)S(1)}, u32[]{:S(2)}, u32[]{:S(2)}) collective-permute-start(bf16[64,2048]{1,0:T(8,128)(2,1)S(1)} %collective-permute-done.17.refs_11_), channel_id=1, source_target_pairs={{0,4},{1,5},{16,20},{17,21},{32,36},{33,37},{48,52},{49,53},{2,6},... | collective-permute-start | bytes 786440 | tf_op jit(solution)/shard_map/a2/ppermute | solution.py:38
  70.6 13.6 %collective-permute-start.22 = (bf16[64,2048]{1,0:T(8,128)(2,1)S(1)}, bf16[64,2048]{1,0:T(8,128)(2,1)S(1)}, u32[]{:S(2)}, u32[]{:S(2)}) collective-permute-start(bf16[64,2048]{1,0:T(8,128)(2,1)S(1)} %collective-permute-done.15.refs_0_), channel_id=1, source_target_pairs={{0,4},{1,5},{16,20},{17,21},{32,36},{33,37},{48,52},{49,53},{2,6},... | collective-permute-start | bytes 786440 | tf_op jit(solution)/shard_map/b3/ppermute | solution.py:38
  76.5 7.7 %collective-permute-start.21 = (bf16[64,2048]{1,0:T(8,128)(2,1)S(1)}, bf16[64,2048]{1,0:T(8,128)(2,1)S(1)}, u32[]{:S(2)}, u32[]{:S(2)}) collective-permute-start(bf16[64,2048]{1,0:T(8,128)(2,1)S(1)} %collective-permute-done.20.refs_1_), channel_id=1, source_target_pairs={{0,12},{1,13},{16,28},{17,29},{32,44},{33,45},{48,60},{49,61},{2,1... | collective-permute-start | bytes 786440 | tf_op jit(solution)/shard_map/b2/ppermute | solution.py:38
  79.1 7.6 %collective-permute-start.24 = (bf16[768,512]{1,0:T(8,128)(2,1)S(1)}, bf16[768,512]{1,0:T(8,128)(2,1)S(1)}, u32[]{:S(2)}, u32[]{:S(2)}) collective-permute-start(bf16[768,512]{1,0:T(8,128)(2,1)S(1)} %get-tuple-element.82.own_ref), channel_id=1, source_target_pairs={{0,1},{1,0},{16,17},{17,16},{32,33},{33,32},{48,49},{49,48},{2,3},... | collective-permute-start | bytes 2359304 | tf_op jit(solution)/shard_map/swap/ppermute | solution.py:38
  85.5 2.9 %collective-permute-start.23 = (bf16[256,512]{1,0:T(8,128)(2,1)S(1)}, bf16[256,512]{1,0:T(8,128)(2,1)S(1)}, u32[]{:S(2)}, u32[]{:S(2)}) collective-permute-start(bf16[256,512]{1,0:T(8,128)(2,1)S(1)} %far.1.own_ref), channel_id=1, source_target_pairs={{0,1},{1,0},{16,17},{17,16},{32,33},{33,32},{48,49},{49,48},{2,3},... | collective-permute-start | bytes 786440 | tf_op jit(solution)/shard_map/swap_last/ppermute | solution.py:38
